TPU v7x, 128 devices: a whole 4x4x4 slice. The times are simulated.
128 devices in a mesh: section: 2 (over core), tensor: 16 (over x, z), ctx: 4 (over y).
Axes of the slice: x: 4, y: 4, z: 4, core: 2. Of those that a mesh axis runs over, the one named last changes fastest.
Arguments:
- inputs: bfloat16 [2, 4, 1024, 1024], P(None, 'ctx', 'tensor'), may hold values from -6 to 6
- segments: int32 [2, 4096], replicated, may hold values from 0 to 2, as said below
- gain_one: bfloat16 [2, 1024], P('section'), may hold values from 0.5 to 1.5
- bias_one: bfloat16 [2, 1024], P('section'), may hold values from -1.1953125 to 1.1953125
- w_qkv: bfloat16 [2, 1024, 3, 1024], P('section', None, None, 'tensor'), may hold values from -0.1875 to 0.1875
- b_qv: bfloat16 [2, 2, 1024], P('section', None, 'tensor'), may hold values from -1.1953125 to 1.1953125
- w_out: bfloat16 [2, 1024, 1024], P('section', 'tensor'), may hold values from -0.75 to 0.75
- b_out: bfloat16 [2, 1024], P('section'), may hold values from -1.1953125 to 1.1953125
- gain_two: bfloat16 [2, 1024], P('section'), may hold values from 0.5 to 1.5
- bias_two: bfloat16 [2, 1024], P('section'), may hold values from -1.1953125 to 1.1953125
- w_up: bfloat16 [2, 1024, 4096], P('section', None, 'tensor'), may hold values from -0.1875 to 0.1875
- b_up: bfloat16 [2, 4096], P('section', 'tensor'), may hold values from -1.1953125 to 1.1953125
- w_down: bfloat16 [2, 4096, 1024], P('section', 'tensor'), may hold values from -0.09375 to 0.09375
- b_down: bfloat16 [2, 1024], P('section'), may hold values from -1.1953125 to 1.1953125
- cotangent: bfloat16 [2, 4, 1024, 1024], P(None, 'ctx', 'tensor'), may hold values from -6 to 6
Outputs:
- boundary: float32 [2, 2, 4, 1024, 1024], P('section', None, 'ctx', 'tensor')
- grad_gain_one: float32 [2, 1024], P('section')
- grad_bias_one: float32 [2, 1024], P('section')
- grad_w_qkv: float32 [2, 1024, 3, 1024], P('section', None, None, 'tensor')
- grad_b_qv: float32 [2, 2, 1024], P('section', None, 'tensor')
- grad_w_out: float32 [2, 1024, 1024], P('section', 'tensor')
- grad_b_out: float32 [2, 1024], P('section')
- grad_gain_two: float32 [2, 1024], P('section')
- grad_bias_two: float32 [2, 1024], P('section')
- grad_w_up: float32 [2, 1024, 4096], P('section', None, 'tensor')
- grad_b_up: float32 [2, 4096], P('section', 'tensor')
- grad_w_down: float32 [2, 4096, 1024], P('section', 'tensor')
- grad_b_down: float32 [2, 1024], P('section')
Inputs may be any that keep to these rules, and one draw needn't show every extreme that they name: `segments`: in each sequence the numbers start at 0, never fall and end at 2; every document has at least 200 tokens, and document 1 begins in the first block and ends in the last.
All inputs are finite; a program needn't handle non-finite values.
Results may differ from a plain program's by a relative error of at most 0.02.
Values may be sent and summed in bfloat16 or wider, within the bound.
No kernel may reach another device: no remote copies, remote signals or barrier semaphores. Data moves between devices by JAX's collectives and lax.ppermute only.
A program may use at most 192 MiB of HBM per device.

v0:
```python
import jax
import jax.numpy as jnp
from jax import lax
from jax.sharding import PartitionSpec as P

HEAD_DIM = 64


EPSILON = 1e-05
SCORE_SCALE = 0.125
MASK_FILL = -1e30


def passed_along(block, axis, distance):
    devices = range(lax.axis_size(axis))
    route = [(i - distance, i) for i in devices if i - distance in devices]
    return lax.ppermute(block, axis, route)


def layer_norm(values, gain, bias):
    center = values - jnp.mean(values, axis=-1, keepdims=True)
    spread = jnp.mean(center * center, axis=-1, keepdims=True)
    return center * lax.rsqrt(spread + EPSILON) * gain + bias


def local_dot(left, right):
    return jnp.dot(left, right, preferred_element_type=jnp.float32)


def back_dot(left, right):
    return jnp.einsum("rf,df->rd", left, right, preferred_element_type=jnp.float32)


def outer_sum(left, right):
    return jnp.einsum("rd,rf->df", left, right, preferred_element_type=jnp.float32)


def visible(segment_ids, block_index, block_rows):
    segment_here = lax.dynamic_slice_in_dim(segment_ids, block_index * block_rows, block_rows)
    places = block_index * block_rows + jnp.arange(block_rows)
    key_places = jnp.arange(segment_ids.shape[0])
    return (segment_here[:, None] == segment_ids[None, :]) & (
        places[:, None] >= key_places[None, :]
    )


def head_scores(queries, key_rows, allowed, head_count):
    block_rows = queries.shape[0]
    scores = (
        jnp.einsum(
            "qhd,khd->hqk",
            queries.reshape(block_rows, head_count, HEAD_DIM),
            key_rows.reshape(-1, head_count, HEAD_DIM),
            preferred_element_type=jnp.float32,
        )
        * SCORE_SCALE
    )
    return jnp.where(allowed[None], scores, MASK_FILL)


def totals(gradients):
    (
        g_gain_one,
        g_bias_one,
        g_w_qkv,
        g_b_qv,
        g_w_out,
        g_b_out,
        g_gain_two,
        g_bias_two,
        g_w_up,
        g_b_up,
        g_w_down,
        g_b_down,
    ) = gradients
    g_w_qkv, g_b_qv, g_w_out, g_w_up, g_b_up, g_w_down = (
        lax.psum(g_w_qkv.astype(jnp.bfloat16), "ctx").astype(jnp.float32),
        lax.psum(g_b_qv.astype(jnp.bfloat16), "ctx").astype(jnp.float32),
        lax.psum(g_w_out.astype(jnp.bfloat16), "ctx").astype(jnp.float32),
        lax.psum(g_w_up.astype(jnp.bfloat16), "ctx").astype(jnp.float32),
        lax.psum(g_b_up.astype(jnp.bfloat16), "ctx").astype(jnp.float32),
        lax.psum(g_w_down.astype(jnp.bfloat16), "ctx").astype(jnp.float32),
    )
    g_gain_one, g_bias_one, g_b_out, g_gain_two, g_bias_two, g_b_down = lax.psum(
        (g_gain_one, g_bias_one, g_b_out, g_gain_two, g_bias_two, g_b_down), ("tensor", "ctx")
    )
    return (
        g_gain_one,
        g_bias_one,
        g_w_qkv,
        g_b_qv,
        g_w_out,
        g_b_out,
        g_gain_two,
        g_bias_two,
        g_w_up,
        g_b_up,
        g_w_down,
        g_b_down,
    )


def layer_forward(residual, segment_ids, params, block_index):
    (
        gain_one,
        bias_one,
        w_qkv,
        b_qv,
        w_out,
        b_out,
        gain_two,
        bias_two,
        w_up,
        b_up,
        w_down,
        b_down,
    ) = params
    model_width = residual.shape[1]
    local_width = w_qkv.shape[2]
    head_count = local_width // HEAD_DIM
    normed = layer_norm(residual, gain_one, bias_one).astype(jnp.bfloat16)
    normed_all = lax.all_gather(normed, "tensor", axis=0, tiled=True)
    block_rows = normed_all.shape[0]
    projected = local_dot(normed_all, w_qkv.reshape(model_width, 3 * local_width)).reshape(
        block_rows, 3, local_width
    )
    queries = (projected[:, 0] + b_qv[0]).astype(jnp.bfloat16)
    key_rows = projected[:, 1].astype(jnp.bfloat16)
    value_rows = (projected[:, 2] + b_qv[1]).astype(jnp.bfloat16)
    key_all, value_all = (
        lax.all_gather(key_rows, "ctx", axis=0, tiled=True),
        lax.all_gather(value_rows, "ctx", axis=0, tiled=True),
    )
    allowed = visible(segment_ids, block_index, block_rows)
    scores = head_scores(queries, key_all, allowed, head_count)
    row_peak = jnp.max(scores, axis=-1, keepdims=True)
    exponent = jnp.exp(scores - row_peak)
    row_total = jnp.sum(exponent, axis=-1, keepdims=True)
    probs_low = (exponent / row_total).astype(jnp.bfloat16)
    mixed_heads = jnp.einsum(
        "hqk,khd->qhd",
        probs_low,
        value_all.reshape(-1, head_count, HEAD_DIM),
        preferred_element_type=jnp.float32,
    )
    mixed_heads = mixed_heads.reshape(block_rows, local_width).astype(jnp.bfloat16)
    hidden = residual + (
        lax.psum_scatter(
            local_dot(mixed_heads, w_out).astype(jnp.bfloat16),
            "tensor",
            scatter_dimension=0,
            tiled=True,
        ).astype(jnp.float32)
        + b_out
    )
    normed_two = layer_norm(hidden, gain_two, bias_two).astype(jnp.bfloat16)
    normed_two_all = lax.all_gather(normed_two, "tensor", axis=0, tiled=True)
    up_value = local_dot(normed_two_all, w_up) + b_up
    activated = jax.nn.gelu(up_value).astype(jnp.bfloat16)
    down_sum = lax.psum_scatter(
        local_dot(activated, w_down).astype(jnp.bfloat16), "tensor", scatter_dimension=0, tiled=True
    ).astype(jnp.float32)
    result = hidden + (down_sum + b_down)
    stored = (
        residual,
        normed_all,
        queries,
        key_all,
        value_all,
        row_peak,
        row_total,
        mixed_heads,
        hidden,
        normed_two_all,
        up_value,
    )
    return (result, stored)


def layer_backward(grad_out, stored, params, segment_ids, block_index):
    (
        gain_one,
        bias_one,
        w_qkv,
        b_qv,
        w_out,
        b_out,
        gain_two,
        bias_two,
        w_up,
        b_up,
        w_down,
        b_down,
    ) = params
    (
        residual,
        normed_all,
        queries,
        key_all,
        value_all,
        row_peak,
        row_total,
        mixed_heads,
        hidden,
        normed_two_all,
        up_value,
    ) = stored
    model_width = residual.shape[1]
    block_rows = normed_all.shape[0]
    local_width = w_qkv.shape[2]
    head_count = local_width // HEAD_DIM
    grad_down = grad_out.astype(jnp.bfloat16)
    g_b_down = jnp.sum(grad_down.astype(jnp.float32), axis=0)
    grad_down_all = lax.all_gather(grad_down, "tensor", axis=0, tiled=True)
    activated, gelu_pull = jax.vjp(jax.nn.gelu, up_value)
    g_w_down = outer_sum(activated.astype(jnp.bfloat16), grad_down_all)
    (grad_up,) = gelu_pull(back_dot(grad_down_all, w_down))
    grad_up = grad_up.astype(jnp.bfloat16)
    g_b_up = jnp.sum(grad_up.astype(jnp.float32), axis=0)
    g_w_up = outer_sum(normed_two_all, grad_up)
    grad_normed_two = lax.psum_scatter(
        back_dot(grad_up, w_up).astype(jnp.bfloat16), "tensor", scatter_dimension=0, tiled=True
    ).astype(jnp.float32)
    _, norm_two_pull = jax.vjp(layer_norm, hidden, gain_two, bias_two)
    grad_hidden_part, g_gain_two, g_bias_two = norm_two_pull(grad_normed_two)
    grad_hidden = grad_out + grad_hidden_part
    grad_attn = grad_hidden.astype(jnp.bfloat16)
    g_b_out = jnp.sum(grad_attn.astype(jnp.float32), axis=0)
    grad_attn_all = lax.all_gather(grad_attn, "tensor", axis=0, tiled=True)
    g_w_out = outer_sum(mixed_heads, grad_attn_all)
    grad_mixed = (
        back_dot(grad_attn_all, w_out)
        .astype(jnp.bfloat16)
        .reshape(block_rows, head_count, HEAD_DIM)
    )
    allowed = visible(segment_ids, block_index, block_rows)
    scores = head_scores(queries, key_all, allowed, head_count)
    probs_full = jnp.exp(scores - row_peak) / row_total
    probs_low = probs_full.astype(jnp.bfloat16)
    query_heads = queries.reshape(block_rows, head_count, HEAD_DIM)
    key_heads = key_all.reshape(-1, head_count, HEAD_DIM)
    value_heads = value_all.reshape(-1, head_count, HEAD_DIM)
    grad_probs = jnp.einsum(
        "qhd,khd->hqk", grad_mixed, value_heads, preferred_element_type=jnp.float32
    )
    grad_scores = probs_full * (
        grad_probs - jnp.sum(grad_probs * probs_full, axis=-1, keepdims=True)
    )
    grad_scores = jnp.where(allowed[None], grad_scores, 0.0).astype(jnp.bfloat16)
    grad_query = (
        jnp.einsum("hqk,khd->qhd", grad_scores, key_heads, preferred_element_type=jnp.float32)
        * SCORE_SCALE
    )
    grad_key_part = (
        jnp.einsum("hqk,qhd->khd", grad_scores, query_heads, preferred_element_type=jnp.float32)
        * SCORE_SCALE
    )
    grad_value_part = jnp.einsum(
        "hqk,qhd->khd", probs_low, grad_mixed, preferred_element_type=jnp.float32
    )
    grad_keys, grad_values = (
        lax.psum_scatter(
            grad_key_part.reshape(-1, local_width).astype(jnp.bfloat16),
            "ctx",
            scatter_dimension=0,
            tiled=True,
        ).astype(jnp.float32),
        lax.psum_scatter(
            grad_value_part.reshape(-1, local_width).astype(jnp.bfloat16),
            "ctx",
            scatter_dimension=0,
            tiled=True,
        ).astype(jnp.float32),
    )
    grad_qkv = jnp.stack(
        [grad_query.reshape(block_rows, local_width), grad_keys, grad_values], axis=1
    ).astype(jnp.bfloat16)
    g_b_qv = jnp.sum(grad_qkv[:, 0::2].astype(jnp.float32), axis=0)
    flat_grad = grad_qkv.reshape(block_rows, 3 * local_width)
    g_w_qkv = outer_sum(normed_all, flat_grad).reshape(model_width, 3, local_width)
    w_flat = w_qkv.reshape(model_width, 3 * local_width)
    grad_normed = lax.psum_scatter(
        back_dot(flat_grad, w_flat).astype(jnp.bfloat16), "tensor", scatter_dimension=0, tiled=True
    ).astype(jnp.float32)
    _, norm_one_pull = jax.vjp(layer_norm, residual, gain_one, bias_one)
    grad_residual_part, g_gain_one, g_bias_one = norm_one_pull(grad_normed)
    grad_residual = grad_hidden + grad_residual_part
    gradients = (
        g_gain_one,
        g_bias_one,
        g_w_qkv,
        g_b_qv,
        g_w_out,
        g_b_out,
        g_gain_two,
        g_bias_two,
        g_w_up,
        g_b_up,
        g_w_down,
        g_b_down,
    )
    return (grad_residual, gradients)


def per_device(
    inputs,
    segments,
    gain_one,
    bias_one,
    w_qkv,
    b_qv,
    w_out,
    b_out,
    gain_two,
    bias_two,
    w_up,
    b_up,
    w_down,
    b_down,
    cotangent,
):
    shards = (
        gain_one,
        bias_one,
        w_qkv,
        b_qv,
        w_out,
        b_out,
        gain_two,
        bias_two,
        w_up,
        b_up,
        w_down,
        b_down,
    )
    local_params = (
        gain_one[0].astype(jnp.float32),
        bias_one[0].astype(jnp.float32),
        w_qkv[0],
        b_qv[0].astype(jnp.float32),
        w_out[0],
        b_out[0].astype(jnp.float32),
        gain_two[0].astype(jnp.float32),
        bias_two[0].astype(jnp.float32),
        w_up[0],
        b_up[0].astype(jnp.float32),
        w_down[0],
        b_down[0].astype(jnp.float32),
    )
    section_index = lax.axis_index("section")
    block_index = lax.axis_index("ctx")
    batch_count = inputs.shape[0]
    row_count = inputs.shape[2]
    model_width = inputs.shape[3]
    first_inputs = inputs.reshape(batch_count, row_count, model_width).astype(jnp.float32)
    grad_last = cotangent.reshape(batch_count, row_count, model_width).astype(jnp.float32)
    step_list = jnp.arange(batch_count + 1)

    def forward_step(incoming, step_index):
        batch_index = jnp.clip(step_index - section_index, 0, batch_count - 1)
        source = jnp.where(section_index == 0, first_inputs[batch_index], incoming)
        result, stored = layer_forward(source, segments[batch_index], local_params, block_index)
        passed = passed_along(result.astype(jnp.bfloat16), "section", 1)
        return (passed.astype(jnp.float32), (result, stored))

    empty_rows = jnp.zeros((row_count, model_width), jnp.float32)
    _, (results, stored_all) = lax.scan(forward_step, empty_rows, step_list)
    empty_grads = tuple((jnp.zeros(param.shape, jnp.float32) for param in local_params))

    def backward_step(carry, step_index):
        incoming, summed = carry
        batch_raw = step_index - 1 + section_index
        in_range = (batch_raw >= 0) & (batch_raw < batch_count)
        batch_index = jnp.clip(batch_raw, 0, batch_count - 1)
        grad_out = jnp.where(section_index == 1, grad_last[batch_index], incoming)
        stored = jax.tree.map(lambda leaf: leaf[batch_index + section_index], stored_all)
        grad_in, gradients = layer_backward(
            grad_out, stored, local_params, segments[batch_index], block_index
        )
        gradients = tuple((jnp.where(in_range, grad_term, 0.0) for grad_term in gradients))
        summed = tuple((left + right for left, right in zip(summed, gradients)))
        passed = passed_along(grad_in.astype(jnp.bfloat16), "section", -1)
        return ((passed.astype(jnp.float32), summed), grad_in)

    (_, summed), grad_inputs = lax.scan(backward_step, (empty_rows, empty_grads), step_list)
    summed = totals(summed)
    boundary = jnp.where(section_index == 0, grad_inputs[1:], results[1:])
    boundary = boundary.reshape(1, batch_count, 1, row_count, model_width)
    return (boundary,) + tuple(
        (total_grad.reshape(shard.shape) for total_grad, shard in zip(summed, shards))
    )


def solution(mesh):
    return jax.shard_map(
        per_device,
        mesh=mesh,
        in_specs=(
            P(None, "ctx", "tensor", None),
            P(),
            P("section", None),
            P("section", None),
            P("section", None, None, "tensor"),
            P("section", None, "tensor"),
            P("section", "tensor", None),
            P("section", None),
            P("section", None),
            P("section", None),
            P("section", None, "tensor"),
            P("section", "tensor"),
            P("section", "tensor", None),
            P("section", None),
            P(None, "ctx", "tensor", None),
        ),
        out_specs=(
            P("section", None, "ctx", "tensor", None),
            P("section", None),
            P("section", None),
            P("section", None, None, "tensor"),
            P("section", None, "tensor"),
            P("section", "tensor", None),
            P("section", None),
            P("section", None),
            P("section", None),
            P("section", None, "tensor"),
            P("section", "tensor"),
            P("section", "tensor", None),
            P("section", None),
        ),
        check_vma=False,
    )
```

profile of v0, /device:TPU:0, one launch (start us, length us, event | category | flops | bytes accessed | tf_op | source)
XLA Modules:
  0.0 2310.3 jit_solution(10906675205344513456)
XLA Ops:
  22.6 936.4 %while.78 = (s32[]{:T(128)}, f32[64,1024]{1,0:T(8,128)S(1)}, f32[3,64,1024]{2,1,0:T(8,128)}, f32[3,64,1024]{2,1,0:T(8,128)}, bf16[3,1024,1024]{2,1,0:T(8,128)(2,...) while((s32[]{:T(128)}, f32[64,1024]{1,0:T(8,128)S(1)}, ...), condition=%wide.region_9.10_spmd.clone, body=%wide.region_0.9_spmd.clone.sunk | while | flops 2737699840 | bytes 129944720 | solution.py:367
  29.0 46.2 %all-gather.9.cloned.1.call-done = bf16[1024,1024]{1,0:T(8,128)(2,1)} async-done(((bf16[64,1024]{1,0:T(8,128)(2,1)}), bf16[1024,1024]{1,0:T(8,128)(2,1)}) %all-gather.9.cloned.1.call-update) | async-done | bytes 2097168 | tf_op jit(solution)/shard_map/while/body/eval_jaxpr/all_gather | solution.py:122
  131.6 72.9 %reduce-scatter.7.cloned.1.call-done = bf16[64,1024]{1,0:T(8,128)(2,1)} async-done(((bf16[1024,1024]{1,0:T(8,128)(2,1)}), bf16[64,1024]{1,0:T(8,128)(2,1)}) %reduce-scatter.7.cloned.1.call-update) | async-done | bytes 131088 | tf_op jit(solution)/shard_map/while/body/eval_jaxpr/reduce_scatter | solution.py:148
  207.9 44.5 %all-gather.11.cloned.1.call-done = bf16[1024,1024]{1,0:T(8,128)(2,1)} async-done(((bf16[64,1024]{1,0:T(8,128)(2,1)}), bf16[1024,1024]{1,0:T(8,128)(2,1)}) %all-gather.11.cloned.1.call-update) | async-done | bytes 2097168 | tf_op jit(solution)/shard_map/while/body/eval_jaxpr/all_gather | solution.py:157
  267.8 65.2 %reduce-scatter.9.cloned.1.call-done = bf16[64,1024]{1,0:T(8,128)(2,1)} async-done(((bf16[1024,1024]{1,0:T(8,128)(2,1)}), bf16[64,1024]{1,0:T(8,128)(2,1)}) %reduce-scatter.9.cloned.1.call-update) | async-done | bytes 131088 | tf_op jit(solution)/shard_map/while/body/eval_jaxpr/reduce_scatter | solution.py:160
  343.3 42.9 %all-gather.9.cloned.1.call-done = bf16[1024,1024]{1,0:T(8,128)(2,1)} async-done(((bf16[64,1024]{1,0:T(8,128)(2,1)}), bf16[1024,1024]{1,0:T(8,128)(2,1)}) %all-gather.9.cloned.1.call-update) | async-done | bytes 2097168 | tf_op jit(solution)/shard_map/while/body/eval_jaxpr/all_gather | solution.py:122
  442.6 72.8 %reduce-scatter.7.cloned.1.call-done = bf16[64,1024]{1,0:T(8,128)(2,1)} async-done(((bf16[1024,1024]{1,0:T(8,128)(2,1)}), bf16[64,1024]{1,0:T(8,128)(2,1)}) %reduce-scatter.7.cloned.1.call-update) | async-done | bytes 131088 | tf_op jit(solution)/shard_map/while/body/eval_jaxpr/reduce_scatter | solution.py:148
  518.9 44.5 %all-gather.11.cloned.1.call-done = bf16[1024,1024]{1,0:T(8,128)(2,1)} async-done(((bf16[64,1024]{1,0:T(8,128)(2,1)}), bf16[1024,1024]{1,0:T(8,128)(2,1)}) %all-gather.11.cloned.1.call-update) | async-done | bytes 2097168 | tf_op jit(solution)/shard_map/while/body/eval_jaxpr/all_gather | solution.py:157
  578.8 65.2 %reduce-scatter.9.cloned.1.call-done = bf16[64,1024]{1,0:T(8,128)(2,1)} async-done(((bf16[1024,1024]{1,0:T(8,128)(2,1)}), bf16[64,1024]{1,0:T(8,128)(2,1)}) %reduce-scatter.9.cloned.1.call-update) | async-done | bytes 131088 | tf_op jit(solution)/shard_map/while/body/eval_jaxpr/reduce_scatter | solution.py:160
  654.4 42.9 %all-gather.9.cloned.1.call-done = bf16[1024,1024]{1,0:T(8,128)(2,1)} async-done(((bf16[64,1024]{1,0:T(8,128)(2,1)}), bf16[1024,1024]{1,0:T(8,128)(2,1)}) %all-gather.9.cloned.1.call-update) | async-done | bytes 2097168 | tf_op jit(solution)/shard_map/while/body/eval_jaxpr/all_gather | solution.py:122
  753.7 72.8 %reduce-scatter.7.cloned.1.call-done = bf16[64,1024]{1,0:T(8,128)(2,1)} async-done(((bf16[1024,1024]{1,0:T(8,128)(2,1)}), bf16[64,1024]{1,0:T(8,128)(2,1)}) %reduce-scatter.7.cloned.1.call-update) | async-done | bytes 131088 | tf_op jit(solution)/shard_map/while/body/eval_jaxpr/reduce_scatter | solution.py:148
  830.0 44.5 %all-gather.11.cloned.1.call-done = bf16[1024,1024]{1,0:T(8,128)(2,1)} async-done(((bf16[64,1024]{1,0:T(8,128)(2,1)}), bf16[1024,1024]{1,0:T(8,128)(2,1)}) %all-gather.11.cloned.1.call-update) | async-done | bytes 2097168 | tf_op jit(solution)/shard_map/while/body/eval_jaxpr/all_gather | solution.py:157
  889.7 65.4 %reduce-scatter.9.cloned.1.call-done = bf16[64,1024]{1,0:T(8,128)(2,1)} async-done(((bf16[1024,1024]{1,0:T(8,128)(2,1)}), bf16[64,1024]{1,0:T(8,128)(2,1)}) %reduce-scatter.9.cloned.1.call-update) | async-done | bytes 131088 | tf_op jit(solution)/shard_map/while/body/eval_jaxpr/reduce_scatter | solution.py:160
  959.1 971.6 %while.79 = (s32[]{:T(128)}, f32[64,1024]{1,0:T(8,128)}, f32[1024]{0:T(1024)}, f32[1024]{0:T(1024)}, f32[1024,3,64]{0,2,1:T(8,128)}, /*index=5*/f32[2,64]{1,0:T(...) while((s32[]{:T(128)}, f32[64,1024]{1,0:T(8,128)}, ...), condition=%wide.region_32.33_spmd.clone, body=%wide.region_10.32_spmd.clone.sunk | while | flops 5996558336 | bytes 315047296 | solution.py:385
  962.4 45.0 %all-gather.13.cloned.1.call-done = bf16[1024,1024]{1,0:T(8,128)(2,1)} async-done(((bf16[64,1024]{1,0:T(8,128)(2,1)}), bf16[1024,1024]{1,0:T(8,128)(2,1)}) %all-gather.13.cloned.1.call-update) | async-done | bytes 2097168 | tf_op jit(solution)/shard_map/while/body/eval_jaxpr/all_gather | solution.py:214
  1013.9 72.8 %reduce-scatter.11.cloned.1.call-done = bf16[64,1024]{1,0:T(8,128)(2,1)} async-done(((bf16[1024,1024]{1,0:T(8,128)(2,1)}), bf16[64,1024]{1,0:T(8,128)(2,1)}) %reduce-scatter.11.cloned.1.call-update) | async-done | bytes 131088 | tf_op jit(solution)/shard_map/while/body/eval_jaxpr/reduce_scatter | solution.py:221
  1215.3 61.3 %reduce-scatter.17.cloned.1.call-done = bf16[64,1024]{1,0:T(8,128)(2,1)} async-done(((bf16[1024,1024]{1,0:T(8,128)(2,1)}), bf16[64,1024]{1,0:T(8,128)(2,1)}) %reduce-scatter.17.cloned.1.call-update) | async-done | bytes 131088 | tf_op jit(solution)/shard_map/while/body/eval_jaxpr/reduce_scatter | solution.py:282
  1286.4 44.9 %all-gather.13.cloned.1.call-done = bf16[1024,1024]{1,0:T(8,128)(2,1)} async-done(((bf16[64,1024]{1,0:T(8,128)(2,1)}), bf16[1024,1024]{1,0:T(8,128)(2,1)}) %all-gather.13.cloned.1.call-update) | async-done | bytes 2097168 | tf_op jit(solution)/shard_map/while/body/eval_jaxpr/all_gather | solution.py:214
  1337.9 72.7 %reduce-scatter.11.cloned.1.call-done = bf16[64,1024]{1,0:T(8,128)(2,1)} async-done(((bf16[1024,1024]{1,0:T(8,128)(2,1)}), bf16[64,1024]{1,0:T(8,128)(2,1)}) %reduce-scatter.11.cloned.1.call-update) | async-done | bytes 131088 | tf_op jit(solution)/shard_map/while/body/eval_jaxpr/reduce_scatter | solution.py:221
  1539.7 60.6 %reduce-scatter.17.cloned.1.call-done = bf16[64,1024]{1,0:T(8,128)(2,1)} async-done(((bf16[1024,1024]{1,0:T(8,128)(2,1)}), bf16[64,1024]{1,0:T(8,128)(2,1)}) %reduce-scatter.17.cloned.1.call-update) | async-done | bytes 131088 | tf_op jit(solution)/shard_map/while/body/eval_jaxpr/reduce_scatter | solution.py:282
  1610.1 44.9 %all-gather.13.cloned.1.call-done = bf16[1024,1024]{1,0:T(8,128)(2,1)} async-done(((bf16[64,1024]{1,0:T(8,128)(2,1)}), bf16[1024,1024]{1,0:T(8,128)(2,1)}) %all-gather.13.cloned.1.call-update) | async-done | bytes 2097168 | tf_op jit(solution)/shard_map/while/body/eval_jaxpr/all_gather | solution.py:214
  1661.6 72.8 %reduce-scatter.11.cloned.1.call-done = bf16[64,1024]{1,0:T(8,128)(2,1)} async-done(((bf16[1024,1024]{1,0:T(8,128)(2,1)}), bf16[64,1024]{1,0:T(8,128)(2,1)}) %reduce-scatter.11.cloned.1.call-update) | async-done | bytes 131088 | tf_op jit(solution)/shard_map/while/body/eval_jaxpr/reduce_scatter | solution.py:221
  1863.5 60.6 %reduce-scatter.17.cloned.1.call-done = bf16[64,1024]{1,0:T(8,128)(2,1)} async-done(((bf16[1024,1024]{1,0:T(8,128)(2,1)}), bf16[64,1024]{1,0:T(8,128)(2,1)}) %reduce-scatter.17.cloned.1.call-update) | async-done | bytes 131088 | tf_op jit(solution)/shard_map/while/body/eval_jaxpr/reduce_scatter | solution.py:282
  1950.5 343.6 %all-reduce = (f32[1,1024]{1,0:T(1,128)}, f32[1,1024]{1,0:T(1,128)}, f32[1,1024]{1,0:T(1,128)}, f32[1,1024]{1,0:T(1,128)}, f32[1,1024]{1,0:T(1,128)}, /*index=5*/f32[1,1024]{1,0:T(1,128)}) all-reduce(f32[1,1024]{1,0:T(1,128)S(1)} %bitcast.423, ...), channel_id=1, replica_groups=mesh['section'=2,'tensor'=16,'ctx'=4] {'tensor','ctx'}, use_global_device_ids=true, to_apply=%region_33.34 | all-reduce | flops 6144 | bytes 49152 | tf_op jit(solution)/shard_map/psum | solution.py:84
  (705 shorter events, 728.6 us)
Async XLA Ops:
  27.3 177.1 %reduce-scatter.7.cloned.1.call-start = ((), (), s32[]{:S(2)}) async-start(), calls=%async_computation.8 | async-start | bytes 2228224 | tf_op jit(solution)/shard_map/while/body/eval_jaxpr/reduce_scatter | solution.py:148
  131.5 120.9 %all-gather.11.cloned.1.call-start = ((), (), s32[]{:S(2)}) async-start(), calls=%async_computation.9 | async-start | bytes 2228224 | tf_op jit(solution)/shard_map/while/body/eval_jaxpr/all_gather | solution.py:157
  207.9 125.0 %reduce-scatter.9.cloned.1.call-start = ((), (), s32[]{:S(2)}) async-start(), calls=%async_computation.10 | async-start | bytes 2228224 | tf_op jit(solution)/shard_map/while/body/eval_jaxpr/reduce_scatter | solution.py:160
  341.6 173.8 %reduce-scatter.7.cloned.1.call-start = ((), (), s32[]{:S(2)}) async-start(), calls=%async_computation.8 | async-start | bytes 2228224 | tf_op jit(solution)/shard_map/while/body/eval_jaxpr/reduce_scatter | solution.py:148
  442.5 120.9 %all-gather.11.cloned.1.call-start = ((), (), s32[]{:S(2)}) async-start(), calls=%async_computation.9 | async-start | bytes 2228224 | tf_op jit(solution)/shard_map/while/body/eval_jaxpr/all_gather | solution.py:157
  518.9 125.2 %reduce-scatter.9.cloned.1.call-start = ((), (), s32[]{:S(2)}) async-start(), calls=%async_computation.10 | async-start | bytes 2228224 | tf_op jit(solution)/shard_map/while/body/eval_jaxpr/reduce_scatter | solution.py:160
  652.7 173.7 %reduce-scatter.7.cloned.1.call-start = ((), (), s32[]{:S(2)}) async-start(), calls=%async_computation.8 | async-start | bytes 2228224 | tf_op jit(solution)/shard_map/while/body/eval_jaxpr/reduce_scatter | solution.py:148
  753.6 120.9 %all-gather.11.cloned.1.call-start = ((), (), s32[]{:S(2)}) async-start(), calls=%async_computation.9 | async-start | bytes 2228224 | tf_op jit(solution)/shard_map/while/body/eval_jaxpr/all_gather | solution.py:157
  829.9 125.1 %reduce-scatter.9.cloned.1.call-start = ((), (), s32[]{:S(2)}) async-start(), calls=%async_computation.10 | async-start | bytes 2228224 | tf_op jit(solution)/shard_map/while/body/eval_jaxpr/reduce_scatter | solution.py:160
  962.3 124.4 %reduce-scatter.11.cloned.1.call-start = ((), (), s32[]{:S(2)}) async-start(), calls=%async_computation.12 | async-start | bytes 2228224 | tf_op jit(solution)/shard_map/while/body/eval_jaxpr/reduce_scatter | solution.py:221
  1012.8 122.9 %all-gather.15.cloned.1.call-start = ((), (), s32[]{:S(2)}) async-start(), calls=%async_computation.13 | async-start | bytes 2228224 | tf_op jit(solution)/shard_map/while/body/eval_jaxpr/all_gather | solution.py:229
  1091.1 93.4 %reduce-scatter.13.cloned.1.call-start = ((), (), s32[]{:S(2)}) async-start(), calls=%async_computation.14 | async-start | bytes 655360 | tf_op jit(solution)/shard_map/while/body/eval_jaxpr/reduce_scatter | solution.py:268
  1146.2 52.7 %reduce-scatter.15.cloned.1.call-start = ((), (), s32[]{:S(2)}) async-start(), calls=%async_computation.15 | async-start | bytes 655360 | tf_op jit(solution)/shard_map/while/body/eval_jaxpr/reduce_scatter | solution.py:262
  1178.1 98.4 %reduce-scatter.17.cloned.1.call-start = ((), (), s32[]{:S(2)}) async-start(), calls=%async_computation.16 | async-start | bytes 2228224 | tf_op jit(solution)/shard_map/while/body/eval_jaxpr/reduce_scatter | solution.py:282
  1286.3 124.3 %reduce-scatter.11.cloned.1.call-start = ((), (), s32[]{:S(2)}) async-start(), calls=%async_computation.12 | async-start | bytes 2228224 | tf_op jit(solution)/shard_map/while/body/eval_jaxpr/reduce_scatter | solution.py:221
  1336.7 122.7 %all-gather.15.cloned.1.call-start = ((), (), s32[]{:S(2)}) async-start(), calls=%async_computation.13 | async-start | bytes 2228224 | tf_op jit(solution)/shard_map/while/body/eval_jaxpr/all_gather | solution.py:229
  1414.9 93.4 %reduce-scatter.13.cloned.1.call-start = ((), (), s32[]{:S(2)}) async-start(), calls=%async_computation.14 | async-start | bytes 655360 | tf_op jit(solution)/shard_map/while/body/eval_jaxpr/reduce_scatter | solution.py:268
  1470.0 52.7 %reduce-scatter.15.cloned.1.call-start = ((), (), s32[]{:S(2)}) async-start(), calls=%async_computation.15 | async-start | bytes 655360 | tf_op jit(solution)/shard_map/while/body/eval_jaxpr/reduce_scatter | solution.py:262
  1502.0 98.3 %reduce-scatter.17.cloned.1.call-start = ((), (), s32[]{:S(2)}) async-start(), calls=%async_computation.16 | async-start | bytes 2228224 | tf_op jit(solution)/shard_map/while/body/eval_jaxpr/reduce_scatter | solution.py:282
  1610.0 124.3 %reduce-scatter.11.cloned.1.call-start = ((), (), s32[]{:S(2)}) async-start(), calls=%async_computation.12 | async-start | bytes 2228224 | tf_op jit(solution)/shard_map/while/body/eval_jaxpr/reduce_scatter | solution.py:221
  1660.4 122.9 %all-gather.15.cloned.1.call-start = ((), (), s32[]{:S(2)}) async-start(), calls=%async_computation.13 | async-start | bytes 2228224 | tf_op jit(solution)/shard_map/while/body/eval_jaxpr/all_gather | solution.py:229
  1738.7 93.4 %reduce-scatter.13.cloned.1.call-start = ((), (), s32[]{:S(2)}) async-start(), calls=%async_computation.14 | async-start | bytes 655360 | tf_op jit(solution)/shard_map/while/body/eval_jaxpr/reduce_scatter | solution.py:268
  1825.8 98.3 %reduce-scatter.17.cloned.1.call-start = ((), (), s32[]{:S(2)}) async-start(), calls=%async_computation.16 | async-start | bytes 2228224 | tf_op jit(solution)/shard_map/while/body/eval_jaxpr/reduce_scatter | solution.py:282
  1930.9 364.2 %all-reduce.5.cloned.1.call-start = ((), (), s32[]{:S(2)}) async-start(), calls=%async_computation.6 | async-start | bytes 3145728 | tf_op jit(solution)/shard_map/psum | solution.py:77
  (169 other events, 5897.5 us)
Sparse Core Ops, SparseCore 0:
  27.4 47.7 all-gather.8
  131.6 72.7 reduce-scatter.6
  208.0 44.3 all-gather.10
  259.3 73.6 reduce-scatter.8
  341.8 44.4 all-gather.8
  442.7 72.6 reduce-scatter.6
  519.0 44.4 all-gather.10
  570.2 73.7 reduce-scatter.8
  652.9 44.3 all-gather.8
  753.7 72.7 reduce-scatter.6
  830.1 44.4 all-gather.10
  881.3 73.7 reduce-scatter.8
  962.9 44.4 all-gather.12
  1012.9 73.7 reduce-scatter.10
  1091.2 44.4 all-gather.14
  1202.3 74.1 reduce-scatter.16
  1286.8 44.4 all-gather.12
  1336.9 73.6 reduce-scatter.10
  1415.1 44.3 all-gather.14
  1526.2 74.0 reduce-scatter.16
  1610.5 44.4 all-gather.12
  1660.6 73.7 reduce-scatter.10
  1738.8 44.4 all-gather.14
  1850.0 74.1 reduce-scatter.16
  (6 shorter events, 123.5 us)
Sparse Core Ops, SparseCore 1:
  1938.8 50.3 all-reduce.4
where the time goes:
time: 2310 us
  waiting for transfers between devices  1360 us (59%)
  blocking collectives  435 us (19%)
  matrix products  278 us (12%)
  other arithmetic  158 us (7%)
  local copies, waits for them, and re-layouts  46.8 us (2%)
    psum x1, blocking collectives, totals(): lax.psum((g_gain_one, g_bias_one, g_b_out, g_gain_two, g_bias_two, g_b_do...  344 us
    reduce_scatter x3, waiting for transfers between devices, layer_forward(): lax.psum_scatter(local_dot(mixed_heads, w_out).astype(jnp.bfloat16), 'ten...  218 us
    reduce_scatter x3, waiting for transfers between devices, layer_backward(): lax.psum_scatter(back_dot(grad_up, w_up).astype(jnp.bfloat16), 'tensor',...  218 us
    reduce_scatter x3, waiting for transfers between devices, layer_forward(): lax.psum_scatter(local_dot(activated, w_down).astype(jnp.bfloat16), 'tens...  196 us
    reduce_scatter x3, waiting for transfers between devices, layer_backward(): lax.psum_scatter(back_dot(flat_grad, w_flat).astype(jnp.bfloat16), 'tenso...  182 us
    all_gather x3, waiting for transfers between devices, layer_backward(): grad_down_all = lax.all_gather(grad_down, 'tensor', axis=0, tiled=True)  135 us
    all_gather x3, waiting for transfers between devices, layer_forward(): normed_two_all = lax.all_gather(normed_two, 'tensor', axis=0, tiled=True)  134 us
    all_gather x3, waiting for transfers between devices, layer_forward(): normed_all = lax.all_gather(normed, 'tensor', axis=0, tiled=True)  132 us
  transfers between devices with their start and end apart: 37, of which 30 were waited for; matrix products, arithmetic and copies ran while one was open for 10% of the time, Pallas kernels for 0%

commit v1 on v0

v1 whole, which is shorter than its diff:
```python
import functools
import math

import jax
import jax.numpy as jnp
from jax import lax
from jax.experimental import pallas as pl
from jax.experimental.pallas import tpu as pltpu
from jax.sharding import PartitionSpec as P

HEAD_DIM = 64
EPSILON = 1e-05
MASK_FILL = -1e30
BASE_TWO_SCALE = 0.125 * math.log2(math.e)
SIDE = 4
TILE = 256
LOW = jnp.bfloat16
FULL = jnp.float32


def move_z(block, distance):
    route = [
        (x * SIDE + z, x * SIDE + (z + distance) % SIDE) for x in range(SIDE) for z in range(SIDE)
    ]
    return lax.ppermute(block, "tensor", route)


def move_x(block, distance):
    route = [
        (x * SIDE + z, (x + distance) % SIDE * SIDE + z) for x in range(SIDE) for z in range(SIDE)
    ]
    return lax.ppermute(block, "tensor", route)


def move_y(block, distance):
    return lax.ppermute(block, "ctx", [(y, (y + distance) % SIDE) for y in range(SIDE)])


def move_y_open(block, distance):
    route = [(y, y + distance) for y in range(SIDE) if 0 <= y + distance < SIDE]
    return lax.ppermute(block, "ctx", route)


def move_x_in(block, distance, section):
    base = section * SIDE * SIDE
    route = [
        (base + x * SIDE + z, base + (x + distance) % SIDE * SIDE + z)
        for x in range(SIDE)
        for z in range(SIDE)
    ]
    return lax.ppermute(block, ("section", "tensor"), route)


def move_y_in(block, distance, section):
    base = section * SIDE
    route = [(base + y, base + (y + distance) % SIDE) for y in range(SIDE)]
    return lax.ppermute(block, ("section", "ctx"), route)


def swap(block):
    return lax.ppermute(block, "section", [(0, 1), (1, 0)])


def send_to(block, section):
    return lax.ppermute(block, "section", [(1 - section, section)])


def gather_z(rows):
    return jnp.concatenate([rows] + [move_z(rows, d) for d in range(1, SIDE)], axis=0)


def scatter_z(rows):
    chunks = rows.reshape(SIDE, rows.shape[0] // SIDE, rows.shape[1])
    total = chunks[0].astype(FULL)
    for d in range(1, SIDE):
        total = total + move_z(chunks[d], -d).astype(FULL)
    return total


def even_sum(block, move):
    low = block.astype(FULL)
    return (low + move(block, 2).astype(FULL)) + (
        move(block, 1).astype(FULL) + move(block, 3).astype(FULL)
    )


def layer_norm(values, gain, bias):
    center = values - jnp.mean(values, axis=-1, keepdims=True)
    spread = jnp.mean(center * center, axis=-1, keepdims=True)
    return center * lax.rsqrt(spread + EPSILON) * gain + bias


def local_dot(left, right):
    return jnp.dot(left, right, preferred_element_type=FULL)


def back_dot(left, right):
    return jnp.einsum("rf,df->rd", left, right, preferred_element_type=FULL)


def outer_sum(left, right):
    return jnp.einsum("rd,rf->df", left, right, preferred_element_type=FULL)


def nt_dot(left, right):
    return lax.dot_general(left, right, (((1,), (1,)), ((), ())), preferred_element_type=FULL)


def tn_dot(left, right):
    return lax.dot_general(left, right, (((0,), (0,)), ((), ())), preferred_element_type=FULL)


def attend_kernel(
    block_ref, low_ref, high_ref, key_ref, own_ref, kv1_ref, kv2_ref, kv3_ref, out_ref, peak, total, mixed
):
    block = block_ref[0]
    rows_all = own_ref.shape[0]

    @pl.loop(0, rows_all // TILE)
    def _(index):
        rows = pl.ds(pl.multiple_of(index * TILE, TILE), TILE)
        queries = own_ref[rows, 128:256]
        low = low_ref[rows, :]
        high = high_ref[rows, :]

        def scores(key_values, shift):
            places = key_ref[...] - shift
            raw = nt_dot(queries, key_values)
            allowed = places >= low
            if shift == 0:
                allowed = allowed & (places <= high)
            return jnp.where(allowed, raw, MASK_FILL)

        own = own_ref[:, 0:128]
        raw = scores(own, 0)
        top = jnp.max(raw, axis=1, keepdims=True)
        weight = jnp.exp2((raw - top) * BASE_TWO_SCALE)
        peak[...] = top
        total[...] = jnp.sum(weight, axis=1, keepdims=True)
        mixed[...] = local_dot(weight.astype(LOW), own)
        for d, other_ref in enumerate((kv1_ref, kv2_ref, kv3_ref), 1):

            @pl.when(block >= d)
            def _(d=d, other_ref=other_ref):
                other = other_ref[...]
                raw = scores(other, d * rows_all)
                old = peak[...]
                top = jnp.maximum(old, jnp.max(raw, axis=1, keepdims=True))
                keep = jnp.exp2((old - top) * BASE_TWO_SCALE)
                weight = jnp.exp2((raw - top) * BASE_TWO_SCALE)
                peak[...] = top
                total[...] = total[...] * keep + jnp.sum(weight, axis=1, keepdims=True)
                mixed[...] = mixed[...] * keep + local_dot(weight.astype(LOW), other)

        count = total[...]
        level = peak[...] * BASE_TWO_SCALE + jnp.log2(count)
        lanes = lax.broadcasted_iota(jnp.int32, (TILE, 128), 1)
        out_ref[rows, :] = jnp.where(lanes < HEAD_DIM, level, mixed[...] / count)


def attend_back_kernel(
    block_ref,
    low_ref,
    high_ref,
    key_ref,
    own_ref,
    kv1_ref,
    kv2_ref,
    kv3_ref,
    kept_ref,
    grad_ref,
    dq_ref,
    d0_ref,
    d1_ref,
    d2_ref,
    d3_ref,
    query_sum,
    key_sum,
):
    block = block_ref[0]
    rows_all = own_ref.shape[0]
    for d, (kv_ref, out_ref) in enumerate(
        ((own_ref, d0_ref), (kv1_ref, d1_ref), (kv2_ref, d2_ref), (kv3_ref, d3_ref))
    ):

        @pl.when(block >= d)
        def _(d=d, kv_ref=kv_ref, out_ref=out_ref):
            key_sum[...] = jnp.zeros_like(key_sum)

            @pl.loop(0, rows_all // TILE)
            def _(index):
                rows = pl.ds(pl.multiple_of(index * TILE, TILE), TILE)
                key_values = kv_ref[:, 0:128]
                queries = own_ref[rows, 128:256]
                grad = grad_ref[rows, :]
                kept = kept_ref[rows, :]
                level = kept.T[0:1, :]
                meet = jnp.sum((kept * grad.astype(FULL)).T, axis=0, keepdims=True)
                places = key_ref[...] - d * rows_all
                allowed = places >= low_ref[index]
                if d == 0:
                    allowed = allowed & (places <= high_ref[index])
                raw = nt_dot(key_values, queries)
                probs = jnp.where(allowed, jnp.exp2(raw * BASE_TWO_SCALE - level), 0.0)
                grad_scores = (probs * (nt_dot(key_values, grad) - meet)).astype(LOW)
                key_sum[...] += local_dot(grad_scores, queries) * 0.125 + local_dot(
                    probs.astype(LOW), grad
                )
                part = tn_dot(grad_scores, key_values) * 0.125
                if d == 0:
                    query_sum[rows, :] = part
                else:
                    query_sum[rows, :] += part

            out_ref[...] = key_sum[...].astype(LOW)

        if d > 0:

            @pl.when(block < d)
            def _(out_ref=out_ref):
                out_ref[...] = jnp.zeros_like(out_ref)

    lanes = lax.broadcasted_iota(jnp.int32, dq_ref.shape, 1)
    dq_ref[...] = jnp.where(lanes < HEAD_DIM, query_sum[...], 0.0).astype(LOW)


VMEM_SPEC = pl.BlockSpec(memory_space=pltpu.VMEM)
SMEM_SPEC = pl.BlockSpec(memory_space=pltpu.SMEM)


def attend(spots, own, others):
    rows = own.shape[0]
    return pl.pallas_call(
        attend_kernel,
        out_shape=jax.ShapeDtypeStruct((rows, 128), FULL),
        in_specs=[SMEM_SPEC] + [VMEM_SPEC] * 7,
        out_specs=VMEM_SPEC,
        scratch_shapes=[
            pltpu.VMEM((TILE, 1), FULL),
            pltpu.VMEM((TILE, 1), FULL),
            pltpu.VMEM((TILE, 128), FULL),
        ],
        compiler_params=pltpu.CompilerParams(vmem_limit_bytes=40 << 20),
        cost_estimate=pl.CostEstimate(
            flops=4 * rows * 2 * rows * 128, bytes_accessed=4 << 20, transcendentals=rows * 2 * rows
        ),
        name="attend",
    )(
        spots["block"],
        spots["low"].reshape(rows, 1),
        spots["place"].reshape(rows, 1),
        spots["place"].reshape(1, rows),
        own,
        *others,
    )


def attend_back(spots, own, others, kept, grad):
    rows = own.shape[0]
    tiles = rows // TILE
    return pl.pallas_call(
        attend_back_kernel,
        out_shape=[jax.ShapeDtypeStruct((rows, 128), LOW)] * 5,
        in_specs=[SMEM_SPEC] + [VMEM_SPEC] * 9,
        out_specs=[VMEM_SPEC] * 5,
        scratch_shapes=[pltpu.VMEM((rows, 128), FULL), pltpu.VMEM((rows, 128), FULL)],
        compiler_params=pltpu.CompilerParams(vmem_limit_bytes=40 << 20),
        cost_estimate=pl.CostEstimate(
            flops=10 * rows * 2 * rows * 128, bytes_accessed=6 << 20, transcendentals=rows * 2 * rows
        ),
        name="attend_back",
    )(
        spots["block"],
        spots["low"].reshape(tiles, 1, TILE),
        spots["place"].reshape(tiles, 1, TILE),
        spots["place"].reshape(rows, 1),
        own,
        *others,
        kept,
        grad,
    )


def layer_forward(residual, spots, params):
    (gain_one, bias_one, b_out, gain_two, bias_two, b_down), bias_qkv, b_up, w_qkv, w_out, w_up, w_down = params
    normed = layer_norm(residual, gain_one, bias_one).astype(LOW)
    normed_all = gather_z(normed)
    projected = (local_dot(normed_all, w_qkv) + bias_qkv).astype(LOW)
    width = projected.shape[1] // SIDE
    pieces = [projected[:, d * width : (d + 1) * width] for d in range(SIDE)]
    own = jnp.concatenate([pieces[0]] + [move_x(pieces[d], -d) for d in range(1, SIDE)], axis=0)
    others = [move_y_open(own[:, 0:128], d) for d in range(1, SIDE)]
    kept = attend(spots, own, others)
    lanes = lax.broadcasted_iota(jnp.int32, kept.shape, 1)
    mixed = jnp.where(lanes < HEAD_DIM, 0.0, kept).astype(LOW)
    rows = mixed.shape[0] // SIDE
    mixed_rows = jnp.concatenate(
        [mixed[0:rows]] + [move_x(mixed[d * rows : (d + 1) * rows], d) for d in range(1, SIDE)], axis=1
    )
    hidden = residual + (scatter_z(local_dot(mixed_rows, w_out).astype(LOW)) + b_out)
    normed_two_all = gather_z(layer_norm(hidden, gain_two, bias_two).astype(LOW))
    up_value = local_dot(normed_two_all, w_up) + b_up
    activated = jax.nn.gelu(up_value).astype(LOW)
    result = hidden + (scatter_z(local_dot(activated, w_down).astype(LOW)) + b_down)
    return result, (
        residual, normed_all, own, others, kept, mixed_rows, hidden, normed_two_all, up_value, activated
    )


def layer_backward(grad_out, stored, spots, params, section):
    (gain_one, bias_one, b_out, gain_two, bias_two, b_down), bias_qkv, b_up, w_qkv, w_out, w_up, w_down = params
    residual, normed_all, own, others, kept, mixed_rows, hidden, normed_two_all, up_value, activated = stored
    grad_down = grad_out.astype(LOW)
    g_b_down = jnp.sum(grad_down.astype(FULL), axis=0)
    grad_down_all = gather_z(grad_down)
    _, gelu_pull = jax.vjp(jax.nn.gelu, up_value)
    (grad_up,) = gelu_pull(back_dot(grad_down_all, w_down))
    grad_up = grad_up.astype(LOW)
    grad_normed_two = scatter_z(back_dot(grad_up, w_up).astype(LOW))
    g_w_down = outer_sum(activated, grad_down_all).astype(LOW)
    g_b_up = jnp.sum(grad_up.astype(FULL), axis=0)
    g_w_up = outer_sum(normed_two_all, grad_up).astype(LOW)
    _, norm_two_pull = jax.vjp(layer_norm, hidden, gain_two, bias_two)
    grad_hidden_part, g_gain_two, g_bias_two = norm_two_pull(grad_normed_two)
    grad_hidden = grad_out + grad_hidden_part
    grad_attn = grad_hidden.astype(LOW)
    g_b_out = jnp.sum(grad_attn.astype(FULL), axis=0)
    grad_attn_all = gather_z(grad_attn)
    grad_mixed = back_dot(grad_attn_all, w_out).astype(LOW)
    pieces = [grad_mixed[:, d * 128 : (d + 1) * 128] for d in range(SIDE)]
    grad_mixed_own = jnp.concatenate(
        [pieces[0]] + [move_x(pieces[d], -d) for d in range(1, SIDE)], axis=0
    )
    g_w_out = outer_sum(mixed_rows, grad_attn_all).astype(LOW)
    dq, dkv0, dkv1, dkv2, dkv3 = attend_back(spots, own, others, kept, grad_mixed_own)
    dkv = dkv0.astype(FULL)
    for d, part in enumerate((dkv1, dkv2, dkv3), 1):
        dkv = dkv + move_y_open(part, -d).astype(FULL)
    grad_own = jnp.concatenate([dkv.astype(LOW), dq], axis=1)
    rows = grad_own.shape[0] // SIDE
    grad_qkv = jnp.concatenate(
        [grad_own[0:rows]] + [move_x(grad_own[d * rows : (d + 1) * rows], d) for d in range(1, SIDE)],
        axis=1,
    )
    grad_normed = scatter_z(back_dot(grad_qkv, w_qkv).astype(LOW))
    g_w_qkv = outer_sum(normed_all, grad_qkv).astype(LOW)
    g_b_qkv = jnp.sum(grad_qkv.astype(FULL), axis=0)
    _, norm_one_pull = jax.vjp(layer_norm, residual, gain_one, bias_one)
    grad_residual_part, g_gain_one, g_bias_one = norm_one_pull(grad_normed)
    grad_residual = grad_hidden + grad_residual_part
    vectors = jnp.stack([g_gain_one, g_bias_one, g_b_out, g_gain_two, g_bias_two, g_b_down])
    split = jnp.concatenate([g_b_up.reshape(SIDE, TILE), g_b_qkv.reshape(SIDE, TILE)], axis=1)
    w_out_rows = g_w_out.reshape(SIDE, 2, HEAD_DIM, -1)[:, 1].reshape(SIDE * HEAD_DIM, -1)
    weights = (
        settle(g_w_qkv, 1, section),
        settle(w_out_rows, 0, section),
        settle(g_w_up, 1, section),
        settle(g_w_down, 0, section),
    )
    return grad_residual, vectors, split, weights


def settle(grads, axis, section):
    both = (grads.astype(FULL) + send_to(grads, section).astype(FULL)).astype(LOW)
    pieces = jnp.split(both, SIDE, axis=axis)
    total = pieces[0].astype(FULL)
    for d in range(1, SIDE):
        total = total + move_x_in(pieces[d], -d, section).astype(FULL)
    return even_sum(total.astype(LOW), lambda block, d: move_y_in(block, d, section))


def collect(shard, axis, section, here, pad=None):
    pieces = [shard] + [move_x_in(shard, d, section) for d in range(1, SIDE)]
    if pad is not None:
        pieces = [part for piece in pieces for part in (pad, piece)]
    whole = jnp.concatenate(pieces, axis=axis)
    return jnp.where(here == section, whole, send_to(whole, 1 - section))


def per_device(
    inputs,
    segments,
    gain_one,
    bias_one,
    w_qkv,
    b_qv,
    w_out,
    b_out,
    gain_two,
    bias_two,
    w_up,
    b_up,
    w_down,
    b_down,
    cotangent,
):
    here = lax.axis_index("section")
    block = lax.axis_index("ctx")
    spot = lax.axis_index("tensor")
    x_here, z_here = spot // SIDE, spot % SIDE
    row_count, model_width = inputs.shape[2], inputs.shape[3]
    block_rows = row_count * SIDE * SIDE

    sequence = lax.dynamic_index_in_dim(inputs, here, 0, False)[0].astype(FULL)
    grad_last = lax.dynamic_index_in_dim(cotangent, here, 0, False)[0].astype(FULL)
    segment_ids = lax.dynamic_index_in_dim(segments, here, 0, False)
    start_one = jnp.sum((segment_ids < 1).astype(jnp.int32))
    start_two = jnp.sum((segment_ids < 2).astype(jnp.int32))
    order = jnp.arange(block_rows)
    from_x = (x_here + order // (block_rows // SIDE)) % SIDE
    from_z = (z_here - order // row_count % SIDE) % SIDE
    place = block * block_rows + (from_x * SIDE + from_z) * row_count + order % row_count
    low = jnp.where(place >= start_two, start_two, jnp.where(place >= start_one, start_one, 0))
    spots = {
        "block": block.reshape(1).astype(jnp.int32),
        "place": place.astype(jnp.int32),
        "low": low.astype(jnp.int32),
    }

    gap = jnp.zeros((HEAD_DIM,), LOW)
    small = jnp.concatenate(
        [gain_one, bias_one, b_out, gain_two, bias_two, b_down]
        + [
            jnp.concatenate(
                [b_up[0], gap, b_qv[0, 1], b_qv[0, 0], gap, jnp.zeros((model_width - 512,), LOW)]
            )[None],
            jnp.zeros((1, model_width), LOW),
        ],
        axis=0,
    )
    small_other = swap(small)
    smalls = (
        jnp.where(here == 0, small, small_other),
        jnp.where(here == 0, small_other, small),
    )
    split_own = jnp.stack([smalls[0][6, :512], smalls[1][6, :512]])
    split_all = [split_own] + [move_x(split_own, d) for d in range(1, SIDE)]
    w_kvq = jnp.concatenate(
        [w_qkv[0, :, 1], w_qkv[0, :, 2], w_qkv[0, :, 0], jnp.zeros((model_width, HEAD_DIM), LOW)],
        axis=1,
    )
    gap_rows = jnp.zeros((HEAD_DIM, model_width), LOW)
    params = []
    for section in range(2):
        vectors = tuple(smalls[section][row].astype(FULL) for row in range(6))
        bias_up = jnp.concatenate([part[section, 0:256] for part in split_all]).astype(FULL)
        bias_qkv = jnp.concatenate([part[section, 256:512] for part in split_all]).astype(FULL)
        params.append(
            (
                vectors,
                bias_qkv,
                bias_up,
                collect(w_kvq, 1, section, here),
                collect(w_out[0], 0, section, here, gap_rows),
                collect(w_up[0], 1, section, here),
                collect(w_down[0], 0, section, here),
            )
        )

    middle, stored_first = layer_forward(sequence, spots, params[0])
    result, stored_last = layer_forward(middle.astype(LOW).astype(FULL), spots, params[1])
    grad_middle, vectors_last, split_last, weights_last = layer_backward(
        grad_last, stored_last, spots, params[1], 1
    )
    grad_first, vectors_first, split_first, weights_first = layer_backward(
        grad_middle.astype(LOW).astype(FULL), stored_first, spots, params[0], 0
    )

    passed = swap(jnp.where(here == 0, result, grad_first))
    kept = jnp.where(here == 0, grad_first, result)
    boundary = jnp.where(here == 0, jnp.stack([kept, passed]), jnp.stack([passed, kept]))
    boundary = boundary.reshape(1, 2, 1, row_count, model_width)

    pad = jnp.zeros((2, model_width), FULL)
    mine = jnp.where(here == 0, vectors_first, vectors_last)
    theirs = jnp.where(here == 0, vectors_last, vectors_first)
    split_mine = jnp.where(here == 0, split_first, split_last)
    split_theirs = jnp.where(here == 0, split_last, split_first)
    sent = jnp.concatenate([theirs, split_theirs.reshape(2, -1)], axis=0)
    arrived = swap(sent)
    vectors = mine + arrived[:6]
    split = split_mine + arrived[6:].reshape(split_mine.shape)
    vectors = even_sum(vectors, move_z)
    packs = [
        jnp.concatenate(
            [vectors, jnp.pad(split[d], (0, model_width - 512))[None], jnp.zeros((1, model_width), FULL)],
            axis=0,
        )
        for d in range(SIDE)
    ]
    pack = (packs[0] + move_x(packs[2], -2)) + (move_x(packs[1], -1) + move_x(packs[3], -3))
    pack = even_sum(pack, move_y)

    def pick(index):
        return jnp.where(here == 0, weights_first[index], weights_last[index])

    g_kvq = pick(0)
    g_w_qkv = jnp.stack([g_kvq[:, 128:192], g_kvq[:, 0:64], g_kvq[:, 64:128]], axis=1)
    g_b_qv = jnp.stack([pack[6, 384:448], pack[6, 320:384]])
    return (
        boundary,
        pack[0:1],
        pack[1:2],
        g_w_qkv[None],
        g_b_qv[None],
        pick(1)[None],
        pack[2:3],
        pack[3:4],
        pack[4:5],
        pick(2)[None],
        pack[6:7, 0:256],
        pick(3)[None],
        pack[5:6],
    )


def solution(mesh):
    return jax.shard_map(
        per_device,
        mesh=mesh,
        in_specs=(
            P(None, "ctx", "tensor", None),
            P(),
            P("section", None),
            P("section", None),
            P("section", None, None, "tensor"),
            P("section", None, "tensor"),
            P("section", "tensor", None),
            P("section", None),
            P("section", None),
            P("section", None),
            P("section", None, "tensor"),
            P("section", "tensor"),
            P("section", "tensor", None),
            P("section", None),
            P(None, "ctx", "tensor", None),
        ),
        out_specs=(
            P("section", None, "ctx", "tensor", None),
            P("section", None),
            P("section", None),
            P("section", None, None, "tensor"),
            P("section", None, "tensor"),
            P("section", "tensor", None),
            P("section", None),
            P("section", None),
            P("section", None),
            P("section", None, "tensor"),
            P("section", "tensor"),
            P("section", "tensor", None),
            P("section", None),
        ),
        check_vma=False,
    )
```

time: 2310 us -> 753 us (0.33)
  waiting for transfers between devices: 1360 us -> 176 us
  blocking collectives: 435 us -> 0 us
  starting transfers between devices: 9.07 us -> 413 us
  matrix products: 278 us -> 38.9 us
  other arithmetic: 158 us -> 55.1 us
    reduce_scatter x18 -> x0, waiting for transfers between devices: 858 us -> none  [the longest x3 218 us: layer_forward(): lax.psum_scatter(local_dot(mixed_heads, w_out).astype(jnp.bfloat16), 'ten...]
    all_gather x12 -> x0, waiting for transfers between devices: 497 us -> none  [the longest x3 135 us: layer_backward(): grad_down_all = lax.all_gather(grad_down, 'tensor', axis=0, tiled=True)]
    ppermute x6 -> x187, starting transfers between devices: 7.77 us -> 413 us  [the longest x51 101 us: move_z(): return lax.ppermute(block, 'tensor', route)]
    psum x2 -> x0, blocking collectives: 354 us -> none  [the longest x1 344 us: totals(): lax.psum((g_gain_one, g_bias_one, g_b_out, g_gain_two, g_bias_two, g_b_do...]
    dot_general x57 -> x24, matrix products: 278 us -> 38.9 us  [the longest x8 17.4 us: outer_sum(): return jnp.einsum('rd,rf->df', left, right, preferred_element_type=FULL)]
    ppermute x6 -> x187, waiting for transfers between devices: 5.35 us -> 176 us  [the longest x51 59.7 us: move_z(): return lax.ppermute(block, 'tensor', route)]
    all_gather x6 -> x0, blocking collectives: 80.8 us -> none  [the longest x3 40.9 us: layer_forward(): lax.all_gather(key_rows, 'ctx', axis=0, tiled=True)]
    convert_element_type x38 -> x28, other arithmetic: 57.3 us -> 19.4 us  [the longest x8 12.1 us: settle(): (grads.astype(FULL) + send_to(grads, section).astype(FULL)).astype(LOW)]
  transfers between devices with their start and end apart: 37 -> 187, of which waited for: 30 -> 66; matrix products, arithmetic and copies ran while one was open for 10% -> 16% of each run, Pallas kernels for 0% -> 2%
where the time goes in v1:
time: 753 us; the launch traced here: 743 us
  starting transfers between devices  413 us (55%)
  waiting for transfers between devices  176 us (23%)
  other arithmetic  55.1 us (7%)
  matrix products  38.9 us (5%)
  local copies, waits for them, and re-layouts  38.3 us (5%)
  Pallas kernels  15.5 us (2%)
    ppermute x51, starting transfers between devices, move_z(): return lax.ppermute(block, 'tensor', route)  101 us
    ppermute x48, starting transfers between devices, move_x_in(): return lax.ppermute(block, ('section', 'tensor'), route)  98.8 us
    ppermute x24, starting transfers between devices, move_y_in(): return lax.ppermute(block, ('section', 'ctx'), route)  70 us
    ppermute x51, waiting for transfers between devices, move_z(): return lax.ppermute(block, 'tensor', route)  59.7 us
    ppermute x30, starting transfers between devices, move_x(): return lax.ppermute(block, 'tensor', route)  40 us
    ppermute x12, waiting for transfers between devices, move_y_open(): return lax.ppermute(block, 'ctx', route)  39.6 us
    ppermute x30, waiting for transfers between devices, move_x(): return lax.ppermute(block, 'tensor', route)  32.8 us
    ppermute x48, waiting for transfers between devices, move_x_in(): return lax.ppermute(block, ('section', 'tensor'), route)  29.3 us
  transfers between devices with their start and end apart: 187, of which 66 were waited for; matrix products, arithmetic and copies ran while one was open for 16% of the time, Pallas kernels for 2%

profile of v1, /device:TPU:0, one launch (start us, length us, event | category | flops | bytes accessed | tf_op | source)
XLA Modules:
  0.0 742.8 jit_solution(3508341373951689275)
XLA Ops:
  20.3 5.6 collective-permute-done.11
  83.4 9.4 %collective-permute-done.18 = bf16[256,256]{1,0:T(8,128)(2,1)S(1)} collective-permute-done((bf16[256,256]{1,0:T(8,128)(2,1)S(1)}, bf16[256,256]{1,0:T(8,128)(2,1)S(1)}, u32[]{:S(2)}, u32[]{:S(2)}) %collective-permute-start.18) | collective-permute-done | bytes 131104 | tf_op jit(solution)/shard_map/ppermute | solution.py:32
  92.8 5.5 collective-permute-start.42
  99.7 5.3 collective-permute-start.23
  136.7 10.7 %collective-permute-start.31 = (bf16[64,1024]{1,0:T(8,128)(2,1)}, bf16[64,1024]{1,0:T(8,128)(2,1)S(1)}, u32[]{:S(2)}, u32[]{:S(2)}) collective-permute-start(bf16[64,1024]{1,0:T(8,128)(2,1)} %get-tuple-element.167), channel_id=1, source_target_pairs={{0,12},{4,0},{8,4},{12,8},{16,28},{20,16},{24,20},{28,24},{32,44},... | collective-permute-start | bytes 393224 | tf_op jit(solution)/shard_map/ppermute | solution.py:25
  200.4 6.8 collective-permute-start.56
  213.5 6.3 collective-permute-start.60
  225.4 5.7 collective-permute-done.60.kv3_ref
  255.3 15.1 %collective-permute-start.73 = (bf16[64,1024]{1,0:T(8,128)(2,1)S(1)}, bf16[64,1024]{1,0:T(8,128)(2,1)S(1)}, u32[]{:S(2)}, u32[]{:S(2)}) collective-permute-start(bf16[64,1024]{1,0:T(8,128)(2,1)S(1)} %add_convert_fusion.19), channel_id=1, source_target_pairs={{0,12},{4,0},{8,4},{12,8},{16,28},{20,16},{24,20},{28,24},{32,44},... | collective-permute-start | bytes 393224 | tf_op jit(solution)/shard_map/ppermute | solution.py:25
  270.4 8.9 %collective-permute-start.72 = (bf16[64,1024]{1,0:T(8,128)(2,1)S(1)}, bf16[64,1024]{1,0:T(8,128)(2,1)S(1)}, u32[]{:S(2)}, u32[]{:S(2)}) collective-permute-start(bf16[64,1024]{1,0:T(8,128)(2,1)S(1)} %add_convert_fusion.19), channel_id=1, source_target_pairs={{0,8},{4,12},{8,0},{12,4},{16,24},{20,28},{24,16},{28,20},{32,40},... | collective-permute-start | bytes 393224 | tf_op jit(solution)/shard_map/ppermute | solution.py:25
  279.3 8.9 %collective-permute-start.71 = (bf16[64,1024]{1,0:T(8,128)(2,1)S(1)}, bf16[64,1024]{1,0:T(8,128)(2,1)S(1)}, u32[]{:S(2)}, u32[]{:S(2)}) collective-permute-start(bf16[64,1024]{1,0:T(8,128)(2,1)S(1)} %add_convert_fusion.19), channel_id=1, source_target_pairs={{0,4},{4,8},{8,12},{12,0},{16,20},{20,24},{24,28},{28,16},{32,36},... | collective-permute-start | bytes 393224 | tf_op jit(solution)/shard_map/ppermute | solution.py:25
  347.7 6.0 collective-permute-done.87
  353.7 6.8 collective-permute-done.88
  360.4 5.5 collective-permute-done.89
  386.4 5.2 collective-permute-done.94
  453.2 5.6 collective-permute-done.108
  461.9 5.6 collective-permute-done.110
  533.0 7.2 collective-permute-start.130
  540.2 8.9 %collective-permute-start.129 = (f32[8,1024]{1,0:T(8,128)S(1)}, f32[8,1024]{1,0:T(8,128)S(1)}, u32[]{:S(2)}, u32[]{:S(2)}) collective-permute-start(f32[8,1024]{1,0:T(8,128)S(1)} %fusion.75), channel_id=1, source_target_pairs={{0,1},{1,2},{2,3},{3,0},{4,5},{5,6},{6,7},{7,4},{8,9},{9,10},{10,1... | collective-permute-start | bytes 98312 | tf_op jit(solution)/shard_map/ppermute | solution.py:36
  553.0 10.2 %collective-permute-start.128 = (f32[8,1024]{1,0:T(8,128)S(1)}, f32[8,1024]{1,0:T(8,128)S(1)}, u32[]{:S(2)}, u32[]{:S(2)}) collective-permute-start(f32[8,1024]{1,0:T(8,128)S(1)} %fusion.75), channel_id=1, source_target_pairs={{0,2},{1,3},{2,0},{3,1},{4,6},{5,7},{6,4},{7,5},{8,10},{9,11},{10,... | collective-permute-start | bytes 98312 | tf_op jit(solution)/shard_map/ppermute | solution.py:36
  594.4 20.9 %collective-permute-start.120 = (f32[64,1024]{1,0:T(8,128)S(1)}, f32[64,1024]{1,0:T(8,128)S(1)}, u32[]{:S(2)}, u32[]{:S(2)}) collective-permute-start(f32[64,1024]{1,0:T(8,128)S(1)} %broadcast_select_fusion.28), channel_id=1, source_target_pairs={{0,64},{64,0},{1,65},{65,1},{2,66},{66,2},{3,67},{67,3},{4,68},{68... | collective-permute-start | bytes 786440 | tf_op jit(solution)/shard_map/ppermute | solution.py:61
  633.5 6.9 collective-permute-done.162
  641.1 8.8 %collective-permute-start.186 = (bf16[256,1024]{1,0:T(8,128)(2,1)S(1)}, bf16[256,1024]{1,0:T(8,128)(2,1)S(1)}, u32[]{:S(2)}, u32[]{:S(2)}) collective-permute-start(bf16[256,1024]{1,0:T(8,128)(2,1)S(1)} %add_convert_fusion.6), channel_id=1, source_target_pairs={{64,67},{65,64},{66,65},{67,66},{68,71},{69,68},{70,69},{71,70},{7... | collective-permute-start | bytes 1572872 | tf_op jit(solution)/shard_map/ppermute | solution.py:57
  651.4 12.1 %collective-permute-start.184 = (bf16[256,1024]{1,0:T(8,128)(2,1)S(1)}, bf16[256,1024]{1,0:T(8,128)(2,1)S(1)}, u32[]{:S(2)}, u32[]{:S(2)}) collective-permute-start(bf16[256,1024]{1,0:T(8,128)(2,1)S(1)} %add_convert_fusion.6), channel_id=1, source_target_pairs={{64,66},{65,67},{66,64},{67,65},{68,70},{69,71},{70,68},{71,69},{7... | collective-permute-start | bytes 1572872 | tf_op jit(solution)/shard_map/ppermute | solution.py:57
  (984 shorter events, 539.7 us)
Async XLA Ops:
  13.5 44.8 %collective-permute-start.29 = (bf16[64,1024]{1,0:T(8,128)(2,1)}, bf16[64,1024]{1,0:T(8,128)(2,1)S(1)}, u32[]{:S(2)}, u32[]{:S(2)}) collective-permute-start(bf16[64,1024]{1,0:T(8,128)(2,1)} %bitcast.11), channel_id=1, source_target_pairs={{0,48},{4,52},{8,56},{12,60},{16,0},{20,4},{24,8},{28,12},{32,16},... | collective-permute-start | bytes 393224 | tf_op jit(solution)/shard_map/ppermute | solution.py:51
  68.8 29.5 %collective-permute-start.39 = (bf16[1024,256]{1,0:T(8,128)(2,1)S(1)}, bf16[1024,256]{1,0:T(8,128)(2,1)S(1)}, u32[]{:S(2)}, u32[]{:S(2)}) collective-permute-start(bf16[1024,256]{1,0:T(8,128)(2,1)S(1)} %bitcast.144), channel_id=1, source_target_pairs={{0,48},{4,52},{8,56},{12,60},{16,0},{20,4},{24,8},{28,12},{32,16},... | collective-permute-start | bytes 1572872 | tf_op jit(solution)/shard_map/ppermute | solution.py:51
  72.0 27.7 %collective-permute-start.38 = (bf16[1024,256]{1,0:T(8,128)(2,1)S(1)}, bf16[1024,256]{1,0:T(8,128)(2,1)S(1)}, u32[]{:S(2)}, u32[]{:S(2)}) collective-permute-start(bf16[1024,256]{1,0:T(8,128)(2,1)S(1)} %bitcast.145), channel_id=1, source_target_pairs={{0,32},{4,36},{8,40},{12,44},{16,48},{20,52},{24,56},{28,60},{32,0... | collective-permute-start | bytes 1572872 | tf_op jit(solution)/shard_map/ppermute | solution.py:51
  75.3 29.7 %collective-permute-start.37 = (bf16[1024,256]{1,0:T(8,128)(2,1)S(1)}, bf16[1024,256]{1,0:T(8,128)(2,1)S(1)}, u32[]{:S(2)}, u32[]{:S(2)}) collective-permute-start(bf16[1024,256]{1,0:T(8,128)(2,1)S(1)} %bitcast.146), channel_id=1, source_target_pairs={{0,16},{4,20},{8,24},{12,28},{16,32},{20,36},{24,40},{28,44},{32,4... | collective-permute-start | bytes 1572872 | tf_op jit(solution)/shard_map/ppermute | solution.py:51
  78.6 29.9 %collective-permute-start.43 = (bf16[256,1024]{1,0:T(8,128)(2,1)S(1)}, bf16[256,1024]{1,0:T(8,128)(2,1)S(1)}, u32[]{:S(2)}, u32[]{:S(2)}) collective-permute-start(bf16[256,1024]{1,0:T(8,128)(2,1)S(1)} %bitcast.130), channel_id=1, source_target_pairs={{0,48},{4,52},{8,56},{12,60},{16,0},{20,4},{24,8},{28,12},{32,16},... | collective-permute-start | bytes 1572872 | tf_op jit(solution)/shard_map/ppermute | solution.py:51
  98.3 33.5 %collective-permute-start.30 = (bf16[512,1024]{1,0:T(8,128)(2,1)S(1)}, bf16[512,1024]{1,0:T(8,128)(2,1)S(1)}, u32[]{:S(2)}, u32[]{:S(2)}) collective-permute-start(bf16[512,1024]{1,0:T(8,128)(2,1)S(1)} %constant_dynamic-update-slice_fusion), channel_id=1, source_target_pairs={{0,64},{1,65},{2,66},{3,67},{4,68},{5,69},{6,70},{7,71},{8,72},{9,... | collective-permute-start | bytes 3145736 | tf_op jit(solution)/shard_map/ppermute | solution.py:65
  124.5 46.6 %collective-permute-start.40 = (bf16[1024,1024]{1,0:T(8,128)(2,1)}, bf16[1024,1024]{1,0:T(8,128)(2,1)}, u32[]{:S(2)}, u32[]{:S(2)}) collective-permute-start(bf16[1024,1024]{1,0:T(8,128)(2,1)} %get-tuple-element.156), channel_id=1, source_target_pairs={{0,64},{1,65},{2,66},{3,67},{4,68},{5,69},{6,70},{7,71},{8,72},{9,... | collective-permute-start | bytes 6291464 | tf_op jit(solution)/shard_map/ppermute | solution.py:65
  131.9 44.5 %collective-permute-start.44 = (bf16[1024,1024]{1,0:T(8,128)(2,1)}, bf16[1024,1024]{1,0:T(8,128)(2,1)}, u32[]{:S(2)}, u32[]{:S(2)}) collective-permute-start(bf16[1024,1024]{1,0:T(8,128)(2,1)} %get-tuple-element.154), channel_id=1, source_target_pairs={{0,64},{1,65},{2,66},{3,67},{4,68},{5,69},{6,70},{7,71},{8,72},{9,... | collective-permute-start | bytes 6291464 | tf_op jit(solution)/shard_map/ppermute | solution.py:65
  207.2 32.5 %collective-permute-start.67 = (bf16[512,1024]{1,0:T(8,128)(2,1)S(1)}, bf16[512,1024]{1,0:T(8,128)(2,1)S(1)}, u32[]{:S(2)}, u32[]{:S(2)}) collective-permute-start(bf16[512,1024]{1,0:T(8,128)(2,1)S(1)} %constant_dynamic-update-slice_fusion.4), channel_id=1, source_target_pairs={{64,0},{65,1},{66,2},{67,3},{68,4},{69,5},{70,6},{71,7},{72,8},{73... | collective-permute-start | bytes 3145736 | tf_op jit(solution)/shard_map/ppermute | solution.py:65
  223.9 66.2 %collective-permute-start.77 = (bf16[1024,1024]{1,0:T(8,128)(2,1)S(1)}, bf16[1024,1024]{1,0:T(8,128)(2,1)S(1)}, u32[]{:S(2)}, u32[]{:S(2)}) collective-permute-start(bf16[1024,1024]{1,0:T(8,128)(2,1)S(1)} %copy-done.32), channel_id=1, source_target_pairs={{64,0},{65,1},{66,2},{67,3},{68,4},{69,5},{70,6},{71,7},{72,8},{73... | collective-permute-start | bytes 6291464 | tf_op jit(solution)/shard_map/ppermute | solution.py:65
  239.7 63.0 %collective-permute-start.6 = (bf16[1024,1024]{1,0:T(8,128)(2,1)S(1)}, bf16[1024,1024]{1,0:T(8,128)(2,1)S(1)}, u32[]{:S(2)}, u32[]{:S(2)}) collective-permute-start(bf16[1024,1024]{1,0:T(8,128)(2,1)S(1)} %copy-done.33), channel_id=1, source_target_pairs={{64,0},{65,1},{66,2},{67,3},{68,4},{69,5},{70,6},{71,7},{72,8},{73... | collective-permute-start | bytes 6291464 | tf_op jit(solution)/shard_map/ppermute | solution.py:65
  255.3 37.8 %collective-permute-start.73 = (bf16[64,1024]{1,0:T(8,128)(2,1)S(1)}, bf16[64,1024]{1,0:T(8,128)(2,1)S(1)}, u32[]{:S(2)}, u32[]{:S(2)}) collective-permute-start(bf16[64,1024]{1,0:T(8,128)(2,1)S(1)} %add_convert_fusion.19), channel_id=1, source_target_pairs={{0,12},{4,0},{8,4},{12,8},{16,28},{20,16},{24,20},{28,24},{32,44},... | collective-permute-start | bytes 393224 | tf_op jit(solution)/shard_map/ppermute | solution.py:25
  310.5 215.8 %collective-permute-start.166 = (bf16[1024,1024]{0,1:T(8,128)(2,1)}, bf16[1024,1024]{0,1:T(8,128)(2,1)}, u32[]{:S(2)}, u32[]{:S(2)}) collective-permute-start(bf16[1024,1024]{0,1:T(8,128)(2,1)} %convolution_convert_fusion.2), channel_id=1, source_target_pairs={{0,64},{1,65},{2,66},{3,67},{4,68},{5,69},{6,70},{7,71},{8,72},{9,... | collective-permute-start | bytes 6291464 | tf_op jit(solution)/shard_map/ppermute | solution.py:65
  324.0 225.1 %collective-permute-start.180 = (bf16[1024,1024]{1,0:T(8,128)(2,1)}, bf16[1024,1024]{1,0:T(8,128)(2,1)}, u32[]{:S(2)}, u32[]{:S(2)}) collective-permute-start(bf16[1024,1024]{1,0:T(8,128)(2,1)} %convolution_convert_fusion), channel_id=1, source_target_pairs={{0,64},{1,65},{2,66},{3,67},{4,68},{5,69},{6,70},{7,71},{8,72},{9,... | collective-permute-start | bytes 6291464 | tf_op jit(solution)/shard_map/ppermute | solution.py:65
  518.3 57.5 %collective-permute-start.138 = (bf16[1024,1024]{0,1:T(8,128)(2,1)}, bf16[1024,1024]{0,1:T(8,128)(2,1)S(1)}, u32[]{:S(2)}, u32[]{:S(2)}) collective-permute-start(bf16[1024,1024]{0,1:T(8,128)(2,1)} %convolution_convert_fusion.4), channel_id=1, source_target_pairs={{0,64},{1,65},{2,66},{3,67},{4,68},{5,69},{6,70},{7,71},{8,72},{9,... | collective-permute-start | bytes 6291464 | tf_op jit(solution)/shard_map/ppermute | solution.py:65
  526.3 26.7 %collective-permute-start.147 = (bf16[64,1024]{1,0:T(8,128)(2,1)S(1)}, bf16[64,1024]{1,0:T(8,128)(2,1)S(1)}, u32[]{:S(2)}, u32[]{:S(2)}) collective-permute-start(bf16[64,1024]{1,0:T(8,128)(2,1)S(1)} %copy-done.94), channel_id=1, source_target_pairs={{0,32},{4,36},{8,40},{12,44},{16,48},{20,52},{24,56},{28,60},{32,0... | collective-permute-start | bytes 393224 | tf_op jit(solution)/shard_map/ppermute | solution.py:51
  533.0 30.2 %collective-permute-start.130 = (f32[8,1024]{1,0:T(8,128)S(1)}, f32[8,1024]{1,0:T(8,128)S(1)}, u32[]{:S(2)}, u32[]{:S(2)}) collective-permute-start(f32[8,1024]{1,0:T(8,128)S(1)} %fusion.75), channel_id=1, source_target_pairs={{0,3},{1,0},{2,1},{3,2},{4,7},{5,4},{6,5},{7,6},{8,11},{9,8},{10,9... | collective-permute-start | bytes 98312 | tf_op jit(solution)/shard_map/ppermute | solution.py:36
  572.2 44.9 %collective-permute-start.173 = (bf16[1024,1024]{1,0:T(8,128)(2,1)S(1)}, bf16[1024,1024]{1,0:T(8,128)(2,1)S(1)}, u32[]{:S(2)}, u32[]{:S(2)}) collective-permute-start(bf16[1024,1024]{1,0:T(8,128)(2,1)S(1)} %copy-done.25), channel_id=1, source_target_pairs={{64,0},{65,1},{66,2},{67,3},{68,4},{69,5},{70,6},{71,7},{72,8},{73... | collective-permute-start | bytes 6291464 | tf_op jit(solution)/shard_map/ppermute | solution.py:65
  577.8 92.7 %collective-permute-start.131 = (bf16[1024,1024]{0,1:T(8,128)(2,1)S(1)}, bf16[1024,1024]{0,1:T(8,128)(2,1)S(1)}, u32[]{:S(2)}, u32[]{:S(2)}) collective-permute-start(bf16[1024,1024]{0,1:T(8,128)(2,1)S(1)} %copy-done.26), channel_id=1, source_target_pairs={{64,0},{65,1},{66,2},{67,3},{68,4},{69,5},{70,6},{71,7},{72,8},{73... | collective-permute-start | bytes 6291464 | tf_op jit(solution)/shard_map/ppermute | solution.py:65
  590.3 30.2 %collective-permute-start.139 = (bf16[1024,256]{0,1:T(8,128)(2,1)S(1)}, bf16[1024,256]{0,1:T(8,128)(2,1)S(1)}, u32[]{:S(2)}, u32[]{:S(2)}) collective-permute-start(bf16[1024,256]{0,1:T(8,128)(2,1)S(1)} %get-tuple-element.118), channel_id=1, source_target_pairs={{64,112},{68,116},{72,120},{76,124},{80,64},{84,68},{88,72},{92,76... | collective-permute-start | bytes 1572872 | tf_op jit(solution)/shard_map/ppermute | solution.py:51
  591.0 32.0 %collective-permute-start.141 = (bf16[1024,256]{0,1:T(8,128)(2,1)S(1)}, bf16[1024,256]{0,1:T(8,128)(2,1)S(1)}, u32[]{:S(2)}, u32[]{:S(2)}) collective-permute-start(bf16[1024,256]{0,1:T(8,128)(2,1)S(1)} %get-tuple-element.119), channel_id=1, source_target_pairs={{64,80},{68,84},{72,88},{76,92},{80,96},{84,100},{88,104},{92,108}... | collective-permute-start | bytes 1572872 | tf_op jit(solution)/shard_map/ppermute | solution.py:51
  641.1 26.6 %collective-permute-start.186 = (bf16[256,1024]{1,0:T(8,128)(2,1)S(1)}, bf16[256,1024]{1,0:T(8,128)(2,1)S(1)}, u32[]{:S(2)}, u32[]{:S(2)}) collective-permute-start(bf16[256,1024]{1,0:T(8,128)(2,1)S(1)} %add_convert_fusion.6), channel_id=1, source_target_pairs={{64,67},{65,64},{66,65},{67,66},{68,71},{69,68},{70,69},{71,70},{7... | collective-permute-start | bytes 1572872 | tf_op jit(solution)/shard_map/ppermute | solution.py:57
  650.7 25.1 %collective-permute-start.185 = (bf16[256,1024]{1,0:T(8,128)(2,1)S(1)}, bf16[256,1024]{1,0:T(8,128)(2,1)S(1)}, u32[]{:S(2)}, u32[]{:S(2)}) collective-permute-start(bf16[256,1024]{1,0:T(8,128)(2,1)S(1)} %add_convert_fusion.6), channel_id=1, source_target_pairs={{64,65},{65,66},{66,67},{67,64},{68,69},{69,70},{70,71},{71,68},{7... | collective-permute-start | bytes 1572872 | tf_op jit(solution)/shard_map/ppermute | solution.py:57
  651.4 25.1 %collective-permute-start.184 = (bf16[256,1024]{1,0:T(8,128)(2,1)S(1)}, bf16[256,1024]{1,0:T(8,128)(2,1)S(1)}, u32[]{:S(2)}, u32[]{:S(2)}) collective-permute-start(bf16[256,1024]{1,0:T(8,128)(2,1)S(1)} %add_convert_fusion.6), channel_id=1, source_target_pairs={{64,66},{65,67},{66,64},{67,65},{68,70},{69,71},{70,68},{71,69},{7... | collective-permute-start | bytes 1572872 | tf_op jit(solution)/shard_map/ppermute | solution.py:57
  (373 other events, 4686.5 us)

commit v2 on v1

v2 whole, which is shorter than its diff:
```python
import functools
import math

import jax
import jax.numpy as jnp
from jax import lax
from jax.experimental import pallas as pl
from jax.experimental.pallas import tpu as pltpu
from jax.sharding import PartitionSpec as P

HEAD_DIM = 64
EPSILON = 1e-05
MASK_FILL = -1e30
BASE_TWO_SCALE = 0.125 * math.log2(math.e)
SIDE = 4
TILE = 256
LN_TWO = math.log(2.0)
LOW = jnp.bfloat16
FULL = jnp.float32


def move_z(block, distance):
    route = [
        (x * SIDE + z, x * SIDE + (z + distance) % SIDE) for x in range(SIDE) for z in range(SIDE)
    ]
    return lax.ppermute(block, "tensor", route)


def move_x(block, distance):
    route = [
        (x * SIDE + z, (x + distance) % SIDE * SIDE + z) for x in range(SIDE) for z in range(SIDE)
    ]
    return lax.ppermute(block, "tensor", route)


def move_y(block, distance):
    return lax.ppermute(block, "ctx", [(y, (y + distance) % SIDE) for y in range(SIDE)])


def move_y_open(block, distance):
    route = [(y, y + distance) for y in range(SIDE) if 0 <= y + distance < SIDE]
    return lax.ppermute(block, "ctx", route)


def move_x_in(block, distance, section):
    base = section * SIDE * SIDE
    route = [
        (base + x * SIDE + z, base + (x + distance) % SIDE * SIDE + z)
        for x in range(SIDE)
        for z in range(SIDE)
    ]
    return lax.ppermute(block, ("section", "tensor"), route)


def move_y_in(block, distance, section):
    base = section * SIDE
    route = [(base + y, base + (y + distance) % SIDE) for y in range(SIDE)]
    return lax.ppermute(block, ("section", "ctx"), route)


def swap(block):
    return lax.ppermute(block, "section", [(0, 1), (1, 0)])


def send_to(block, section):
    return lax.ppermute(block, "section", [(1 - section, section)])


def gather_z(rows):
    return jnp.concatenate([rows] + [move_z(rows, d) for d in range(1, SIDE)], axis=0)


def scatter_z(rows):
    chunks = rows.reshape(SIDE, rows.shape[0] // SIDE, rows.shape[1])
    total = chunks[0].astype(FULL)
    for d in range(1, SIDE):
        total = total + move_z(chunks[d], -d).astype(FULL)
    return total


def even_sum(block, move):
    low = block.astype(FULL)
    return (low + move(block, 2).astype(FULL)) + (
        move(block, 1).astype(FULL) + move(block, 3).astype(FULL)
    )


def even_pairs(blocks, move):
    return (blocks[0].astype(FULL) + move(blocks[2], -2).astype(FULL)) + (
        move(blocks[1], -1).astype(FULL) + move(blocks[3], -3).astype(FULL)
    )


def layer_norm(values, gain, bias):
    center = values - jnp.mean(values, axis=-1, keepdims=True)
    spread = jnp.mean(center * center, axis=-1, keepdims=True)
    return center * lax.rsqrt(spread + EPSILON) * gain + bias


def local_dot(left, right):
    return jnp.dot(left, right, preferred_element_type=FULL)


def back_dot(left, right):
    return jnp.einsum("rf,df->rd", left, right, preferred_element_type=FULL)


def outer_sum(left, right):
    return jnp.einsum("rd,rf->df", left, right, preferred_element_type=FULL)


def nt_dot(left, right):
    return lax.dot_general(left, right, (((1,), (1,)), ((), ())), preferred_element_type=FULL)


def tn_dot(left, right):
    return lax.dot_general(left, right, (((0,), (0,)), ((), ())), preferred_element_type=FULL)


def attend_kernel(
    scalar_ref, low_ref, high_ref, key_ref, own_ref, kv1_ref, kv2_ref, kv3_ref, out_ref,
    peak, mixed, held, arrived,
):
    block = scalar_ref[0]
    rows_all = own_ref.shape[0]
    tiles = rows_all // TILE
    copies = [
        pltpu.make_async_copy(ref, held.at[d], arrived.at[d])
        for d, ref in enumerate((kv1_ref, kv2_ref, kv3_ref))
    ]
    for copy in copies:
        copy.start()
    peak[...] = jnp.full_like(peak, MASK_FILL)
    mixed[...] = jnp.zeros_like(mixed)
    for d in range(SIDE):
        if d > 0:
            copies[d - 1].wait()
        start = (block - d) * rows_all

        @pl.loop(0, tiles)
        def _(index, d=d, start=start):
            rows = pl.ds(pl.multiple_of(index * TILE, TILE), TILE)
            least, most = scalar_ref[1 + index], scalar_ref[1 + tiles + index]

            def step(masked):
                key_values = own_ref[:, 0:128] if d == 0 else held[d - 1]
                raw = nt_dot(key_values, own_ref[rows, 128:256])
                if masked:
                    places = key_ref[...] - d * rows_all
                    allowed = places >= low_ref[index]
                    if d == 0:
                        allowed = allowed & (places <= high_ref[index])
                    raw = jnp.where(allowed, raw, MASK_FILL)
                old = peak[index]
                top = jnp.maximum(old, jnp.max(raw, axis=0, keepdims=True))
                weight = jnp.exp2(raw - top).astype(LOW)
                lanes = lax.broadcasted_iota(jnp.int32, key_values.shape, 1)
                ones_values = jnp.where(lanes < HEAD_DIM, jnp.ones_like(key_values), key_values)
                peak[index] = top
                mixed[index] = mixed[index] * jnp.exp2(old - top) + tn_dot(ones_values, weight)

            if d == 0:
                step(True)
            else:
                reached = (block >= d) & (least < start + rows_all)
                pl.when(reached & (most <= start))(lambda: step(False))
                pl.when(reached & (most > start))(lambda: step(True))

    @pl.loop(0, tiles)
    def _(index):
        rows = pl.ds(pl.multiple_of(index * TILE, TILE), TILE)
        sums = mixed[index]
        count = sums[0:1, :]
        level = peak[index] + jnp.log2(count)
        lines = lax.broadcasted_iota(jnp.int32, sums.shape, 0)
        out_ref[rows, :] = jnp.where(lines < HEAD_DIM, level, sums / count).T


def attend_back_kernel(
    scalar_ref, low_ref, high_ref, key_ref, own_ref, kv1_ref, kv2_ref, kv3_ref, kept_ref, grad_ref,
    dq_ref, d0_ref, d1_ref, d2_ref, d3_ref,
    query_sum, key_sum, held, arrived,
):
    block = scalar_ref[0]
    rows_all = own_ref.shape[0]
    tiles = rows_all // TILE
    copies = [
        pltpu.make_async_copy(ref, held.at[d], arrived.at[d])
        for d, ref in enumerate((kv1_ref, kv2_ref, kv3_ref))
    ]
    for copy in copies:
        copy.start()
    query_sum[...] = jnp.zeros_like(query_sum)
    for d, out_ref in enumerate((d0_ref, d1_ref, d2_ref, d3_ref)):
        if d > 0:
            copies[d - 1].wait()

        @pl.when(block >= d)
        def _(d=d, out_ref=out_ref):
            start = (block - d) * rows_all
            key_sum[...] = jnp.zeros_like(key_sum)

            @pl.loop(0, tiles)
            def _(index):
                rows = pl.ds(pl.multiple_of(index * TILE, TILE), TILE)
                least, most = scalar_ref[1 + index], scalar_ref[1 + tiles + index]

                def step(masked):
                    queries = own_ref[rows, 128:256]
                    grad = grad_ref[rows, :]
                    kept = kept_ref[rows, :]
                    level = kept.T[0:1, :]
                    meet = jnp.sum((kept * grad.astype(FULL)).T, axis=0, keepdims=True)
                    key_values = own_ref[:, 0:128] if d == 0 else held[d - 1]
                    probs = jnp.exp2(nt_dot(key_values, queries) - level)
                    if masked:
                        places = key_ref[...] - d * rows_all
                        allowed = places >= low_ref[index]
                        if d == 0:
                            allowed = allowed & (places <= high_ref[index])
                        probs = jnp.where(allowed, probs, 0.0)
                    grad_scores = (probs * (nt_dot(key_values, grad) - meet)).astype(LOW)
                    key_sum[...] += local_dot(grad_scores, queries) * LN_TWO + local_dot(
                        probs.astype(LOW), grad
                    )
                    query_sum[rows, :] += tn_dot(grad_scores, key_values)

                if d == 0:
                    step(True)
                else:
                    pl.when(most <= start)(lambda: step(False))
                    pl.when((most > start) & (least < start + rows_all))(lambda: step(True))

            out_ref[...] = key_sum[...].astype(LOW)

        if d > 0:

            @pl.when(block < d)
            def _(out_ref=out_ref):
                out_ref[...] = jnp.zeros_like(out_ref)

    lanes = lax.broadcasted_iota(jnp.int32, dq_ref.shape, 1)
    dq_ref[...] = jnp.where(lanes < HEAD_DIM, query_sum[...] * 0.125, 0.0).astype(LOW)


VMEM_SPEC = pl.BlockSpec(memory_space=pltpu.VMEM)
SMEM_SPEC = pl.BlockSpec(memory_space=pltpu.SMEM)
ANY_SPEC = pl.BlockSpec(memory_space=pl.ANY)


def attend(spots, own, others):
    rows = own.shape[0]
    return pl.pallas_call(
        attend_kernel,
        out_shape=jax.ShapeDtypeStruct((rows, 128), FULL),
        in_specs=[SMEM_SPEC] + [VMEM_SPEC] * 4 + [ANY_SPEC] * 3,
        out_specs=VMEM_SPEC,
        scratch_shapes=[
            pltpu.VMEM((rows // TILE, 1, TILE), FULL),
            pltpu.VMEM((rows // TILE, 128, TILE), FULL),
            pltpu.VMEM((3, rows, 128), LOW),
            pltpu.SemaphoreType.DMA((3,)),
        ],
        compiler_params=pltpu.CompilerParams(vmem_limit_bytes=40 << 20),
        cost_estimate=pl.CostEstimate(
            flops=4 * rows * 2 * rows * 128, bytes_accessed=4 << 20, transcendentals=rows * 2 * rows
        ),
        name="attend",
    )(spots["scalars"], spots["low"], spots["high"], spots["keys"], own, *others)


def attend_back(spots, own, others, kept, grad):
    rows = own.shape[0]
    return pl.pallas_call(
        attend_back_kernel,
        out_shape=[jax.ShapeDtypeStruct((rows, 128), LOW)] * 5,
        in_specs=[SMEM_SPEC] + [VMEM_SPEC] * 4 + [ANY_SPEC] * 3 + [VMEM_SPEC] * 2,
        out_specs=[VMEM_SPEC] * 5,
        scratch_shapes=[
            pltpu.VMEM((rows, 128), FULL),
            pltpu.VMEM((rows, 128), FULL),
            pltpu.VMEM((3, rows, 128), LOW),
            pltpu.SemaphoreType.DMA((3,)),
        ],
        compiler_params=pltpu.CompilerParams(vmem_limit_bytes=40 << 20),
        cost_estimate=pl.CostEstimate(
            flops=10 * rows * 2 * rows * 128, bytes_accessed=6 << 20, transcendentals=rows * 2 * rows
        ),
        name="attend_back",
    )(spots["scalars"], spots["low"], spots["high"], spots["keys"], own, *others, kept, grad)


def tie(first, *rest):
    return lax.optimization_barrier((first, *rest))


X_GROUPS = [[x * SIDE + z for x in range(SIDE)] for z in range(SIDE)]


def forward_attention(residual, normed_all, spots, vectors, bias_qkv, w_heads, w_back):
    b_out = vectors[2]
    projected = ((nt_dot(normed_all, w_heads) + bias_qkv) * spots["scale"]).astype(LOW)
    width = projected.shape[1] // SIDE
    pieces = [projected[:, d * width : (d + 1) * width] for d in range(SIDE)]
    own = jnp.concatenate([pieces[0]] + [move_x(pieces[d], -d) for d in range(1, SIDE)], axis=0)
    others = [move_y_open(own[:, 0:128], d) for d in range(1, SIDE)]
    kept = attend(spots, own, others)
    lanes = lax.broadcasted_iota(jnp.int32, kept.shape, 1)
    mixed = jnp.where(lanes < HEAD_DIM, 0.0, kept).astype(LOW)
    rows = mixed.shape[0] // SIDE
    mixed_rows = jnp.concatenate(
        [mixed[0:rows]] + [move_x(mixed[d * rows : (d + 1) * rows], d) for d in range(1, SIDE)], axis=1
    )
    hidden = residual + (scatter_z(local_dot(mixed_rows, w_back).astype(LOW)) + b_out)
    return hidden, (residual, normed_all, own, others, kept, mixed_rows)


def forward_hidden_units(hidden, vectors, b_up, w_up, w_down):
    gain_two, bias_two, b_down = vectors[3:6]
    normed_two_all = gather_z(layer_norm(hidden, gain_two, bias_two).astype(LOW))
    up_value = nt_dot(normed_two_all, w_up) + b_up
    activated = jax.nn.gelu(up_value).astype(LOW)
    result = hidden + (scatter_z(local_dot(activated, w_down).astype(LOW)) + b_down)
    return result, (hidden, normed_two_all, up_value, activated)


def backward_hidden_units(grad_out, grad_down_all, stored, vectors, w_up, w_down):
    hidden, normed_two_all, up_value, activated = stored
    gain_two, bias_two = vectors[3:5]
    grad_down = grad_out.astype(LOW)
    g_b_down = jnp.sum(grad_down.astype(FULL), axis=0, keepdims=True)
    _, gelu_pull = jax.vjp(jax.nn.gelu, up_value)
    (grad_up,) = gelu_pull(nt_dot(grad_down_all, w_down))
    grad_up = grad_up.astype(LOW)
    grad_normed_two = scatter_z(local_dot(grad_up, w_up).astype(LOW))
    g_w_down = tn_dot(activated, grad_down_all).astype(LOW)
    g_b_up = jnp.sum(grad_up.astype(FULL), axis=0)
    g_w_up = tn_dot(grad_up, normed_two_all).astype(LOW)
    _, norm_two_pull = jax.vjp(layer_norm, hidden, gain_two, bias_two)
    grad_hidden_part, g_gain_two, g_bias_two = norm_two_pull(grad_normed_two)
    grad_hidden = grad_out + grad_hidden_part
    return grad_hidden, (g_gain_two, g_bias_two, g_b_down), g_b_up, g_w_up, g_w_down


def backward_mixed(grad_hidden, stored, w_back, spots):
    mixed_rows = stored[5]
    grad_attn = grad_hidden.astype(LOW)
    g_b_out = jnp.sum(grad_attn.astype(FULL), axis=0, keepdims=True)
    grad_attn_all = gather_z(grad_attn)
    grad_mixed = (nt_dot(grad_attn_all, w_back) * spots["upper"]).astype(LOW)
    pieces = [grad_mixed[:, d * 128 : (d + 1) * 128] for d in range(SIDE)]
    grad_own = jnp.concatenate(
        [pieces[0]] + [move_x(pieces[d], -d) for d in range(1, SIDE)], axis=0
    )
    g_w_out = tn_dot(mixed_rows, grad_attn_all)
    return grad_own, g_b_out, g_w_out


def backward_heads(grad_mixed_own, stored, spots):
    _, _, own, others, kept, _ = stored
    dq, dkv0, dkv1, dkv2, dkv3 = attend_back(spots, own, others, kept, grad_mixed_own)
    dkv = dkv0.astype(FULL)
    for d, part in enumerate((dkv1, dkv2, dkv3), 1):
        dkv = dkv + move_y_open(part, -d).astype(FULL)
    grad_own = jnp.concatenate([dkv.astype(LOW), dq], axis=1)
    rows = grad_own.shape[0] // SIDE
    return jnp.concatenate(
        [grad_own[0:rows]] + [move_x(grad_own[d * rows : (d + 1) * rows], d) for d in range(1, SIDE)],
        axis=1,
    )


def backward_entry(grad_qkv, grad_hidden, stored, vectors, w_heads):
    residual, normed_all = stored[0:2]
    gain_one, bias_one = vectors[0:2]
    grad_normed = scatter_z(local_dot(grad_qkv, w_heads).astype(LOW))
    g_w_heads = tn_dot(grad_qkv, normed_all)
    g_b_qkv = jnp.sum(grad_qkv.astype(FULL), axis=0)
    _, norm_one_pull = jax.vjp(layer_norm, residual, gain_one, bias_one)
    grad_residual_part, g_gain_one, g_bias_one = norm_one_pull(grad_normed)
    return grad_hidden + grad_residual_part, (g_gain_one, g_bias_one), g_b_qkv, g_w_heads


def per_device(
    inputs,
    segments,
    gain_one,
    bias_one,
    w_qkv,
    b_qv,
    w_out,
    b_out,
    gain_two,
    bias_two,
    w_up,
    b_up,
    w_down,
    b_down,
    cotangent,
):
    here = lax.axis_index("section")
    block = lax.axis_index("ctx")
    spot = lax.axis_index("tensor")
    x_here, z_here = spot // SIDE, spot % SIDE
    row_count, model_width = inputs.shape[2], inputs.shape[3]
    block_rows = row_count * SIDE * SIDE

    def owner(layer, yes, no):
        return jnp.where(here == layer, yes, no)

    sequence = lax.dynamic_index_in_dim(inputs, here, 0, False)[0].astype(FULL)
    grad_last = lax.dynamic_index_in_dim(cotangent, here, 0, False)[0].astype(FULL)
    grad_last_all = lax.dynamic_index_in_dim(cotangent, here, 0, False)[0]

    heads_kv = jnp.concatenate([w_qkv[0, :, 1].T, w_qkv[0, :, 2].T], axis=0)
    heads_qo = jnp.concatenate([w_qkv[0, :, 0].T, w_out[0]], axis=0)
    heads_qo_other = swap(heads_qo)
    gap = jnp.zeros((HEAD_DIM,), LOW)
    small = jnp.concatenate(
        [gain_one, bias_one, b_out, gain_two, bias_two, b_down]
        + [
            jnp.concatenate(
                [b_up[0], gap, b_qv[0, 1], b_qv[0, 0], gap, jnp.zeros((model_width - 512,), LOW)]
            )[None],
            jnp.zeros((1, model_width), LOW),
        ],
        axis=0,
    )
    small_other = swap(small)
    up_own, down_other = w_up[0].T, swap(w_down[0])

    def gather_heads(layer, after=None):
        half = owner(layer, heads_kv, heads_qo_other)
        if after is not None:
            half, _ = tie(half, after)
        mine = jnp.stack([half] + [move_x(half, d) for d in range(1, SIDE)])
        return mine, swap(mine)

    def join_heads(layer, mine, theirs):
        key_value, query_out = owner(layer, mine, theirs), owner(layer, theirs, mine)
        whole = jnp.concatenate([key_value, query_out], axis=1).reshape(SIDE * TILE, model_width)
        return whole, query_out.reshape(SIDE * 128, model_width)

    def gather_units(layer, after=None):
        half = owner(layer, up_own, down_other)
        if after is not None:
            half, _ = tie(half, after)
        return lax.all_gather(half, "tensor", axis=0, tiled=True, axis_index_groups=X_GROUPS)

    def join_units(layer, mine):
        theirs = swap(mine)
        return owner(layer, mine, theirs), owner(layer, theirs, mine)

    smalls = (owner(0, small, small_other), owner(0, small_other, small))
    vectors = [
        tuple(smalls[layer][row : row + 1].astype(FULL) for row in range(6)) for layer in range(2)
    ]
    normed = layer_norm(sequence, *vectors[0][0:2]).astype(LOW)
    heads_first = join_heads(0, *gather_heads(0, normed))
    units_first = gather_units(0)
    normed_all = gather_z(normed)
    normed_all, segments = tie(normed_all, segments)
    segment_ids = lax.dynamic_index_in_dim(segments, here, 0, False)
    start_one = jnp.sum((segment_ids < 1).astype(jnp.int32))
    start_two = jnp.sum((segment_ids < 2).astype(jnp.int32))

    def first_of(place):
        return jnp.where(place >= start_two, start_two, jnp.where(place >= start_one, start_one, 0))

    order = jnp.arange(block_rows)
    from_x = (x_here + order // TILE) % SIDE
    from_z = (z_here - order // row_count % SIDE) % SIDE
    place = block * block_rows + (from_x * SIDE + from_z) * row_count + order % row_count
    tile_first = block * block_rows + (x_here + jnp.arange(SIDE)) % SIDE * TILE
    lane = jnp.arange(SIDE * TILE) % TILE
    spots = {
        "scalars": jnp.concatenate(
            [block[None], first_of(tile_first), first_of(tile_first + TILE - 1)]
        ).astype(jnp.int32),
        "high": place.astype(jnp.int32).reshape(SIDE, 1, TILE),
        "low": first_of(place).astype(jnp.int32).reshape(SIDE, 1, TILE),
        "keys": place.astype(jnp.int32).reshape(block_rows, 1),
        "scale": jnp.where(lane < 128, 1.0, jnp.where(lane < 192, BASE_TWO_SCALE, 0.0)).astype(FULL),
        "upper": (jnp.arange(SIDE * 128) % 128 >= HEAD_DIM).astype(FULL),
    }

    split_own = jnp.concatenate([smalls[0][6:7, :512], smalls[1][6:7, :512]], axis=0)
    split_all = [split_own] + [move_x(split_own, d) for d in range(1, SIDE)]
    bias_heads = [
        jnp.concatenate([part[layer : layer + 1, 256:512] for part in split_all], axis=1).astype(FULL)
        for layer in range(2)
    ]
    turn = ((x_here - jnp.arange(SIDE)) % SIDE)[None, :] == jnp.arange(SIDE)[:, None]
    bias_up = [
        jnp.sum(
            jnp.where(
                turn[:, :, None], jnp.stack([part[layer, 0:256] for part in split_all]).astype(FULL)[None], 0.0
            ),
            axis=1,
        ).reshape(1, -1)
        for layer in range(2)
    ]

    hidden, kept_heads_first = forward_attention(sequence, normed_all, spots, vectors[0], bias_heads[0], *heads_first)
    heads_last = gather_heads(1, kept_heads_first[4])
    units_first = join_units(0, units_first)
    units_last = gather_units(1, kept_heads_first[4])
    hidden, grad_last_all = tie(hidden, gather_z(grad_last_all))
    middle, kept_units_first = forward_hidden_units(hidden, vectors[0], bias_up[0], *units_first)
    middle, *heads_last = tie(middle, *heads_last)
    heads_last = join_heads(1, *heads_last)
    middle = middle.astype(LOW).astype(FULL)
    normed_all = gather_z(layer_norm(middle, *vectors[1][0:2]).astype(LOW))
    hidden, kept_heads_last = forward_attention(
        middle, normed_all, spots, vectors[1], bias_heads[1], *heads_last
    )
    units_last = join_units(1, units_last)
    result, kept_units_last = forward_hidden_units(hidden, vectors[1], bias_up[1], *units_last)

    def swap_grads(layer, first, second):
        return owner(layer, first, second), swap(owner(layer, second, first))

    def add_grads(kept, arrived):
        return (kept.astype(FULL) + arrived.astype(FULL)).astype(LOW)

    def scatter_units(grads):
        return lax.psum_scatter(
            grads, "tensor", scatter_dimension=0, tiled=True, axis_index_groups=X_GROUPS
        )

    def split_heads(g_w_heads, g_w_out):
        heads = g_w_heads.reshape(SIDE, TILE, model_width)
        key_value = heads[:, 0:128].astype(LOW)
        return key_value, (heads[:, 128:256] + g_w_out.reshape(SIDE, 128, model_width)).astype(LOW)

    def scatter_heads(grads):
        total = grads[0].astype(FULL)
        for d in range(1, SIDE):
            total = total + move_x(grads[d], -d).astype(FULL)
        return total.astype(LOW)

    def pack_vectors(heads, units, g_b_out, g_b_up, g_b_qkv):
        by_turn = jnp.sum(
            jnp.where(turn[:, :, None], g_b_up.reshape(SIDE, 1, TILE), 0.0), axis=0
        )
        return jnp.concatenate(
            [
                *heads, g_b_out, *units,
                jnp.concatenate([by_turn, g_b_qkv.reshape(SIDE, TILE)], axis=1).reshape(2, -1),
            ],
            axis=0,
        )

    grad_hidden, vec_units_last, g_b_up_last, g_up, g_down = backward_hidden_units(
        grad_last, grad_last_all, kept_units_last, vectors[1], *units_last
    )
    units_kept, units_arrived = swap_grads(1, g_up, g_down)
    grad_mixed, g_b_out_last, g_out = backward_mixed(grad_hidden, kept_heads_last, heads_last[1], spots)
    grad_mixed, units_kept, units_arrived = tie(grad_mixed, units_kept, units_arrived)
    units_sum_last = scatter_units(add_grads(units_kept, units_arrived))
    grad_qkv = backward_heads(grad_mixed, kept_heads_last, spots)
    grad_middle, vec_heads_last, g_b_qkv_last, g_heads = backward_entry(
        grad_qkv, grad_hidden, kept_heads_last, vectors[1], heads_last[0]
    )
    heads_kept, heads_arrived = swap_grads(1, *split_heads(g_heads, g_out))

    grad_middle = grad_middle.astype(LOW).astype(FULL)
    grad_middle, units_sum_last = tie(grad_middle, units_sum_last)
    units_sum_last = lax.psum(units_sum_last, "ctx")
    grad_hidden, vec_units_first, g_b_up_first, g_up, g_down = backward_hidden_units(
        grad_middle, gather_z(grad_middle.astype(LOW)), kept_units_first, vectors[0], *units_first
    )
    units_kept, units_arrived = swap_grads(0, g_up, g_down)
    grad_hidden, heads_kept, heads_arrived = tie(grad_hidden, heads_kept, heads_arrived)
    heads_sum_last = scatter_heads(add_grads(heads_kept, heads_arrived))
    grad_mixed, g_b_out_first, g_out = backward_mixed(grad_hidden, kept_heads_first, heads_first[1], spots)
    grad_mixed, units_kept, units_arrived, heads_sum_last, units_sum_last = tie(
        grad_mixed, units_kept, units_arrived, heads_sum_last, units_sum_last
    )
    units_sum_first = scatter_units(add_grads(units_kept, units_arrived))
    grad_qkv = backward_heads(grad_mixed, kept_heads_first, spots)
    grad_qkv, units_sum_first = tie(grad_qkv, units_sum_first)
    units_sum_first, heads_sum_last = lax.psum((units_sum_first, heads_sum_last), "ctx")
    gain_one, bias_one = vectors[0][0:2]
    residual, normed_all = kept_heads_first[0:2]
    grad_normed = local_dot(grad_qkv, heads_first[0])
    g_bias_one = jnp.sum(grad_normed, axis=0, keepdims=True)
    g_gain_one = jnp.sum(grad_normed * ((normed_all.astype(FULL) - bias_one) / gain_one), axis=0, keepdims=True)
    g_b_qkv_first = jnp.sum(grad_qkv.astype(FULL), axis=0)
    sums_first = pack_vectors(
        (g_gain_one, g_bias_one), vec_units_first, g_b_out_first, g_b_up_first, g_b_qkv_first
    )
    sums_last = pack_vectors(vec_heads_last, vec_units_last, g_b_out_last, g_b_up_last, g_b_qkv_last)
    sums = owner(0, sums_first, sums_last) + swap(owner(0, sums_last, sums_first))
    common = jnp.pad(sums[:6], ((0, 10), (0, 0))).astype(LOW)
    chunks = grad_normed.astype(LOW).reshape(SIDE, row_count, model_width)
    chunks = [jnp.concatenate([chunks[d], common], axis=0) for d in range(SIDE)]
    chunks = even_pairs(chunks, move_z)
    heads_kept, heads_arrived = swap_grads(0, *split_heads(tn_dot(grad_qkv, normed_all), g_out))
    halves = add_grads(heads_kept, heads_arrived)
    common = chunks[row_count : row_count + 6].astype(LOW)
    split = sums[6:].reshape(SIDE, 1, 512).astype(LOW)
    packs = [
        jnp.concatenate(
            [
                halves[d],
                common,
                jnp.pad(split[d], ((0, 0), (0, model_width - 512))),
                jnp.zeros((9, model_width), LOW),
            ],
            axis=0,
        )
        for d in range(SIDE)
    ]
    pack = even_sum(even_pairs(packs, move_x).astype(LOW), move_y)
    heads_sum_first, pack = pack[:128], pack[128:]
    _, norm_one_pull = jax.vjp(lambda rows: layer_norm(rows, gain_one, bias_one), residual)
    grad_first = grad_hidden + norm_one_pull(chunks[:row_count])[0]

    passed = swap(owner(0, result, grad_first))
    kept = owner(0, grad_first, result)
    boundary = owner(0, jnp.stack([kept, passed]), jnp.stack([passed, kept]))
    boundary = boundary.reshape(1, 2, 1, row_count, model_width)

    units_sum = owner(0, units_sum_first, units_sum_last)
    heads_sum = owner(0, heads_sum_first, heads_sum_last)
    units_theirs = swap(owner(0, units_sum_last, units_sum_first))
    heads_theirs = swap(owner(0, heads_sum_last, heads_sum_first).astype(LOW))
    g_key_value = heads_sum.astype(FULL)
    g_query_out = heads_theirs.astype(FULL)
    g_w_qkv = jnp.stack([g_query_out[0:64].T, g_key_value[0:64].T, g_key_value[64:128].T], axis=1)
    g_b_qv = jnp.stack([pack[6, 384:448], pack[6, 320:384]])
    return (
        boundary,
        pack[0:1],
        pack[1:2],
        g_w_qkv[None],
        g_b_qv[None],
        g_query_out[64:128][None],
        pack[2:3],
        pack[3:4],
        pack[4:5],
        units_sum.astype(FULL).T[None],
        pack[6:7, 0:256],
        units_theirs.astype(FULL)[None],
        pack[5:6],
    )


def solution(mesh):
    return jax.shard_map(
        per_device,
        mesh=mesh,
        in_specs=(
            P(None, "ctx", "tensor", None),
            P(),
            P("section", None),
            P("section", None),
            P("section", None, None, "tensor"),
            P("section", None, "tensor"),
            P("section", "tensor", None),
            P("section", None),
            P("section", None),
            P("section", None),
            P("section", None, "tensor"),
            P("section", "tensor"),
            P("section", "tensor", None),
            P("section", None),
            P(None, "ctx", "tensor", None),
        ),
        out_specs=(
            P("section", None, "ctx", "tensor", None),
            P("section", None),
            P("section", None),
            P("section", None, None, "tensor"),
            P("section", None, "tensor"),
            P("section", "tensor", None),
            P("section", None),
            P("section", None),
            P("section", None),
            P("section", None, "tensor"),
            P("section", "tensor"),
            P("section", "tensor", None),
            P("section", None),
        ),
        check_vma=False,
    )
```

time: 753 us -> 522 us (0.69)
  starting transfers between devices: 413 us -> 142 us
  waiting for transfers between devices: 176 us -> 202 us
  other arithmetic: 55.1 us -> 67.8 us
  between operations: 5.36 us -> 17.2 us
  local copies, waits for them, and re-layouts: 38.3 us -> 29.9 us
    ppermute x88 -> x0, starting transfers between devices: 197 us -> none  [the longest x48 98.8 us: move_x_in(): return lax.ppermute(block, ('section', 'tensor'), route)]
    ppermute x51 -> x48, starting transfers between devices: 101 us -> 53.5 us  [move_z(): return lax.ppermute(block, 'tensor', route)]
    ppermute x88 -> x0, waiting for transfers between devices: 40.1 us -> none  [the longest x48 29.3 us: move_x_in(): return lax.ppermute(block, ('section', 'tensor'), route)]
    ppermute x30 -> x39, waiting for transfers between devices: 32.8 us -> 66.9 us  [move_x(): return lax.ppermute(block, 'tensor', route)]
    ppermute x3, starting transfers between devices: 26.3 us -> 4.64 us  [move_y(): lax.ppermute(block, 'ctx', [(y, (y + distance) % SIDE) for y in range(SID...]
    ppermute x3 -> x15, starting transfers between devices: 21.2 us -> 2.03 us  [swap(): return lax.ppermute(block, 'section', [(0, 1), (1, 0)])]
    select_n x7 -> x17, other arithmetic: 4.69 us -> 18.9 us  [the longest x13 15.6 us: owner(): return jnp.where(here == layer, yes, no)]
    psum x0 -> x2, waiting for transfers between devices: none -> 11.9 us  [the longest x1 11.9 us: per_device(): lax.psum((units_sum_first, heads_sum_last), 'ctx')]
  transfers between devices with their start and end apart: 187 -> 123, of which waited for: 66 -> 76; matrix products, arithmetic and copies ran while one was open for 16% -> 20% of each run, Pallas kernels for 2% -> 4%
where the time goes in v2:
time: 522 us; the launch traced here: 512 us
  waiting for transfers between devices  202 us (39%)
  starting transfers between devices  142 us (27%)
  other arithmetic  67.8 us (13%)
  matrix products  33.9 us (6%)
  local copies, waits for them, and re-layouts  29.9 us (6%)
  Pallas kernels  19.2 us (4%)
  between operations  17.2 us (3%)
    ppermute x48, waiting for transfers between devices, move_z(): return lax.ppermute(block, 'tensor', route)  67.5 us
    ppermute x39, waiting for transfers between devices, move_x(): return lax.ppermute(block, 'tensor', route)  66.9 us
    ppermute x48, starting transfers between devices, move_z(): return lax.ppermute(block, 'tensor', route)  53.5 us
    ppermute x39, starting transfers between devices, move_x(): return lax.ppermute(block, 'tensor', route)  48.8 us
    ppermute x12, waiting for transfers between devices, move_y_open(): return lax.ppermute(block, 'ctx', route)  44.9 us
    ppermute x12, starting transfers between devices, move_y_open(): return lax.ppermute(block, 'ctx', route)  33.1 us
    select_n x13, other arithmetic, owner(): return jnp.where(here == layer, yes, no)  15.6 us
    dot_general x8, matrix products, tn_dot(): lax.dot_general(left, right, (((0,), (0,)), ((), ())), preferred_element_...  13.4 us
  transfers between devices with their start and end apart: 123, of which 76 were waited for; matrix products, arithmetic and copies ran while one was open for 20% of the time, Pallas kernels for 4%

profile of v2, /device:TPU:0, one launch (start us, length us, event | category | flops | bytes accessed | tf_op | source)
XLA Modules:
  0.0 512.4 jit_solution(15969227533939448412)
XLA Ops:
  11.3 4.1 collective-permute-start.26
  30.6 5.8 %collective-permute-done.7 = bf16[128,1024]{1,0:T(8,128)(2,1)S(1)} collective-permute-done((bf16[128,1024]{1,0:T(8,128)(2,1)S(1)}, bf16[128,1024]{1,0:T(8,128)(2,1)S(1)}, u32[]{:S(2)}, u32[]{:S(2)}) %collective-permute-start.7) | collective-permute-done | bytes 262176 | tf_op jit(solution)/shard_map/ppermute | solution.py:33
  38.9 4.2 collective-permute-done.5
  53.9 4.2 collective-permute-done.2
  72.4 4.9 collective-permute-start.17
  88.7 4.1 attend.2.kept_ref
  123.0 4.9 collective-permute-done.38
  160.4 5.1 %collective-permute-start.44 = (bf16[256,256]{1,0:T(8,128)(2,1)S(1)}, bf16[256,256]{1,0:T(8,128)(2,1)S(1)}, u32[]{:S(2)}, u32[]{:S(2)}) collective-permute-start(bf16[256,256]{1,0:T(8,128)(2,1)S(1)} %get-tuple-element.221), channel_id=1, source_target_pairs={{0,32},{4,36},{8,40},{12,44},{16,48},{20,52},{24,56},{28,60},{32,0... | collective-permute-start | bytes 393224 | tf_op jit(solution)/shard_map/ppermute | solution.py:33
  171.3 9.1 %collective-permute-start.48 = (bf16[1024,128]{1,0:T(8,128)(2,1)}, bf16[1024,128]{1,0:T(8,128)(2,1)S(1)}, u32[]{:S(2)}, u32[]{:S(2)}) collective-permute-start(bf16[1024,128]{1,0:T(8,128)(2,1)} %slice.638), channel_id=1, source_target_pairs={{0,3},{4,7},{8,11},{12,15},{16,19},{20,23},{24,27},{28,31},{32,35}... | collective-permute-start | bytes 786440 | tf_op jit(solution)/shard_map/ppermute | solution.py:42
  180.4 5.2 %collective-permute-start.47 = (bf16[1024,128]{1,0:T(8,128)(2,1)}, bf16[1024,128]{1,0:T(8,128)(2,1)S(1)}, u32[]{:S(2)}, u32[]{:S(2)}) collective-permute-start(bf16[1024,128]{1,0:T(8,128)(2,1)} %slice.638), channel_id=1, source_target_pairs={{0,2},{1,3},{4,6},{5,7},{8,10},{9,11},{12,14},{13,15},{16,18},{17,... | collective-permute-start | bytes 786440 | tf_op jit(solution)/shard_map/ppermute | solution.py:42
  195.2 4.2 attend.3.kept_ref
  268.5 5.3 %attend_back.2 = (bf16[1024,128]{1,0:T(8,128)(2,1)S(1)}, bf16[1024,128]{1,0:T(8,128)(2,1)S(1)}, bf16[1024,128]{1,0:T(8,128)(2,1)S(1)}, bf16[1024,128]{1,0:T(8,128)(2,1)S(1)}, bf16[1024,128]{1,0:T(8,128)(2,1)S(1)}) custom-call(s32[9]{0:T(128)S(1)} %pad_add_fusion.scalar_ref, s32[4,1,256]{2,1,0:T(1,128)S(1)} %get-tuple-element.299.low_ref, ...), custom_call_target="tpu_custom_call" | custom-call | flops 2684354560 | bytes 6291456 | tf_op jit(solution)/shard_map/attend_back/pallas_call | solution.py:274
  277.9 10.6 %collective-permute-done.68 = bf16[1024,128]{1,0:T(8,128)(2,1)S(1)} collective-permute-done((bf16[1024,128]{1,0:T(8,128)(2,1)S(1)}, bf16[1024,128]{1,0:T(8,128)(2,1)S(1)}, u32[]{:S(2)}, u32[]{:S(2)}) %collective-permute-start.68) | collective-permute-done | bytes 262176 | tf_op jit(solution)/shard_map/ppermute | solution.py:42
  288.6 9.1 %collective-permute-done.69 = bf16[1024,128]{1,0:T(8,128)(2,1)S(1)} collective-permute-done((bf16[1024,128]{1,0:T(8,128)(2,1)S(1)}, bf16[1024,128]{1,0:T(8,128)(2,1)S(1)}, u32[]{:S(2)}, u32[]{:S(2)}) %collective-permute-start.69) | collective-permute-done | bytes 262176 | tf_op jit(solution)/shard_map/ppermute | solution.py:42
  367.1 11.1 %collective-permute-done.88 = bf16[256,128]{1,0:T(8,128)(2,1)S(1)} collective-permute-done((bf16[256,128]{1,0:T(8,128)(2,1)S(1)}, bf16[256,128]{1,0:T(8,128)(2,1)S(1)}, u32[]{:S(2)}, u32[]{:S(2)}) %collective-permute-start.88) | collective-permute-done | bytes 65568 | tf_op jit(solution)/shard_map/ppermute | solution.py:33
  378.2 4.3 collective-permute-done.87
  383.4 4.6 add_convert_fusion
  394.7 5.6 %attend_back.3 = (bf16[1024,128]{1,0:T(8,128)(2,1)S(1)}, bf16[1024,128]{1,0:T(8,128)(2,1)S(1)}, bf16[1024,128]{1,0:T(8,128)(2,1)}, bf16[1024,128]{1,0:T(8,128)(2,1)}, bf16[1024,128]{1,0:T(8,128)(2,1)S(1)}) custom-call(s32[9]{0:T(128)S(1)} %pad_add_fusion.scalar_ref, s32[4,1,256]{2,1,0:T(1,128)S(1)} %get-tuple-element.299.low_ref, ...), custom_call_target="tpu_custom_call" | custom-call | flops 2684354560 | bytes 6291456 | tf_op jit(solution)/shard_map/attend_back/pallas_call | solution.py:274
  405.4 5.2 %collective-permute-done.94 = bf16[1024,128]{1,0:T(8,128)(2,1)S(1)} collective-permute-done((bf16[1024,128]{1,0:T(8,128)(2,1)}, bf16[1024,128]{1,0:T(8,128)(2,1)S(1)}, u32[]{:S(2)}, u32[]{:S(2)}) %collective-permute-start.94) | collective-permute-done | bytes 262176 | tf_op jit(solution)/shard_map/ppermute | solution.py:42
  410.6 4.1 collective-permute-done.95
  414.7 4.2 collective-permute-done.96
  446.1 5.0 collective-permute-done.101
  465.8 11.9 %all-reduce.11.cloned.1.call-done = (bf16[128,1024]{1,0:T(8,128)(2,1)}, bf16[256,1024]{1,0:T(8,128)(2,1)}) async-done(((bf16[128,1024]{1,0:T(8,128)(2,1)}, bf16[256,1024]{1,0:T(8,128)(2,1)}), (bf16[128,1024]{1,0:T(8,128)(2,1)}, bf16[256,1024]{1,0:T(8,128)(2,1)})) %all-reduce.11.cloned.1.call-update) | async-done | bytes 786448 | tf_op jit(solution)/shard_map/psum | solution.py:583
  489.5 6.9 %collective-permute-done.114 = bf16[144,1024]{1,0:T(8,128)(2,1)S(1)} collective-permute-done((bf16[144,1024]{1,0:T(8,128)(2,1)S(1)}, bf16[144,1024]{1,0:T(8,128)(2,1)S(1)}, u32[]{:S(2)}, u32[]{:S(2)}) %collective-permute-start.114) | collective-permute-done | bytes 294944 | tf_op jit(solution)/shard_map/ppermute | solution.py:37
  (765 shorter events, 351.4 us)
Async XLA Ops:
  7.2 86.4 %all-gather.5.cloned.1.call-start = ((), (), s32[]{:S(2)}) async-start(), calls=%async_computation.3 | async-start | bytes 2621440 | tf_op jit(solution)/shard_map/all_gather | solution.py:448
  11.3 98.0 %collective-permute-start.26 = (bf16[64,1024]{1,0:T(8,128)(2,1)S(1)}, bf16[64,1024]{1,0:T(8,128)(2,1)}, u32[]{:S(2)}, u32[]{:S(2)}) collective-permute-start(bf16[64,1024]{1,0:T(8,128)(2,1)S(1)} %get-tuple-element.146), channel_id=1, source_target_pairs={{0,12},{4,0},{8,4},{12,8},{16,28},{20,16},{24,20},{28,24},{32,44},... | collective-permute-start | bytes 393224 | tf_op jit(solution)/shard_map/ppermute | solution.py:26
  23.5 23.1 %collective-permute-start.11 = (bf16[2,512]{1,0:T(2,128)(2,1)}, bf16[2,512]{1,0:T(2,128)(2,1)}, u32[]{:S(2)}, u32[]{:S(2)}) collective-permute-start(bf16[2,512]{1,0:T(2,128)(2,1)} %pad_maximum_fusion.46), channel_id=1, source_target_pairs={{0,48},{4,52},{8,56},{12,60},{16,0},{20,4},{24,8},{28,12},{32,16},... | collective-permute-start | bytes 6152 | tf_op jit(solution)/shard_map/ppermute | solution.py:33
  30.6 156.4 %all-gather.3.cloned.1.call-start = ((), (), s32[]{:S(2)}) async-start(), calls=%async_computation.2 | async-start | bytes 2621440 | tf_op jit(solution)/shard_map/all_gather | solution.py:448
  43.2 16.4 %collective-permute-start.8 = (bf16[4,128,1024]{2,1,0:T(8,128)(2,1)S(1)}, bf16[4,128,1024]{2,1,0:T(8,128)(2,1)S(1)}, u32[]{:S(2)}, u32[]{:S(2)}) collective-permute-start(bf16[4,128,1024]{2,1,0:T(8,128)(2,1)S(1)} %pad_maximum_fusion.2), channel_id=1, source_target_pairs={{0,64},{64,0},{1,65},{65,1},{2,66},{66,2},{3,67},{67,3},{4,68},{68... | collective-permute-start | bytes 3145736 | tf_op jit(solution)/shard_map/ppermute | solution.py:62
  93.6 43.0 %collective-permute-start.32 = (bf16[1024,1024]{1,0:T(8,128)(2,1)}, bf16[1024,1024]{1,0:T(8,128)(2,1)}, u32[]{:S(2)}, u32[]{:S(2)}) collective-permute-start(bf16[1024,1024]{1,0:T(8,128)(2,1)} %all-gather.5.cloned.1.call-done), channel_id=1, source_target_pairs={{0,64},{64,0},{1,65},{65,1},{2,66},{66,2},{3,67},{67,3},{4,68},{68... | collective-permute-start | bytes 6291464 | tf_op jit(solution)/shard_map/ppermute | solution.py:62
  114.6 206.9 %reduce-scatter.3.cloned.1.call-start = ((), (), s32[]{:S(2)}) async-start(), calls=%async_computation.4 | async-start | bytes 2621440 | tf_op jit(solution)/shard_map/reduce_scatter | solution.py:527
  132.7 16.6 %collective-permute-start.39 = (bf16[4,128,1024]{2,1,0:T(8,128)(2,1)S(1)}, bf16[4,128,1024]{2,1,0:T(8,128)(2,1)S(1)}, u32[]{:S(2)}, u32[]{:S(2)}) collective-permute-start(bf16[4,128,1024]{2,1,0:T(8,128)(2,1)S(1)} %pad_maximum_fusion.3), channel_id=1, source_target_pairs={{0,64},{64,0},{1,65},{65,1},{2,66},{66,2},{3,67},{67,3},{4,68},{68... | collective-permute-start | bytes 3145736 | tf_op jit(solution)/shard_map/ppermute | solution.py:62
  186.9 42.6 %collective-permute-start.28 = (bf16[1024,1024]{1,0:T(8,128)(2,1)}, bf16[1024,1024]{1,0:T(8,128)(2,1)S(1)}, u32[]{:S(2)}, u32[]{:S(2)}) collective-permute-start(bf16[1024,1024]{1,0:T(8,128)(2,1)} %all-gather.3.cloned.1.call-done), channel_id=1, source_target_pairs={{0,64},{64,0},{1,65},{65,1},{2,66},{66,2},{3,67},{67,3},{4,68},{68... | collective-permute-start | bytes 6291464 | tf_op jit(solution)/shard_map/ppermute | solution.py:62
  239.3 24.0 %collective-permute-start.67 = (bf16[1024,1024]{1,0:T(8,128)(2,1)S(1)}, bf16[1024,1024]{1,0:T(8,128)(2,1)S(1)}, u32[]{:S(2)}, u32[]{:S(2)}) collective-permute-start(bf16[1024,1024]{1,0:T(8,128)(2,1)S(1)} %get-tuple-element.162), channel_id=1, source_target_pairs={{0,64},{64,0},{1,65},{65,1},{2,66},{66,2},{3,67},{67,3},{4,68},{68... | collective-permute-start | bytes 6291464 | tf_op jit(solution)/shard_map/ppermute | solution.py:62
  265.6 117.8 %all-reduce.9.cloned.1.call-start = ((), (), s32[]{:S(2)}) async-start(), calls=%async_computation.5 | async-start | bytes 1048576 | tf_op jit(solution)/shard_map/psum | solution.py:569
  275.3 22.4 %collective-permute-start.69 = (bf16[1024,128]{1,0:T(8,128)(2,1)S(1)}, bf16[1024,128]{1,0:T(8,128)(2,1)S(1)}, u32[]{:S(2)}, u32[]{:S(2)}) collective-permute-start(bf16[1024,128]{1,0:T(8,128)(2,1)S(1)} %get-tuple-element.61), channel_id=1, source_target_pairs={{2,0},{3,1},{6,4},{7,5},{10,8},{11,9},{14,12},{15,13},{18,16},{19,... | collective-permute-start | bytes 786440 | tf_op jit(solution)/shard_map/ppermute | solution.py:42
  276.6 23.8 %collective-permute-start.70 = (bf16[1024,128]{1,0:T(8,128)(2,1)S(1)}, bf16[1024,128]{1,0:T(8,128)(2,1)S(1)}, u32[]{:S(2)}, u32[]{:S(2)}) collective-permute-start(bf16[1024,128]{1,0:T(8,128)(2,1)S(1)} %get-tuple-element.62), channel_id=1, source_target_pairs={{3,0},{7,4},{11,8},{15,12},{19,16},{23,20},{27,24},{31,28},{35,32}... | collective-permute-start | bytes 786440 | tf_op jit(solution)/shard_map/ppermute | solution.py:42
  328.4 20.0 %collective-permute-start.83 = (bf16[4,128,1024]{2,1,0:T(8,128)(2,1)}, bf16[4,128,1024]{2,1,0:T(8,128)(2,1)}, u32[]{:S(2)}, u32[]{:S(2)}) collective-permute-start(bf16[4,128,1024]{2,1,0:T(8,128)(2,1)} %get-tuple-element.149), channel_id=1, source_target_pairs={{0,64},{64,0},{1,65},{65,1},{2,66},{66,2},{3,67},{67,3},{4,68},{68... | collective-permute-start | bytes 3145736 | tf_op jit(solution)/shard_map/ppermute | solution.py:62
  328.5 100.7 %reduce-scatter.5.cloned.1.call-start = ((), (), s32[]{:S(2)}) async-start(), calls=%async_computation.6 | async-start | bytes 2621440 | tf_op jit(solution)/shard_map/reduce_scatter | solution.py:527
  345.9 37.6 %collective-permute-start.90 = (bf16[1024,1024]{1,0:T(8,128)(2,1)}, bf16[1024,1024]{1,0:T(8,128)(2,1)}, u32[]{:S(2)}, u32[]{:S(2)}) collective-permute-start(bf16[1024,1024]{1,0:T(8,128)(2,1)} %get-tuple-element.160), channel_id=1, source_target_pairs={{0,64},{64,0},{1,65},{65,1},{2,66},{66,2},{3,67},{67,3},{4,68},{68... | collective-permute-start | bytes 6291464 | tf_op jit(solution)/shard_map/ppermute | solution.py:62
  360.7 21.8 %collective-permute-start.91 = (bf16[128,1024]{1,0:T(8,128)(2,1)S(1)}, bf16[128,1024]{1,0:T(8,128)(2,1)S(1)}, u32[]{:S(2)}, u32[]{:S(2)}) collective-permute-start(bf16[128,1024]{1,0:T(8,128)(2,1)S(1)} %get-tuple-element.175), channel_id=1, source_target_pairs={{0,48},{4,52},{8,56},{12,60},{16,0},{20,4},{24,8},{28,12},{32,16},... | collective-permute-start | bytes 786440 | tf_op jit(solution)/shard_map/ppermute | solution.py:33
  363.6 18.9 %collective-permute-start.93 = (bf16[128,1024]{1,0:T(8,128)(2,1)S(1)}, bf16[128,1024]{1,0:T(8,128)(2,1)S(1)}, u32[]{:S(2)}, u32[]{:S(2)}) collective-permute-start(bf16[128,1024]{1,0:T(8,128)(2,1)S(1)} %get-tuple-element.176), channel_id=1, source_target_pairs={{0,16},{4,20},{8,24},{12,28},{16,32},{20,36},{24,40},{28,44},{32,4... | collective-permute-start | bytes 786440 | tf_op jit(solution)/shard_map/ppermute | solution.py:33
  363.6 18.9 %collective-permute-start.92 = (bf16[128,1024]{1,0:T(8,128)(2,1)S(1)}, bf16[128,1024]{1,0:T(8,128)(2,1)S(1)}, u32[]{:S(2)}, u32[]{:S(2)}) collective-permute-start(bf16[128,1024]{1,0:T(8,128)(2,1)S(1)} %get-tuple-element.177), channel_id=1, source_target_pairs={{0,32},{4,36},{8,40},{12,44},{16,48},{20,52},{24,56},{28,60},{32,0... | collective-permute-start | bytes 786440 | tf_op jit(solution)/shard_map/ppermute | solution.py:33
  388.0 89.7 %all-reduce.11.cloned.1.call-start = ((), (), s32[]{:S(2)}) async-start(), calls=%async_computation.7 | async-start | bytes 1572864 | tf_op jit(solution)/shard_map/psum | solution.py:583
  392.3 63.3 %collective-permute-start.104 = (bf16[64,1024]{1,0:T(8,128)(2,1)}, bf16[64,1024]{1,0:T(8,128)(2,1)}, u32[]{:S(2)}, u32[]{:S(2)}) collective-permute-start(bf16[64,1024]{1,0:T(8,128)(2,1)} %get-tuple-element.192), channel_id=1, source_target_pairs={{0,12},{4,0},{8,4},{12,8},{16,28},{20,16},{24,20},{28,24},{32,44},... | collective-permute-start | bytes 393224 | tf_op jit(solution)/shard_map/ppermute | solution.py:26
  392.5 63.1 %collective-permute-start.106 = (bf16[64,1024]{1,0:T(8,128)(2,1)}, bf16[64,1024]{1,0:T(8,128)(2,1)}, u32[]{:S(2)}, u32[]{:S(2)}) collective-permute-start(bf16[64,1024]{1,0:T(8,128)(2,1)} %get-tuple-element.193), channel_id=1, source_target_pairs={{0,4},{4,8},{8,12},{12,0},{16,20},{20,24},{24,28},{28,16},{32,36},... | collective-permute-start | bytes 393224 | tf_op jit(solution)/shard_map/ppermute | solution.py:26
  462.8 17.5 %collective-permute-start.109 = (bf16[144,1024]{1,0:T(8,128)(2,1)}, bf16[144,1024]{1,0:T(8,128)(2,1)S(1)}, u32[]{:S(2)}, u32[]{:S(2)}) collective-permute-start(bf16[144,1024]{1,0:T(8,128)(2,1)} %get-tuple-element.256), channel_id=1, source_target_pairs={{0,32},{4,36},{8,40},{12,44},{16,48},{20,52},{24,56},{28,60},{32,0... | collective-permute-start | bytes 884744 | tf_op jit(solution)/shard_map/ppermute | solution.py:33
  463.5 16.8 %collective-permute-start.110 = (bf16[144,1024]{1,0:T(8,128)(2,1)}, bf16[144,1024]{1,0:T(8,128)(2,1)}, u32[]{:S(2)}, u32[]{:S(2)}) collective-permute-start(bf16[144,1024]{1,0:T(8,128)(2,1)} %get-tuple-element.257), channel_id=1, source_target_pairs={{0,48},{4,52},{8,56},{12,60},{16,0},{20,4},{24,8},{28,12},{32,16},... | collective-permute-start | bytes 884744 | tf_op jit(solution)/shard_map/ppermute | solution.py:33
  (268 other events, 2663.4 us)
Sparse Core Ops, SparseCore 0:
  30.7 30.7 all-gather.4
  114.7 38.6 all-gather.2
  265.7 34.9 reduce-scatter.2
  328.6 39.9 all-reduce.8
  388.2 25.2 reduce-scatter.4
  436.6 41.0 all-reduce.10

commit v3 on v2

--- a/solution.py
+++ b/solution.py
@@ -261,7 +261,7 @@
             pltpu.VMEM((3, rows, 128), LOW),
             pltpu.SemaphoreType.DMA((3,)),
         ],
-        compiler_params=pltpu.CompilerParams(vmem_limit_bytes=40 << 20),
+        compiler_params=pltpu.CompilerParams(vmem_limit_bytes=60 << 20),
         cost_estimate=pl.CostEstimate(
             flops=4 * rows * 2 * rows * 128, bytes_accessed=4 << 20, transcendentals=rows * 2 * rows
         ),
@@ -282,7 +282,7 @@
             pltpu.VMEM((3, rows, 128), LOW),
             pltpu.SemaphoreType.DMA((3,)),
         ],
-        compiler_params=pltpu.CompilerParams(vmem_limit_bytes=40 << 20),
+        compiler_params=pltpu.CompilerParams(vmem_limit_bytes=60 << 20),
         cost_estimate=pl.CostEstimate(
             flops=10 * rows * 2 * rows * 128, bytes_accessed=6 << 20, transcendentals=rows * 2 * rows
         ),
@@ -352,13 +352,12 @@
     grad_own = jnp.concatenate(
         [pieces[0]] + [move_x(pieces[d], -d) for d in range(1, SIDE)], axis=0
     )
-    g_w_out = tn_dot(mixed_rows, grad_attn_all)
+    g_w_out = tn_dot(mixed_rows, grad_attn_all).astype(LOW)
     return grad_own, g_b_out, g_w_out
 
 
-def backward_heads(grad_mixed_own, stored, spots):
-    _, _, own, others, kept, _ = stored
-    dq, dkv0, dkv1, dkv2, dkv3 = attend_back(spots, own, others, kept, grad_mixed_own)
+def backward_heads(parts):
+    dq, dkv0, dkv1, dkv2, dkv3 = parts
     dkv = dkv0.astype(FULL)
     for d, part in enumerate((dkv1, dkv2, dkv3), 1):
         dkv = dkv + move_y_open(part, -d).astype(FULL)
@@ -374,7 +373,7 @@
     residual, normed_all = stored[0:2]
     gain_one, bias_one = vectors[0:2]
     grad_normed = scatter_z(local_dot(grad_qkv, w_heads).astype(LOW))
-    g_w_heads = tn_dot(grad_qkv, normed_all)
+    g_w_heads = tn_dot(grad_qkv, normed_all).astype(LOW)
     g_b_qkv = jnp.sum(grad_qkv.astype(FULL), axis=0)
     _, norm_one_pull = jax.vjp(layer_norm, residual, gain_one, bias_one)
     grad_residual_part, g_gain_one, g_bias_one = norm_one_pull(grad_normed)
@@ -412,40 +411,45 @@
     grad_last = lax.dynamic_index_in_dim(cotangent, here, 0, False)[0].astype(FULL)
     grad_last_all = lax.dynamic_index_in_dim(cotangent, here, 0, False)[0]
 
-    heads_kv = jnp.concatenate([w_qkv[0, :, 1].T, w_qkv[0, :, 2].T], axis=0)
-    heads_qo = jnp.concatenate([w_qkv[0, :, 0].T, w_out[0]], axis=0)
+    gap = jnp.zeros((HEAD_DIM,), LOW)
+    biases = jnp.concatenate(
+        [b_up[0], gap, b_qv[0, 1], b_qv[0, 0], gap, jnp.zeros((model_width - 512,), LOW)]
+    )[None]
+    heads_kv = jnp.concatenate(
+        [w_qkv[0, :, 1].T, w_qkv[0, :, 2].T, biases, jnp.zeros((15, model_width), LOW)], axis=0
+    )
+    heads_qo = jnp.concatenate(
+        [w_qkv[0, :, 0].T, w_out[0], jnp.zeros((16, model_width), LOW)], axis=0
+    )
     heads_qo_other = swap(heads_qo)
-    gap = jnp.zeros((HEAD_DIM,), LOW)
     small = jnp.concatenate(
-        [gain_one, bias_one, b_out, gain_two, bias_two, b_down]
-        + [
-            jnp.concatenate(
-                [b_up[0], gap, b_qv[0, 1], b_qv[0, 0], gap, jnp.zeros((model_width - 512,), LOW)]
-            )[None],
-            jnp.zeros((1, model_width), LOW),
-        ],
+        [gain_one, bias_one, b_out, gain_two, bias_two, b_down, jnp.zeros((2, model_width), LOW)],
         axis=0,
     )
     small_other = swap(small)
     up_own, down_other = w_up[0].T, swap(w_down[0])
-
-    def gather_heads(layer, after=None):
-        half = owner(layer, heads_kv, heads_qo_other)
-        if after is not None:
-            half, _ = tie(half, after)
-        mine = jnp.stack([half] + [move_x(half, d) for d in range(1, SIDE)])
-        return mine, swap(mine)
+    downward = [(x_here - d) % SIDE for d in range(SIDE)]
+
+    def reorder(pieces):
+        return [lax.dynamic_index_in_dim(pieces, place, 0, False) for place in downward]
+
+    def half_heads(layer):
+        return owner(layer, heads_kv, heads_qo_other)
 
     def join_heads(layer, mine, theirs):
         key_value, query_out = owner(layer, mine, theirs), owner(layer, theirs, mine)
-        whole = jnp.concatenate([key_value, query_out], axis=1).reshape(SIDE * TILE, model_width)
-        return whole, query_out.reshape(SIDE * 128, model_width)
-
-    def gather_units(layer, after=None):
-        half = owner(layer, up_own, down_other)
-        if after is not None:
-            half, _ = tie(half, after)
+        whole = jnp.concatenate([key_value[:, :128], query_out[:, :128]], axis=1)
+        back = query_out[:, :128].reshape(SIDE * 128, model_width)
+        rows = key_value[:, 128, :512].astype(FULL)
+        bias_heads = rows[:, 256:].reshape(1, SIDE * TILE)
+        bias_up = jnp.concatenate(reorder(rows[:, :256])).reshape(1, SIDE * TILE)
+        return (whole.reshape(SIDE * TILE, model_width), back), bias_heads, bias_up
+
+    def gather_whole(half):
         return lax.all_gather(half, "tensor", axis=0, tiled=True, axis_index_groups=X_GROUPS)
+
+    def gather_units(layer):
+        return gather_whole(owner(layer, up_own, down_other))
 
     def join_units(layer, mine):
         theirs = swap(mine)
@@ -456,9 +460,13 @@
         tuple(smalls[layer][row : row + 1].astype(FULL) for row in range(6)) for layer in range(2)
     ]
     normed = layer_norm(sequence, *vectors[0][0:2]).astype(LOW)
-    heads_first = join_heads(0, *gather_heads(0, normed))
+    half, normed = tie(half_heads(0), normed)
+    mine = jnp.stack([half] + [move_x(half, d) for d in range(1, SIDE)])
+    normed_all, mine = tie(gather_z(normed), mine)
+    heads_first, bias_heads_first, bias_up_first = join_heads(0, mine, swap(mine))
     units_first = gather_units(0)
-    normed_all = gather_z(normed)
+    heads_last = gather_whole(half_heads(1)).reshape(SIDE, -1, model_width)
+    units_last = gather_units(1)
     normed_all, segments = tie(normed_all, segments)
     segment_ids = lax.dynamic_index_in_dim(segments, here, 0, False)
     start_one = jnp.sum((segment_ids < 1).astype(jnp.int32))
@@ -484,38 +492,20 @@
         "upper": (jnp.arange(SIDE * 128) % 128 >= HEAD_DIM).astype(FULL),
     }
 
-    split_own = jnp.concatenate([smalls[0][6:7, :512], smalls[1][6:7, :512]], axis=0)
-    split_all = [split_own] + [move_x(split_own, d) for d in range(1, SIDE)]
-    bias_heads = [
-        jnp.concatenate([part[layer : layer + 1, 256:512] for part in split_all], axis=1).astype(FULL)
-        for layer in range(2)
-    ]
-    turn = ((x_here - jnp.arange(SIDE)) % SIDE)[None, :] == jnp.arange(SIDE)[:, None]
-    bias_up = [
-        jnp.sum(
-            jnp.where(
-                turn[:, :, None], jnp.stack([part[layer, 0:256] for part in split_all]).astype(FULL)[None], 0.0
-            ),
-            axis=1,
-        ).reshape(1, -1)
-        for layer in range(2)
-    ]
-
-    hidden, kept_heads_first = forward_attention(sequence, normed_all, spots, vectors[0], bias_heads[0], *heads_first)
-    heads_last = gather_heads(1, kept_heads_first[4])
+    hidden, kept_heads_first = forward_attention(sequence, normed_all, spots, vectors[0], bias_heads_first, *heads_first)
     units_first = join_units(0, units_first)
-    units_last = gather_units(1, kept_heads_first[4])
     hidden, grad_last_all = tie(hidden, gather_z(grad_last_all))
-    middle, kept_units_first = forward_hidden_units(hidden, vectors[0], bias_up[0], *units_first)
-    middle, *heads_last = tie(middle, *heads_last)
-    heads_last = join_heads(1, *heads_last)
+    middle, kept_units_first = forward_hidden_units(hidden, vectors[0], bias_up_first, *units_first)
+    mine = jnp.stack(reorder(heads_last))
+    middle, mine, theirs = tie(middle, mine, swap(mine))
+    heads_last, bias_heads_last, bias_up_last = join_heads(1, mine, theirs)
     middle = middle.astype(LOW).astype(FULL)
     normed_all = gather_z(layer_norm(middle, *vectors[1][0:2]).astype(LOW))
     hidden, kept_heads_last = forward_attention(
-        middle, normed_all, spots, vectors[1], bias_heads[1], *heads_last
+        middle, normed_all, spots, vectors[1], bias_heads_last, *heads_last
     )
     units_last = join_units(1, units_last)
-    result, kept_units_last = forward_hidden_units(hidden, vectors[1], bias_up[1], *units_last)
+    result, kept_units_last = forward_hidden_units(hidden, vectors[1], bias_up_last, *units_last)
 
     def swap_grads(layer, first, second):
         return owner(layer, first, second), swap(owner(layer, second, first))
@@ -523,21 +513,16 @@
     def add_grads(kept, arrived):
         return (kept.astype(FULL) + arrived.astype(FULL)).astype(LOW)
 
-    def scatter_units(grads):
+    def scatter_whole(grads):
         return lax.psum_scatter(
             grads, "tensor", scatter_dimension=0, tiled=True, axis_index_groups=X_GROUPS
         )
 
     def split_heads(g_w_heads, g_w_out):
         heads = g_w_heads.reshape(SIDE, TILE, model_width)
-        key_value = heads[:, 0:128].astype(LOW)
-        return key_value, (heads[:, 128:256] + g_w_out.reshape(SIDE, 128, model_width)).astype(LOW)
-
-    def scatter_heads(grads):
-        total = grads[0].astype(FULL)
-        for d in range(1, SIDE):
-            total = total + move_x(grads[d], -d).astype(FULL)
-        return total.astype(LOW)
+        return heads[:, 0:128], heads[:, 128:256] + g_w_out.reshape(SIDE, 128, model_width)
+
+    turn = jnp.stack(downward)[None, :] == jnp.arange(SIDE)[:, None]
 
     def pack_vectors(heads, units, g_b_out, g_b_up, g_b_qkv):
         by_turn = jnp.sum(
@@ -554,33 +539,37 @@
     grad_hidden, vec_units_last, g_b_up_last, g_up, g_down = backward_hidden_units(
         grad_last, grad_last_all, kept_units_last, vectors[1], *units_last
     )
-    units_kept, units_arrived = swap_grads(1, g_up, g_down)
+    grad_hidden, units_kept, units_arrived = tie(grad_hidden, *swap_grads(1, g_up, g_down))
+    units_sum_last = scatter_whole(add_grads(units_kept, units_arrived))
     grad_mixed, g_b_out_last, g_out = backward_mixed(grad_hidden, kept_heads_last, heads_last[1], spots)
-    grad_mixed, units_kept, units_arrived = tie(grad_mixed, units_kept, units_arrived)
-    units_sum_last = scatter_units(add_grads(units_kept, units_arrived))
-    grad_qkv = backward_heads(grad_mixed, kept_heads_last, spots)
+    grad_qkv = backward_heads(attend_back(spots, *kept_heads_last[2:5], grad_mixed))
     grad_middle, vec_heads_last, g_b_qkv_last, g_heads = backward_entry(
         grad_qkv, grad_hidden, kept_heads_last, vectors[1], heads_last[0]
     )
     heads_kept, heads_arrived = swap_grads(1, *split_heads(g_heads, g_out))
 
     grad_middle = grad_middle.astype(LOW).astype(FULL)
-    grad_middle, units_sum_last = tie(grad_middle, units_sum_last)
-    units_sum_last = lax.psum(units_sum_last, "ctx")
+    grad_down_all, heads_kept, heads_arrived = tie(
+        gather_z(grad_middle.astype(LOW)), heads_kept, heads_arrived
+    )
+    heads_sum_last = scatter_whole(
+        jnp.concatenate(reorder(add_grads(heads_kept, heads_arrived)), axis=0)
+    )
     grad_hidden, vec_units_first, g_b_up_first, g_up, g_down = backward_hidden_units(
-        grad_middle, gather_z(grad_middle.astype(LOW)), kept_units_first, vectors[0], *units_first
-    )
-    units_kept, units_arrived = swap_grads(0, g_up, g_down)
-    grad_hidden, heads_kept, heads_arrived = tie(grad_hidden, heads_kept, heads_arrived)
-    heads_sum_last = scatter_heads(add_grads(heads_kept, heads_arrived))
+        grad_middle, grad_down_all, kept_units_first, vectors[0], *units_first
+    )
+    grad_hidden, units_kept, units_arrived, units_sum_last = tie(
+        grad_hidden, *swap_grads(0, g_up, g_down), units_sum_last
+    )
+    units_sum_first = scatter_whole(add_grads(units_kept, units_arrived))
     grad_mixed, g_b_out_first, g_out = backward_mixed(grad_hidden, kept_heads_first, heads_first[1], spots)
-    grad_mixed, units_kept, units_arrived, heads_sum_last, units_sum_last = tie(
-        grad_mixed, units_kept, units_arrived, heads_sum_last, units_sum_last
-    )
-    units_sum_first = scatter_units(add_grads(units_kept, units_arrived))
-    grad_qkv = backward_heads(grad_mixed, kept_heads_first, spots)
-    grad_qkv, units_sum_first = tie(grad_qkv, units_sum_first)
-    units_sum_first, heads_sum_last = lax.psum((units_sum_first, heads_sum_last), "ctx")
+    parts = attend_back(spots, *kept_heads_first[2:5], grad_mixed)
+    parts, units_sum_first, heads_sum_last = tie(parts, units_sum_first, heads_sum_last)
+    units_sum_first, units_sum_last, heads_sum_last = lax.psum(
+        (units_sum_first, units_sum_last, heads_sum_last), "ctx"
+    )
+    grad_qkv = backward_heads(parts)
+
     gain_one, bias_one = vectors[0][0:2]
     residual, normed_all = kept_heads_first[0:2]
     grad_normed = local_dot(grad_qkv, heads_first[0])
@@ -591,14 +580,15 @@
         (g_gain_one, g_bias_one), vec_units_first, g_b_out_first, g_b_up_first, g_b_qkv_first
     )
     sums_last = pack_vectors(vec_heads_last, vec_units_last, g_b_out_last, g_b_up_last, g_b_qkv_last)
+    common = jnp.pad(jnp.concatenate([sums_first[:6], sums_last[:6]]), ((0, 4), (0, 0))).astype(LOW)
+    chunks = grad_normed.astype(LOW).reshape(SIDE, row_count, model_width)
+    chunks = even_pairs([jnp.concatenate([chunks[d], common], axis=0) for d in range(SIDE)], move_z)
+    heads_kept, heads_arrived = swap_grads(0, *split_heads(tn_dot(grad_qkv, normed_all).astype(LOW), g_out))
+    halves = add_grads(heads_kept, heads_arrived)
+    sums_first = jnp.concatenate([chunks[row_count : row_count + 6], sums_first[6:]])
+    sums_last = jnp.concatenate([chunks[row_count + 6 : row_count + 12], sums_last[6:]])
     sums = owner(0, sums_first, sums_last) + swap(owner(0, sums_last, sums_first))
-    common = jnp.pad(sums[:6], ((0, 10), (0, 0))).astype(LOW)
-    chunks = grad_normed.astype(LOW).reshape(SIDE, row_count, model_width)
-    chunks = [jnp.concatenate([chunks[d], common], axis=0) for d in range(SIDE)]
-    chunks = even_pairs(chunks, move_z)
-    heads_kept, heads_arrived = swap_grads(0, *split_heads(tn_dot(grad_qkv, normed_all), g_out))
-    halves = add_grads(heads_kept, heads_arrived)
-    common = chunks[row_count : row_count + 6].astype(LOW)
+    common = sums[:6].astype(LOW)
     split = sums[6:].reshape(SIDE, 1, 512).astype(LOW)
     packs = [
         jnp.concatenate(
@@ -613,6 +603,9 @@
         for d in range(SIDE)
     ]
     pack = even_sum(even_pairs(packs, move_x).astype(LOW), move_y)
+    pack, units_sum_first, units_sum_last, heads_sum_last = tie(
+        pack, units_sum_first, units_sum_last, heads_sum_last
+    )
     heads_sum_first, pack = pack[:128], pack[128:]
     _, norm_one_pull = jax.vjp(lambda rows: layer_norm(rows, gain_one, bias_one), residual)
     grad_first = grad_hidden + norm_one_pull(chunks[:row_count])[0]

time: 522 us -> 505 us (0.967)
  waiting for transfers between devices: 202 us -> 191 us
  other arithmetic: 67.8 us -> 57.3 us
  matrix products: 33.9 us -> 40.3 us
  Pallas kernels: 19.2 us -> 25.5 us
    psum x2 -> x1, waiting for transfers between devices: 11.9 us -> 0.02 us  [per_device(): lax.psum((units_sum_first, units_sum_last, heads_sum_last), 'ctx')]
    select_n x13 -> x14, other arithmetic: 15.6 us -> 6.53 us  [owner(): return jnp.where(here == layer, yes, no)]
    ppermute x12, waiting for transfers between devices: 44.9 us -> 38 us  [move_y_open(): return lax.ppermute(block, 'ctx', route)]
    unnamed x342 -> x246, local copies, waits for them, and re-layouts: 12.9 us -> 7.21 us
    ppermute x48, waiting for transfers between devices: 67.5 us -> 73 us  [move_z(): return lax.ppermute(block, 'tensor', route)]
    slice x8 -> x6, local copies, waits for them, and re-layouts: 7.73 us -> 2.48 us  [the longest x2 1.19 us: join_heads(): bias_up = jnp.concatenate(reorder(rows[:, :256])).reshape(1, SIDE * TILE)]
    ppermute x39 -> x30, waiting for transfers between devices: 66.9 us -> 61.8 us  [move_x(): return lax.ppermute(block, 'tensor', route)]
    ppermute x39 -> x30, starting transfers between devices: 48.8 us -> 44.2 us  [move_x(): return lax.ppermute(block, 'tensor', route)]
  transfers between devices with their start and end apart: 123 -> 115, of which waited for: 76 -> 74; matrix products, arithmetic and copies ran while one was open for 20% -> 21% of each run, Pallas kernels for 4% -> 4%
where the time goes in v3:
time: 505 us; the launch traced here: 496 us
  waiting for transfers between devices  191 us (38%)
  starting transfers between devices  138 us (27%)
  other arithmetic  57.3 us (11%)
  matrix products  40.3 us (8%)
  local copies, waits for them, and re-layouts  27.2 us (5%)
  Pallas kernels  25.5 us (5%)
  between operations  16.7 us (3%)
    ppermute x48, waiting for transfers between devices, move_z(): return lax.ppermute(block, 'tensor', route)  73 us
    ppermute x30, waiting for transfers between devices, move_x(): return lax.ppermute(block, 'tensor', route)  61.8 us
    ppermute x48, starting transfers between devices, move_z(): return lax.ppermute(block, 'tensor', route)  56.2 us
    ppermute x30, starting transfers between devices, move_x(): return lax.ppermute(block, 'tensor', route)  44.2 us
    ppermute x12, waiting for transfers between devices, move_y_open(): return lax.ppermute(block, 'ctx', route)  38 us
    ppermute x12, starting transfers between devices, move_y_open(): return lax.ppermute(block, 'ctx', route)  33 us
    dot_general x8, matrix products, local_dot(): return jnp.dot(left, right, preferred_element_type=FULL)  15.5 us
    pallas_call x2, Pallas kernels, attend_back(): pl.pallas_call(attend_back_kernel, out_shape=[jax.ShapeDtypeStruct((rows,...  14.3 us
  transfers between devices with their start and end apart: 115, of which 74 were waited for; matrix products, arithmetic and copies ran while one was open for 21% of the time, Pallas kernels for 4%

profile of v3, /device:TPU:0, one launch (start us, length us, event | category | flops | bytes accessed | tf_op | source)
XLA Modules:
  0.0 496.3 jit_solution(9568857758455066127)
XLA Ops:
  18.0 4.1 collective-permute-start.4
  33.8 5.0 %collective-permute-done.7 = bf16[144,1024]{1,0:T(8,128)(2,1)S(1)} collective-permute-done((bf16[144,1024]{1,0:T(8,128)(2,1)S(1)}, bf16[144,1024]{1,0:T(8,128)(2,1)S(1)}, u32[]{:S(2)}, u32[]{:S(2)}) %collective-permute-start.7) | collective-permute-done | bytes 294944 | tf_op jit(solution)/shard_map/ppermute | solution.py:33
  39.7 4.9 collective-permute-done.5
  70.8 4.7 collective-permute-start.14
  82.6 3.9 collective-permute-done.14.kv3_ref
  88.6 5.6 %attend.2.kept_ref = f32[1024,128]{1,0:T(8,128)} custom-call(s32[9]{0:T(128)} %pad_add_fusion.scalar_ref, s32[4,1,256]{2,1,0:T(1,128)} %get-tuple-element.305.low_ref, s32[4,1,256]{2,1,0:T(1,128)} %get-tuple-element.306.high_ref, s32[1024,1]{1,0:T(8,128)} %fusion.34.key_ref, bf16[1024,256]{1,0:T(8,128)(2,1)} %copy-done.11, bf16[1024,128]{1,0:T(8,128)(2,1)} %copy-done.89, ...), custom_call_target="tpu_custom_call" | custom-call | flops 1073741824 | bytes 4194304 | tf_op jit(solution)/shard_map/attend/pallas_call | solution.py:253
  110.5 5.0 %collective-permute-done.20 = bf16[64,1024]{1,0:T(8,128)(2,1)S(1)} collective-permute-done((bf16[64,1024]{1,0:T(8,128)(2,1)S(1)}, bf16[64,1024]{1,0:T(8,128)(2,1)S(1)}, u32[]{:S(2)}, u32[]{:S(2)}) %collective-permute-start.20) | collective-permute-done | bytes 131104 | tf_op jit(solution)/shard_map/ppermute | solution.py:26
  158.0 4.7 collective-permute-done.39
  167.5 11.3 %collective-permute-start.42 = (bf16[1024,128]{1,0:T(8,128)(2,1)S(1)}, bf16[1024,128]{1,0:T(8,128)(2,1)S(1)}, u32[]{:S(2)}, u32[]{:S(2)}) collective-permute-start(bf16[1024,128]{1,0:T(8,128)(2,1)S(1)} %slice.586), channel_id=1, source_target_pairs={{0,3},{4,7},{8,11},{12,15},{16,19},{20,23},{24,27},{28,31},{32,35}... | collective-permute-start | bytes 786440 | tf_op jit(solution)/shard_map/ppermute | solution.py:42
  186.8 5.6 %attend.3.kept_ref = f32[1024,128]{1,0:T(8,128)} custom-call(s32[9]{0:T(128)} %pad_add_fusion.scalar_ref, s32[4,1,256]{2,1,0:T(1,128)} %get-tuple-element.305.low_ref, s32[4,1,256]{2,1,0:T(1,128)} %get-tuple-element.306.high_ref, s32[1024,1]{1,0:T(8,128)} %fusion.34.key_ref, bf16[1024,256]{1,0:T(8,128)(2,1)} %copy-done.12, ...), custom_call_target="tpu_custom_call" | custom-call | flops 1073741824 | bytes 4194304 | tf_op jit(solution)/shard_map/attend/pallas_call | solution.py:253
  259.8 7.2 %attend_back.2 = (bf16[1024,128]{1,0:T(8,128)(2,1)}, bf16[1024,128]{1,0:T(8,128)(2,1)}, bf16[1024,128]{1,0:T(8,128)(2,1)}, bf16[1024,128]{1,0:T(8,128)(2,1)}, bf16[1024,128]{1,0:T(8,128)(2,1)}) custom-call(s32[9]{0:T(128)} %pad_add_fusion.scalar_ref, s32[4,1,256]{2,1,0:T(1,128)} %get-tuple-element.305.low_ref, s32[4,1,256]{2,1,0:T(1,128)} %get-tuple-element.306.high_ref, ...), custom_call_target="tpu_custom_call" | custom-call | flops 2684354560 | bytes 6291456 | tf_op jit(solution)/shard_map/attend_back/pallas_call | solution.py:274
  271.0 4.5 add_convert_fusion.1
  275.5 7.2 %collective-permute-done.62 = bf16[1024,128]{1,0:T(8,128)(2,1)S(1)} collective-permute-done((bf16[1024,128]{1,0:T(8,128)(2,1)}, bf16[1024,128]{1,0:T(8,128)(2,1)S(1)}, u32[]{:S(2)}, u32[]{:S(2)}) %collective-permute-start.62) | collective-permute-done | bytes 262176 | tf_op jit(solution)/shard_map/ppermute | solution.py:42
  282.7 9.3 %collective-permute-done.63 = bf16[1024,128]{1,0:T(8,128)(2,1)S(1)} collective-permute-done((bf16[1024,128]{1,0:T(8,128)(2,1)}, bf16[1024,128]{1,0:T(8,128)(2,1)S(1)}, u32[]{:S(2)}, u32[]{:S(2)}) %collective-permute-start.63) | collective-permute-done | bytes 262176 | tf_op jit(solution)/shard_map/ppermute | solution.py:42
  328.6 3.8 convert_reduce_fusion.3
  346.9 3.9 collective-permute-done.77
  352.0 3.9 add_convert_fusion
  380.9 7.1 %attend_back.3 = (bf16[1024,128]{1,0:T(8,128)(2,1)}, bf16[1024,128]{1,0:T(8,128)(2,1)}, bf16[1024,128]{1,0:T(8,128)(2,1)}, bf16[1024,128]{1,0:T(8,128)(2,1)}, bf16[1024,128]{1,0:T(8,128)(2,1)}) custom-call(s32[9]{0:T(128)} %pad_add_fusion.scalar_ref, s32[4,1,256]{2,1,0:T(1,128)} %get-tuple-element.305.low_ref, s32[4,1,256]{2,1,0:T(1,128)} %get-tuple-element.306.high_ref, ...), custom_call_target="tpu_custom_call" | custom-call | flops 2684354560 | bytes 6291456 | tf_op jit(solution)/shard_map/attend_back/pallas_call | solution.py:274
  388.0 4.5 reduce-scatter.6.cloned.1.call-done
  405.6 5.5 %collective-permute-done.87 = bf16[1024,128]{1,0:T(8,128)(2,1)S(1)} collective-permute-done((bf16[1024,128]{1,0:T(8,128)(2,1)}, bf16[1024,128]{1,0:T(8,128)(2,1)S(1)}, u32[]{:S(2)}, u32[]{:S(2)}) %collective-permute-start.87) | collective-permute-done | bytes 262176 | tf_op jit(solution)/shard_map/ppermute | solution.py:42
  451.2 5.8 %collective-permute-done.100 = bf16[144,1024]{1,0:T(8,128)(2,1)S(1)} collective-permute-done((bf16[144,1024]{1,0:T(8,128)(2,1)S(1)}, bf16[144,1024]{1,0:T(8,128)(2,1)S(1)}, u32[]{:S(2)}, u32[]{:S(2)}) %collective-permute-start.100) | collective-permute-done | bytes 294944 | tf_op jit(solution)/shard_map/ppermute | solution.py:33
  456.9 6.2 %collective-permute-done.101 = bf16[144,1024]{1,0:T(8,128)(2,1)S(1)} collective-permute-done((bf16[144,1024]{1,0:T(8,128)(2,1)S(1)}, bf16[144,1024]{1,0:T(8,128)(2,1)S(1)}, u32[]{:S(2)}, u32[]{:S(2)}) %collective-permute-start.101) | collective-permute-done | bytes 294944 | tf_op jit(solution)/shard_map/ppermute | solution.py:33
  466.3 7.1 %collective-permute-done.105 = bf16[144,1024]{1,0:T(8,128)(2,1)S(1)} collective-permute-done((bf16[144,1024]{1,0:T(8,128)(2,1)S(1)}, bf16[144,1024]{1,0:T(8,128)(2,1)S(1)}, u32[]{:S(2)}, u32[]{:S(2)}) %collective-permute-start.105) | collective-permute-done | bytes 294944 | tf_op jit(solution)/shard_map/ppermute | solution.py:37
  473.4 5.9 %collective-permute-done.104 = bf16[144,1024]{1,0:T(8,128)(2,1)S(1)} collective-permute-done((bf16[144,1024]{1,0:T(8,128)(2,1)S(1)}, bf16[144,1024]{1,0:T(8,128)(2,1)S(1)}, u32[]{:S(2)}, u32[]{:S(2)}) %collective-permute-start.104) | collective-permute-done | bytes 294944 | tf_op jit(solution)/shard_map/ppermute | solution.py:37
  (669 shorter events, 342.9 us)
Async XLA Ops:
  7.2 88.2 %all-gather.6.cloned.1.call-start = ((), (), s32[]{:S(2)}) async-start(), calls=%async_computation.4 | async-start | bytes 2621440 | tf_op jit(solution)/shard_map/all_gather | solution.py:449
  10.9 21.8 %collective-permute-start.24 = (bf16[256,1024]{1,0:T(8,128)(2,1)}, bf16[256,1024]{1,0:T(8,128)(2,1)S(1)}, u32[]{:S(2)}, u32[]{:S(2)}) collective-permute-start(bf16[256,1024]{1,0:T(8,128)(2,1)} %bitcast.231), channel_id=1, source_target_pairs={{0,64},{64,0},{1,65},{65,1},{2,66},{66,2},{3,67},{67,3},{4,68},{68... | collective-permute-start | bytes 1572872 | tf_op jit(solution)/shard_map/ppermute | solution.py:62
  23.7 15.2 %collective-permute-start.7 = (bf16[144,1024]{1,0:T(8,128)(2,1)S(1)}, bf16[144,1024]{1,0:T(8,128)(2,1)S(1)}, u32[]{:S(2)}, u32[]{:S(2)}) collective-permute-start(bf16[144,1024]{1,0:T(8,128)(2,1)S(1)} %get-tuple-element.56), channel_id=1, source_target_pairs={{0,48},{4,52},{8,56},{12,60},{16,0},{20,4},{24,8},{28,12},{32,16},... | collective-permute-start | bytes 884744 | tf_op jit(solution)/shard_map/ppermute | solution.py:33
  33.8 75.3 %all-gather.8.cloned.1.call-start = ((), (), s32[]{:S(2)}) async-start(), calls=%async_computation.5 | async-start | bytes 1474560 | tf_op jit(solution)/shard_map/all_gather | solution.py:449
  62.1 121.6 %all-gather.4.cloned.1.call-start = ((), (), s32[]{:S(2)}) async-start(), calls=%async_computation.3 | async-start | bytes 2621440 | tf_op jit(solution)/shard_map/all_gather | solution.py:449
  70.8 15.8 %collective-permute-start.14 = (bf16[1024,128]{1,0:T(8,128)(2,1)S(1)}, bf16[1024,128]{1,0:T(8,128)(2,1)S(1)}, u32[]{:S(2)}, u32[]{:S(2)}) collective-permute-start(bf16[1024,128]{1,0:T(8,128)(2,1)S(1)} %slice.557), channel_id=1, source_target_pairs={{0,3},{4,7},{8,11},{12,15},{16,19},{20,23},{24,27},{28,31},{32,35}... | collective-permute-start | bytes 786440 | tf_op jit(solution)/shard_map/ppermute | solution.py:42
  95.4 29.7 %collective-permute-start.29 = (bf16[1024,1024]{1,0:T(8,128)(2,1)}, bf16[1024,1024]{1,0:T(8,128)(2,1)}, u32[]{:S(2)}, u32[]{:S(2)}) collective-permute-start(bf16[1024,1024]{1,0:T(8,128)(2,1)} %all-gather.6.cloned.1.call-done), channel_id=1, source_target_pairs={{0,64},{64,0},{1,65},{65,1},{2,66},{66,2},{3,67},{67,3},{4,68},{68... | collective-permute-start | bytes 6291464 | tf_op jit(solution)/shard_map/ppermute | solution.py:62
  118.6 22.4 %collective-permute-start.33 = (bf16[4,144,1024]{2,1,0:T(8,128)(2,1)S(1)}, bf16[4,144,1024]{2,1,0:T(8,128)(2,1)S(1)}, u32[]{:S(2)}, u32[]{:S(2)}) collective-permute-start(bf16[4,144,1024]{2,1,0:T(8,128)(2,1)S(1)} %pad_maximum_fusion.3), channel_id=1, source_target_pairs={{0,64},{64,0},{1,65},{65,1},{2,66},{66,2},{3,67},{67,3},{4,68},{68... | collective-permute-start | bytes 3538952 | tf_op jit(solution)/shard_map/ppermute | solution.py:62
  134.7 217.3 %reduce-scatter.4.cloned.1.call-start = ((), (), s32[]{:S(2)}) async-start(), calls=%async_computation.6 | async-start | bytes 2621440 | tf_op jit(solution)/shard_map/reduce_scatter | solution.py:517
  167.5 18.0 %collective-permute-start.42 = (bf16[1024,128]{1,0:T(8,128)(2,1)S(1)}, bf16[1024,128]{1,0:T(8,128)(2,1)S(1)}, u32[]{:S(2)}, u32[]{:S(2)}) collective-permute-start(bf16[1024,128]{1,0:T(8,128)(2,1)S(1)} %slice.586), channel_id=1, source_target_pairs={{0,3},{4,7},{8,11},{12,15},{16,19},{20,23},{24,27},{28,31},{32,35}... | collective-permute-start | bytes 786440 | tf_op jit(solution)/shard_map/ppermute | solution.py:42
  183.6 31.5 %collective-permute-start.25 = (bf16[1024,1024]{1,0:T(8,128)(2,1)}, bf16[1024,1024]{1,0:T(8,128)(2,1)}, u32[]{:S(2)}, u32[]{:S(2)}) collective-permute-start(bf16[1024,1024]{1,0:T(8,128)(2,1)} %all-gather.4.cloned.1.call-done), channel_id=1, source_target_pairs={{0,64},{64,0},{1,65},{65,1},{2,66},{66,2},{3,67},{67,3},{4,68},{68... | collective-permute-start | bytes 6291464 | tf_op jit(solution)/shard_map/ppermute | solution.py:62
  267.1 15.7 %collective-permute-start.62 = (bf16[1024,128]{1,0:T(8,128)(2,1)}, bf16[1024,128]{1,0:T(8,128)(2,1)S(1)}, u32[]{:S(2)}, u32[]{:S(2)}) collective-permute-start(bf16[1024,128]{1,0:T(8,128)(2,1)} %get-tuple-element.68), channel_id=1, source_target_pairs={{1,0},{2,1},{3,2},{5,4},{6,5},{7,6},{9,8},{10,9},{11,10},{13,12},{... | collective-permute-start | bytes 786440 | tf_op jit(solution)/shard_map/ppermute | solution.py:42
  268.4 23.7 %collective-permute-start.63 = (bf16[1024,128]{1,0:T(8,128)(2,1)}, bf16[1024,128]{1,0:T(8,128)(2,1)S(1)}, u32[]{:S(2)}, u32[]{:S(2)}) collective-permute-start(bf16[1024,128]{1,0:T(8,128)(2,1)} %get-tuple-element.69), channel_id=1, source_target_pairs={{2,0},{3,1},{6,4},{7,5},{10,8},{11,9},{14,12},{15,13},{18,16},{19,... | collective-permute-start | bytes 786440 | tf_op jit(solution)/shard_map/ppermute | solution.py:42
  269.7 25.1 %collective-permute-start.64 = (bf16[1024,128]{1,0:T(8,128)(2,1)}, bf16[1024,128]{1,0:T(8,128)(2,1)S(1)}, u32[]{:S(2)}, u32[]{:S(2)}) collective-permute-start(bf16[1024,128]{1,0:T(8,128)(2,1)} %get-tuple-element.70), channel_id=1, source_target_pairs={{3,0},{7,4},{11,8},{15,12},{19,16},{23,20},{27,24},{31,28},{35,32}... | collective-permute-start | bytes 786440 | tf_op jit(solution)/shard_map/ppermute | solution.py:42
  275.5 112.5 %reduce-scatter.8.cloned.1.call-start = ((), (), s32[]{:S(2)}) async-start(), calls=%async_computation.8 | async-start | bytes 1310720 | tf_op jit(solution)/shard_map/reduce_scatter | solution.py:517
  311.6 17.0 %collective-permute-start.74 = (bf16[4,128,1024]{2,1,0:T(8,128)(2,1)S(1)}, bf16[4,128,1024]{2,1,0:T(8,128)(2,1)S(1)}, u32[]{:S(2)}, u32[]{:S(2)}) collective-permute-start(bf16[4,128,1024]{2,1,0:T(8,128)(2,1)S(1)} %get-tuple-element.165), channel_id=1, source_target_pairs={{0,64},{64,0},{1,65},{65,1},{2,66},{66,2},{3,67},{67,3},{4,68},{68... | collective-permute-start | bytes 3145736 | tf_op jit(solution)/shard_map/ppermute | solution.py:62
  336.3 15.6 %collective-permute-start.78 = (bf16[1024,1024]{1,0:T(8,128)(2,1)}, bf16[1024,1024]{1,0:T(8,128)(2,1)}, u32[]{:S(2)}, u32[]{:S(2)}) collective-permute-start(bf16[1024,1024]{1,0:T(8,128)(2,1)} %get-tuple-element.161), channel_id=1, source_target_pairs={{0,64},{64,0},{1,65},{65,1},{2,66},{66,2},{3,67},{67,3},{4,68},{68... | collective-permute-start | bytes 6291464 | tf_op jit(solution)/shard_map/ppermute | solution.py:62
  337.9 54.6 %reduce-scatter.6.cloned.1.call-start = ((), (), s32[]{:S(2)}) async-start(), calls=%async_computation.7 | async-start | bytes 2621440 | tf_op jit(solution)/shard_map/reduce_scatter | solution.py:517
  355.9 123.6 %all-reduce.8.cloned.1.call-start = ((), (), s32[]{:S(2)}) async-start(), calls=%async_computation.9 | async-start | bytes 2621440 | tf_op jit(solution)/shard_map/psum | solution.py:568
  375.1 74.5 %collective-permute-start.94 = (bf16[64,1024]{1,0:T(8,128)(2,1)}, bf16[64,1024]{1,0:T(8,128)(2,1)}, u32[]{:S(2)}, u32[]{:S(2)}) collective-permute-start(bf16[64,1024]{1,0:T(8,128)(2,1)} %get-tuple-element.198), channel_id=1, source_target_pairs={{0,12},{4,0},{8,4},{12,8},{16,28},{20,16},{24,20},{28,24},{32,44},... | collective-permute-start | bytes 393224 | tf_op jit(solution)/shard_map/ppermute | solution.py:26
  375.8 74.0 %collective-permute-start.96 = (bf16[64,1024]{1,0:T(8,128)(2,1)}, bf16[64,1024]{1,0:T(8,128)(2,1)}, u32[]{:S(2)}, u32[]{:S(2)}) collective-permute-start(bf16[64,1024]{1,0:T(8,128)(2,1)} %get-tuple-element.199), channel_id=1, source_target_pairs={{0,4},{4,8},{8,12},{12,0},{16,20},{20,24},{24,28},{28,16},{32,36},... | collective-permute-start | bytes 393224 | tf_op jit(solution)/shard_map/ppermute | solution.py:26
  395.1 16.0 %collective-permute-start.87 = (bf16[1024,128]{1,0:T(8,128)(2,1)}, bf16[1024,128]{1,0:T(8,128)(2,1)S(1)}, u32[]{:S(2)}, u32[]{:S(2)}) collective-permute-start(bf16[1024,128]{1,0:T(8,128)(2,1)} %get-tuple-element.88), channel_id=1, source_target_pairs={{3,0},{7,4},{11,8},{15,12},{19,16},{23,20},{27,24},{31,28},{35,32}... | collective-permute-start | bytes 786440 | tf_op jit(solution)/shard_map/ppermute | solution.py:42
  447.2 16.0 %collective-permute-start.101 = (bf16[144,1024]{1,0:T(8,128)(2,1)S(1)}, bf16[144,1024]{1,0:T(8,128)(2,1)S(1)}, u32[]{:S(2)}, u32[]{:S(2)}) collective-permute-start(bf16[144,1024]{1,0:T(8,128)(2,1)S(1)} %get-tuple-element.268), channel_id=1, source_target_pairs={{0,48},{4,52},{8,56},{12,60},{16,0},{20,4},{24,8},{28,12},{32,16},... | collective-permute-start | bytes 884744 | tf_op jit(solution)/shard_map/ppermute | solution.py:33
  463.5 15.8 %collective-permute-start.104 = (bf16[144,1024]{1,0:T(8,128)(2,1)S(1)}, bf16[144,1024]{1,0:T(8,128)(2,1)S(1)}, u32[]{:S(2)}, u32[]{:S(2)}) collective-permute-start(bf16[144,1024]{1,0:T(8,128)(2,1)S(1)} %add_convert_fusion.4), channel_id=1, source_target_pairs={{0,1},{1,2},{2,3},{3,0},{4,5},{5,6},{6,7},{7,4},{8,9},{9,10},{10,1... | collective-permute-start | bytes 884744 | tf_op jit(solution)/shard_map/ppermute | solution.py:37
  (211 other events, 1785.3 us)
Sparse Core Ops, SparseCore 0:
  33.9 38.0 all-gather.5
  74.3 24.4 all-gather.7
  134.8 39.9 all-gather.3
  275.6 45.1 reduce-scatter.3
  338.0 19.9 reduce-scatter.7
  360.2 32.1 reduce-scatter.5
  419.3 46.0 all-reduce.7

commit v4 on v3

--- a/solution.py
+++ b/solution.py
@@ -97,6 +97,19 @@
     return center * lax.rsqrt(spread + EPSILON) * gain + bias
 
 
+def layer_norm_back(grad, values, gain):
+    center = values - jnp.mean(values, axis=-1, keepdims=True)
+    scale = lax.rsqrt(jnp.mean(center * center, axis=-1, keepdims=True) + EPSILON)
+    unit = center * scale
+    part = grad * gain
+    back = scale * (
+        part
+        - jnp.mean(part, axis=-1, keepdims=True)
+        - unit * jnp.mean(part * unit, axis=-1, keepdims=True)
+    )
+    return back, jnp.sum(grad * unit, axis=0, keepdims=True), jnp.sum(grad, axis=0, keepdims=True)
+
+
 def local_dot(left, right):
     return jnp.dot(left, right, preferred_element_type=FULL)
 
@@ -117,9 +130,35 @@
     return lax.dot_general(left, right, (((0,), (0,)), ((), ())), preferred_element_type=FULL)
 
 
+def place_in_block(order, x_here, z_here):
+    from_x = (x_here + (order >> 8)) & 3
+    from_z = (z_here - ((order >> 6) & 3)) & 3
+    return (from_x << 8) + (from_z << 6) + (order & 63)
+
+
+def first_of_document(place, start_one, start_two):
+    return jnp.where(place >= start_two, start_two, jnp.where(place >= start_one, start_one, 0))
+
+
+def tile_bounds(scalar_ref, pair, rows_all):
+    block, x_here, _, start_one, start_two = [scalar_ref[i] for i in range(5)]
+    least, most = [], []
+    for part in range(2):
+        place = block * rows_all + ((x_here + pair * 2 + part) & 3) * TILE
+        least.append(first_of_document(place, start_one, start_two))
+        most.append(first_of_document(place + TILE - 1, start_one, start_two))
+    return jnp.minimum(*least), jnp.maximum(*most)
+
+
+def tile_limits(scalar_ref, index, rows_all):
+    block, x_here, z_here, start_one, start_two = [scalar_ref[i] for i in range(5)]
+    order = lax.broadcasted_iota(jnp.int32, (1, TILE), 1) + index * TILE
+    high = block * rows_all + place_in_block(order, x_here, z_here)
+    return first_of_document(high, start_one, start_two), high
+
+
 def attend_kernel(
-    scalar_ref, low_ref, high_ref, key_ref, own_ref, kv1_ref, kv2_ref, kv3_ref, out_ref,
-    peak, mixed, held, arrived,
+    scalar_ref, own_ref, kv1_ref, kv2_ref, kv3_ref, out_ref, peak, mixed, held, keys, arrived
 ):
     block = scalar_ref[0]
     rows_all = own_ref.shape[0]
@@ -132,32 +171,39 @@
         copy.start()
     peak[...] = jnp.full_like(peak, MASK_FILL)
     mixed[...] = jnp.zeros_like(mixed)
+    keys[...] = place_in_block(
+        lax.broadcasted_iota(jnp.int32, keys.shape, 0), scalar_ref[1], scalar_ref[2]
+    )
     for d in range(SIDE):
         if d > 0:
             copies[d - 1].wait()
         start = (block - d) * rows_all
 
-        @pl.loop(0, tiles)
-        def _(index, d=d, start=start):
-            rows = pl.ds(pl.multiple_of(index * TILE, TILE), TILE)
-            least, most = scalar_ref[1 + index], scalar_ref[1 + tiles + index]
+        @pl.loop(0, tiles // 2)
+        def _(pair, d=d, start=start):
+            least, most = tile_bounds(scalar_ref, pair, rows_all)
+            indices = [pair * 2, pair * 2 + 1]
 
             def step(masked):
                 key_values = own_ref[:, 0:128] if d == 0 else held[d - 1]
-                raw = nt_dot(key_values, own_ref[rows, 128:256])
-                if masked:
-                    places = key_ref[...] - d * rows_all
-                    allowed = places >= low_ref[index]
-                    if d == 0:
-                        allowed = allowed & (places <= high_ref[index])
-                    raw = jnp.where(allowed, raw, MASK_FILL)
-                old = peak[index]
-                top = jnp.maximum(old, jnp.max(raw, axis=0, keepdims=True))
-                weight = jnp.exp2(raw - top).astype(LOW)
                 lanes = lax.broadcasted_iota(jnp.int32, key_values.shape, 1)
                 ones_values = jnp.where(lanes < HEAD_DIM, jnp.ones_like(key_values), key_values)
-                peak[index] = top
-                mixed[index] = mixed[index] * jnp.exp2(old - top) + tn_dot(ones_values, weight)
+                raws = []
+                for index in indices:
+                    rows = pl.ds(pl.multiple_of(index * TILE, TILE), TILE)
+                    raws.append(nt_dot(key_values, own_ref[rows, 128:256]))
+                for index, raw in zip(indices, raws):
+                    if masked:
+                        low, high = tile_limits(scalar_ref, index, rows_all)
+                        allowed = keys[...] >= low - start
+                        if d == 0:
+                            allowed = allowed & (keys[...] <= high - start)
+                        raw = jnp.where(allowed, raw, MASK_FILL)
+                    old = peak[index]
+                    top = jnp.maximum(old, jnp.max(raw, axis=0, keepdims=True))
+                    weight = jnp.exp2(raw - top).astype(LOW)
+                    peak[index] = top
+                    mixed[index] = mixed[index] * jnp.exp2(old - top) + tn_dot(ones_values, weight)
 
             if d == 0:
                 step(True)
@@ -177,9 +223,9 @@
 
 
 def attend_back_kernel(
-    scalar_ref, low_ref, high_ref, key_ref, own_ref, kv1_ref, kv2_ref, kv3_ref, kept_ref, grad_ref,
+    scalar_ref, own_ref, kv1_ref, kv2_ref, kv3_ref, kept_ref, grad_ref,
     dq_ref, d0_ref, d1_ref, d2_ref, d3_ref,
-    query_sum, key_sum, held, arrived,
+    query_sum, key_sum, held, keys, stats, arrived,
 ):
     block = scalar_ref[0]
     rows_all = own_ref.shape[0]
@@ -191,6 +237,17 @@
     for copy in copies:
         copy.start()
     query_sum[...] = jnp.zeros_like(query_sum)
+    keys[...] = place_in_block(
+        lax.broadcasted_iota(jnp.int32, keys.shape, 0), scalar_ref[1], scalar_ref[2]
+    )
+
+    @pl.loop(0, tiles)
+    def _(index):
+        rows = pl.ds(pl.multiple_of(index * TILE, TILE), TILE)
+        kept = kept_ref[rows, :]
+        stats[index, 0:1, :] = kept.T[0:1, :]
+        stats[index, 1:2, :] = jnp.sum((kept * grad_ref[rows, :].astype(FULL)).T, axis=0, keepdims=True)
+
     for d, out_ref in enumerate((d0_ref, d1_ref, d2_ref, d3_ref)):
         if d > 0:
             copies[d - 1].wait()
@@ -200,30 +257,29 @@
             start = (block - d) * rows_all
             key_sum[...] = jnp.zeros_like(key_sum)
 
-            @pl.loop(0, tiles)
-            def _(index):
-                rows = pl.ds(pl.multiple_of(index * TILE, TILE), TILE)
-                least, most = scalar_ref[1 + index], scalar_ref[1 + tiles + index]
+            @pl.loop(0, tiles // 2)
+            def _(pair):
+                least, most = tile_bounds(scalar_ref, pair, rows_all)
+                indices = [pair * 2, pair * 2 + 1]
 
                 def step(masked):
-                    queries = own_ref[rows, 128:256]
-                    grad = grad_ref[rows, :]
-                    kept = kept_ref[rows, :]
-                    level = kept.T[0:1, :]
-                    meet = jnp.sum((kept * grad.astype(FULL)).T, axis=0, keepdims=True)
                     key_values = own_ref[:, 0:128] if d == 0 else held[d - 1]
-                    probs = jnp.exp2(nt_dot(key_values, queries) - level)
-                    if masked:
-                        places = key_ref[...] - d * rows_all
-                        allowed = places >= low_ref[index]
-                        if d == 0:
-                            allowed = allowed & (places <= high_ref[index])
-                        probs = jnp.where(allowed, probs, 0.0)
-                    grad_scores = (probs * (nt_dot(key_values, grad) - meet)).astype(LOW)
-                    key_sum[...] += local_dot(grad_scores, queries) * LN_TWO + local_dot(
-                        probs.astype(LOW), grad
-                    )
-                    query_sum[rows, :] += tn_dot(grad_scores, key_values)
+                    spans = [pl.ds(pl.multiple_of(index * TILE, TILE), TILE) for index in indices]
+                    raws = [nt_dot(key_values, own_ref[rows, 128:256]) for rows in spans]
+                    meets = [nt_dot(key_values, grad_ref[rows, :]) for rows in spans]
+                    for index, rows, raw, meet in zip(indices, spans, raws, meets):
+                        probs = jnp.exp2(raw - stats[index, 0:1, :])
+                        if masked:
+                            low, high = tile_limits(scalar_ref, index, rows_all)
+                            allowed = keys[...] >= low - start
+                            if d == 0:
+                                allowed = allowed & (keys[...] <= high - start)
+                            probs = jnp.where(allowed, probs, 0.0)
+                        grad_scores = (probs * (meet - stats[index, 1:2, :])).astype(LOW)
+                        key_sum[...] += local_dot(grad_scores, own_ref[rows, 128:256]) * LN_TWO + local_dot(
+                            probs.astype(LOW), grad_ref[rows, :]
+                        )
+                        query_sum[rows, :] += tn_dot(grad_scores, key_values)
 
                 if d == 0:
                     step(True)
@@ -245,7 +301,7 @@
 
 VMEM_SPEC = pl.BlockSpec(memory_space=pltpu.VMEM)
 SMEM_SPEC = pl.BlockSpec(memory_space=pltpu.SMEM)
-ANY_SPEC = pl.BlockSpec(memory_space=pl.ANY)
+FAR_SPEC = pl.BlockSpec(memory_space=pltpu.HBM)
 
 
 def attend(spots, own, others):
@@ -253,20 +309,21 @@
     return pl.pallas_call(
         attend_kernel,
         out_shape=jax.ShapeDtypeStruct((rows, 128), FULL),
-        in_specs=[SMEM_SPEC] + [VMEM_SPEC] * 4 + [ANY_SPEC] * 3,
+        in_specs=[SMEM_SPEC, VMEM_SPEC] + [FAR_SPEC] * 3,
         out_specs=VMEM_SPEC,
         scratch_shapes=[
             pltpu.VMEM((rows // TILE, 1, TILE), FULL),
             pltpu.VMEM((rows // TILE, 128, TILE), FULL),
             pltpu.VMEM((3, rows, 128), LOW),
+            pltpu.VMEM((rows, 1), jnp.int32),
             pltpu.SemaphoreType.DMA((3,)),
         ],
-        compiler_params=pltpu.CompilerParams(vmem_limit_bytes=60 << 20),
+        compiler_params=pltpu.CompilerParams(vmem_limit_bytes=40 << 20),
         cost_estimate=pl.CostEstimate(
             flops=4 * rows * 2 * rows * 128, bytes_accessed=4 << 20, transcendentals=rows * 2 * rows
         ),
         name="attend",
-    )(spots["scalars"], spots["low"], spots["high"], spots["keys"], own, *others)
+    )(spots["scalars"], own, *others)
 
 
 def attend_back(spots, own, others, kept, grad):
@@ -274,20 +331,22 @@
     return pl.pallas_call(
         attend_back_kernel,
         out_shape=[jax.ShapeDtypeStruct((rows, 128), LOW)] * 5,
-        in_specs=[SMEM_SPEC] + [VMEM_SPEC] * 4 + [ANY_SPEC] * 3 + [VMEM_SPEC] * 2,
+        in_specs=[SMEM_SPEC, VMEM_SPEC] + [FAR_SPEC] * 3 + [VMEM_SPEC] * 2,
         out_specs=[VMEM_SPEC] * 5,
         scratch_shapes=[
             pltpu.VMEM((rows, 128), FULL),
             pltpu.VMEM((rows, 128), FULL),
             pltpu.VMEM((3, rows, 128), LOW),
+            pltpu.VMEM((rows, 1), jnp.int32),
+            pltpu.VMEM((rows // TILE, 8, TILE), FULL),
             pltpu.SemaphoreType.DMA((3,)),
         ],
-        compiler_params=pltpu.CompilerParams(vmem_limit_bytes=60 << 20),
+        compiler_params=pltpu.CompilerParams(vmem_limit_bytes=40 << 20),
         cost_estimate=pl.CostEstimate(
             flops=10 * rows * 2 * rows * 128, bytes_accessed=6 << 20, transcendentals=rows * 2 * rows
         ),
         name="attend_back",
-    )(spots["scalars"], spots["low"], spots["high"], spots["keys"], own, *others, kept, grad)
+    )(spots["scalars"], own, *others, kept, grad)
 
 
 def tie(first, *rest):
@@ -297,14 +356,18 @@
 X_GROUPS = [[x * SIDE + z for x in range(SIDE)] for z in range(SIDE)]
 
 
-def forward_attention(residual, normed_all, spots, vectors, bias_qkv, w_heads, w_back):
+def forward_attention(residual, normed_all, spots, vectors, bias_qkv, w_heads, w_back, early=None):
     b_out = vectors[2]
     projected = ((nt_dot(normed_all, w_heads) + bias_qkv) * spots["scale"]).astype(LOW)
     width = projected.shape[1] // SIDE
     pieces = [projected[:, d * width : (d + 1) * width] for d in range(SIDE)]
     own = jnp.concatenate([pieces[0]] + [move_x(pieces[d], -d) for d in range(1, SIDE)], axis=0)
+    if early is not None:
+        own, early = tie(own, early)
     others = [move_y_open(own[:, 0:128], d) for d in range(1, SIDE)]
     kept = attend(spots, own, others)
+    if early is not None:
+        kept, early = tie(kept, gather_z(early))
     lanes = lax.broadcasted_iota(jnp.int32, kept.shape, 1)
     mixed = jnp.where(lanes < HEAD_DIM, 0.0, kept).astype(LOW)
     rows = mixed.shape[0] // SIDE
@@ -312,7 +375,7 @@
         [mixed[0:rows]] + [move_x(mixed[d * rows : (d + 1) * rows], d) for d in range(1, SIDE)], axis=1
     )
     hidden = residual + (scatter_z(local_dot(mixed_rows, w_back).astype(LOW)) + b_out)
-    return hidden, (residual, normed_all, own, others, kept, mixed_rows)
+    return hidden, (residual, normed_all, own, others, kept, mixed_rows), early
 
 
 def forward_hidden_units(hidden, vectors, b_up, w_up, w_down):
@@ -326,7 +389,7 @@
 
 def backward_hidden_units(grad_out, grad_down_all, stored, vectors, w_up, w_down):
     hidden, normed_two_all, up_value, activated = stored
-    gain_two, bias_two = vectors[3:5]
+    gain_two = vectors[3]
     grad_down = grad_out.astype(LOW)
     g_b_down = jnp.sum(grad_down.astype(FULL), axis=0, keepdims=True)
     _, gelu_pull = jax.vjp(jax.nn.gelu, up_value)
@@ -336,8 +399,7 @@
     g_w_down = tn_dot(activated, grad_down_all).astype(LOW)
     g_b_up = jnp.sum(grad_up.astype(FULL), axis=0)
     g_w_up = tn_dot(grad_up, normed_two_all).astype(LOW)
-    _, norm_two_pull = jax.vjp(layer_norm, hidden, gain_two, bias_two)
-    grad_hidden_part, g_gain_two, g_bias_two = norm_two_pull(grad_normed_two)
+    grad_hidden_part, g_gain_two, g_bias_two = layer_norm_back(grad_normed_two, hidden, gain_two)
     grad_hidden = grad_out + grad_hidden_part
     return grad_hidden, (g_gain_two, g_bias_two, g_b_down), g_b_up, g_w_up, g_w_down
 
@@ -371,12 +433,11 @@
 
 def backward_entry(grad_qkv, grad_hidden, stored, vectors, w_heads):
     residual, normed_all = stored[0:2]
-    gain_one, bias_one = vectors[0:2]
+    gain_one = vectors[0]
     grad_normed = scatter_z(local_dot(grad_qkv, w_heads).astype(LOW))
     g_w_heads = tn_dot(grad_qkv, normed_all).astype(LOW)
     g_b_qkv = jnp.sum(grad_qkv.astype(FULL), axis=0)
-    _, norm_one_pull = jax.vjp(layer_norm, residual, gain_one, bias_one)
-    grad_residual_part, g_gain_one, g_bias_one = norm_one_pull(grad_normed)
+    grad_residual_part, g_gain_one, g_bias_one = layer_norm_back(grad_normed, residual, gain_one)
     return grad_hidden + grad_residual_part, (g_gain_one, g_bias_one), g_b_qkv, g_w_heads
 
 
@@ -402,7 +463,6 @@
     spot = lax.axis_index("tensor")
     x_here, z_here = spot // SIDE, spot % SIDE
     row_count, model_width = inputs.shape[2], inputs.shape[3]
-    block_rows = row_count * SIDE * SIDE
 
     def owner(layer, yes, no):
         return jnp.where(here == layer, yes, no)
@@ -448,9 +508,6 @@
     def gather_whole(half):
         return lax.all_gather(half, "tensor", axis=0, tiled=True, axis_index_groups=X_GROUPS)
 
-    def gather_units(layer):
-        return gather_whole(owner(layer, up_own, down_other))
-
     def join_units(layer, mine):
         theirs = swap(mine)
         return owner(layer, mine, theirs), owner(layer, theirs, mine)
@@ -462,46 +519,35 @@
     normed = layer_norm(sequence, *vectors[0][0:2]).astype(LOW)
     half, normed = tie(half_heads(0), normed)
     mine = jnp.stack([half] + [move_x(half, d) for d in range(1, SIDE)])
-    normed_all, mine = tie(gather_z(normed), mine)
+    half = owner(0, up_own, down_other)
+    normed_all, mine, half = tie(gather_z(normed), mine, half)
     heads_first, bias_heads_first, bias_up_first = join_heads(0, mine, swap(mine))
-    units_first = gather_units(0)
+    units_first = gather_whole(half)
     heads_last = gather_whole(half_heads(1)).reshape(SIDE, -1, model_width)
-    units_last = gather_units(1)
+    units_last = gather_whole(owner(1, up_own, down_other))
     normed_all, segments = tie(normed_all, segments)
     segment_ids = lax.dynamic_index_in_dim(segments, here, 0, False)
     start_one = jnp.sum((segment_ids < 1).astype(jnp.int32))
     start_two = jnp.sum((segment_ids < 2).astype(jnp.int32))
 
-    def first_of(place):
-        return jnp.where(place >= start_two, start_two, jnp.where(place >= start_one, start_one, 0))
-
-    order = jnp.arange(block_rows)
-    from_x = (x_here + order // TILE) % SIDE
-    from_z = (z_here - order // row_count % SIDE) % SIDE
-    place = block * block_rows + (from_x * SIDE + from_z) * row_count + order % row_count
-    tile_first = block * block_rows + (x_here + jnp.arange(SIDE)) % SIDE * TILE
     lane = jnp.arange(SIDE * TILE) % TILE
     spots = {
-        "scalars": jnp.concatenate(
-            [block[None], first_of(tile_first), first_of(tile_first + TILE - 1)]
-        ).astype(jnp.int32),
-        "high": place.astype(jnp.int32).reshape(SIDE, 1, TILE),
-        "low": first_of(place).astype(jnp.int32).reshape(SIDE, 1, TILE),
-        "keys": place.astype(jnp.int32).reshape(block_rows, 1),
+        "scalars": jnp.stack([block, x_here, z_here, start_one, start_two]).astype(jnp.int32),
         "scale": jnp.where(lane < 128, 1.0, jnp.where(lane < 192, BASE_TWO_SCALE, 0.0)).astype(FULL),
         "upper": (jnp.arange(SIDE * 128) % 128 >= HEAD_DIM).astype(FULL),
     }
 
-    hidden, kept_heads_first = forward_attention(sequence, normed_all, spots, vectors[0], bias_heads_first, *heads_first)
+    hidden, kept_heads_first, grad_last_all = forward_attention(
+        sequence, normed_all, spots, vectors[0], bias_heads_first, *heads_first, grad_last_all
+    )
     units_first = join_units(0, units_first)
-    hidden, grad_last_all = tie(hidden, gather_z(grad_last_all))
     middle, kept_units_first = forward_hidden_units(hidden, vectors[0], bias_up_first, *units_first)
     mine = jnp.stack(reorder(heads_last))
     middle, mine, theirs = tie(middle, mine, swap(mine))
     heads_last, bias_heads_last, bias_up_last = join_heads(1, mine, theirs)
     middle = middle.astype(LOW).astype(FULL)
     normed_all = gather_z(layer_norm(middle, *vectors[1][0:2]).astype(LOW))
-    hidden, kept_heads_last = forward_attention(
+    hidden, kept_heads_last, _ = forward_attention(
         middle, normed_all, spots, vectors[1], bias_heads_last, *heads_last
     )
     units_last = join_units(1, units_last)
@@ -593,7 +639,6 @@
     packs = [
         jnp.concatenate(
             [
-                halves[d],
                 common,
                 jnp.pad(split[d], ((0, 0), (0, model_width - 512))),
                 jnp.zeros((9, model_width), LOW),
@@ -602,13 +647,13 @@
         )
         for d in range(SIDE)
     ]
-    pack = even_sum(even_pairs(packs, move_x).astype(LOW), move_y)
+    pack = jnp.concatenate([even_pairs(halves, move_x), even_pairs(packs, move_x)], axis=0)
+    pack = even_sum(pack.astype(LOW), move_y)
     pack, units_sum_first, units_sum_last, heads_sum_last = tie(
         pack, units_sum_first, units_sum_last, heads_sum_last
     )
     heads_sum_first, pack = pack[:128], pack[128:]
-    _, norm_one_pull = jax.vjp(lambda rows: layer_norm(rows, gain_one, bias_one), residual)
-    grad_first = grad_hidden + norm_one_pull(chunks[:row_count])[0]
+    grad_first = grad_hidden + layer_norm_back(chunks[:row_count], residual, gain_one)[0]
 
     passed = swap(owner(0, result, grad_first))
     kept = owner(0, grad_first, result)

time: 505 us -> 503 us (level)
  waiting for transfers between devices: 191 us -> 200 us
  other arithmetic: 57.3 us -> 49.6 us
  Pallas kernels: 25.5 us -> 19.1 us
  starting transfers between devices: 138 us -> 144 us
    ppermute x30 -> x33, waiting for transfers between devices: 61.8 us -> 69.6 us  [move_x(): return lax.ppermute(block, 'tensor', route)]
    broadcast_in_dim x0 -> x6, local copies, waits for them, and re-layouts: none -> 5.53 us  [the longest x3 3.08 us: layer_norm_back(): jnp.sum(grad * unit, axis=0, keepdims=True)]
    ppermute x30 -> x33, starting transfers between devices: 44.2 us -> 48.9 us  [move_x(): return lax.ppermute(block, 'tensor', route)]
  transfers between devices with their start and end apart: 115 -> 118, of which waited for: 74 -> 70; matrix products, arithmetic and copies ran while one was open for 21% -> 20% of each run, Pallas kernels for 4% -> 3%
where the time goes in v4:
time: 503 us; the launch traced here: 496 us
  waiting for transfers between devices  200 us (40%)
  starting transfers between devices  144 us (29%)
  other arithmetic  49.6 us (10%)
  matrix products  35.9 us (7%)
  local copies, waits for them, and re-layouts  31.3 us (6%)
  Pallas kernels  19.1 us (4%)
  between operations  16.7 us (3%)
    ppermute x48, waiting for transfers between devices, move_z(): return lax.ppermute(block, 'tensor', route)  73.4 us
    ppermute x33, waiting for transfers between devices, move_x(): return lax.ppermute(block, 'tensor', route)  69.6 us
    ppermute x48, starting transfers between devices, move_z(): return lax.ppermute(block, 'tensor', route)  56.9 us
    ppermute x33, starting transfers between devices, move_x(): return lax.ppermute(block, 'tensor', route)  48.9 us
    ppermute x12, waiting for transfers between devices, move_y_open(): return lax.ppermute(block, 'ctx', route)  33.4 us
    ppermute x12, starting transfers between devices, move_y_open(): return lax.ppermute(block, 'ctx', route)  32.1 us
    dot_general x8, matrix products, local_dot(): return jnp.dot(left, right, preferred_element_type=FULL)  14.3 us
    pallas_call x2, Pallas kernels, attend_back(): pl.pallas_call(attend_back_kernel, out_shape=[jax.ShapeDtypeStruct((rows,...  11.9 us
  transfers between devices with their start and end apart: 118, of which 70 were waited for; matrix products, arithmetic and copies ran while one was open for 20% of the time, Pallas kernels for 3%

profile of v4, /device:TPU:0, one launch (start us, length us, event | category | flops | bytes accessed | tf_op | source)
XLA Modules:
  0.0 496.3 jit_solution(13670883201945328278)
XLA Ops:
  17.4 4.1 collective-permute-start.4
  32.5 5.8 %collective-permute-done.7 = bf16[144,1024]{1,0:T(8,128)(2,1)S(1)} collective-permute-done((bf16[144,1024]{1,0:T(8,128)(2,1)S(1)}, bf16[144,1024]{1,0:T(8,128)(2,1)S(1)}, u32[]{:S(2)}, u32[]{:S(2)}) %collective-permute-start.7) | collective-permute-done | bytes 294944 | tf_op jit(solution)/shard_map/ppermute | solution.py:33
  39.2 4.9 collective-permute-done.5
  55.6 5.1 %collective-permute-done.12 = bf16[256,256]{1,0:T(8,128)(2,1)S(1)} collective-permute-done((bf16[256,256]{1,0:T(8,128)(2,1)S(1)}, bf16[256,256]{1,0:T(8,128)(2,1)S(1)}, u32[]{:S(2)}, u32[]{:S(2)}) %collective-permute-start.12) | collective-permute-done | bytes 131104 | tf_op jit(solution)/shard_map/ppermute | solution.py:33
  63.4 4.5 collective-permute-start.18
  68.9 5.2 %collective-permute-start.15 = (bf16[1024,128]{1,0:T(8,128)(2,1)S(1)}, bf16[1024,128]{1,0:T(8,128)(2,1)S(1)}, u32[]{:S(2)}, u32[]{:S(2)}) collective-permute-start(bf16[1024,128]{1,0:T(8,128)(2,1)S(1)} %slice.437), channel_id=1, source_target_pairs={{0,3},{4,7},{8,11},{12,15},{16,19},{20,23},{24,27},{28,31},{32,35}... | collective-permute-start | bytes 786440 | tf_op jit(solution)/shard_map/ppermute | solution.py:42
  110.0 3.9 collective-permute-done.24
  155.0 5.8 %collective-permute-done.38 = bf16[256,256]{1,0:T(8,128)(2,1)S(1)} collective-permute-done((bf16[256,256]{1,0:T(8,128)(2,1)S(1)}, bf16[256,256]{1,0:T(8,128)(2,1)S(1)}, u32[]{:S(2)}, u32[]{:S(2)}) %collective-permute-start.38) | collective-permute-done | bytes 131104 | tf_op jit(solution)/shard_map/ppermute | solution.py:33
  160.8 5.3 %collective-permute-done.37 = bf16[256,256]{1,0:T(8,128)(2,1)S(1)} collective-permute-done((bf16[256,256]{1,0:T(8,128)(2,1)S(1)}, bf16[256,256]{1,0:T(8,128)(2,1)S(1)}, u32[]{:S(2)}, u32[]{:S(2)}) %collective-permute-start.37) | collective-permute-done | bytes 131104 | tf_op jit(solution)/shard_map/ppermute | solution.py:33
  166.8 10.8 %collective-permute-start.41 = (bf16[1024,128]{1,0:T(8,128)(2,1)}, bf16[1024,128]{1,0:T(8,128)(2,1)S(1)}, u32[]{:S(2)}, u32[]{:S(2)}) collective-permute-start(bf16[1024,128]{1,0:T(8,128)(2,1)} %slice.585), channel_id=1, source_target_pairs={{0,3},{4,7},{8,11},{12,15},{16,19},{20,23},{24,27},{28,31},{32,35}... | collective-permute-start | bytes 786440 | tf_op jit(solution)/shard_map/ppermute | solution.py:42
  202.6 5.3 %collective-permute-done.47 = bf16[64,1024]{1,0:T(8,128)(2,1)S(1)} collective-permute-done((bf16[64,1024]{1,0:T(8,128)(2,1)S(1)}, bf16[64,1024]{1,0:T(8,128)(2,1)S(1)}, u32[]{:S(2)}, u32[]{:S(2)}) %collective-permute-start.47) | collective-permute-done | bytes 131104 | tf_op jit(solution)/shard_map/ppermute | solution.py:26
  230.0 3.9 collective-permute-done.54
  254.1 6.3 %attend_back.2 = (bf16[1024,128]{1,0:T(8,128)(2,1)S(1)}, bf16[1024,128]{1,0:T(8,128)(2,1)S(1)}, bf16[1024,128]{1,0:T(8,128)(2,1)}, bf16[1024,128]{1,0:T(8,128)(2,1)}, bf16[1024,128]{1,0:T(8,128)(2,1)}) custom-call(s32[5]{0:T(128)S(1)} %stack.94.scalar_ref, bf16[1024,256]{1,0:T(8,128)(2,1)S(1)} %pad_maximum_fusion.10.own_ref, ...), custom_call_target="tpu_custom_call" | custom-call | flops 2684354560 | bytes 6291456 | tf_op jit(solution)/shard_map/attend_back/pallas_call | solution.py:331
  266.7 7.5 %collective-permute-done.62 = bf16[1024,128]{1,0:T(8,128)(2,1)S(1)} collective-permute-done((bf16[1024,128]{1,0:T(8,128)(2,1)}, bf16[1024,128]{1,0:T(8,128)(2,1)S(1)}, u32[]{:S(2)}, u32[]{:S(2)}) %collective-permute-start.62) | collective-permute-done | bytes 262176 | tf_op jit(solution)/shard_map/ppermute | solution.py:42
  274.2 9.3 %collective-permute-done.63 = bf16[1024,128]{1,0:T(8,128)(2,1)S(1)} collective-permute-done((bf16[1024,128]{1,0:T(8,128)(2,1)}, bf16[1024,128]{1,0:T(8,128)(2,1)S(1)}, u32[]{:S(2)}, u32[]{:S(2)}) %collective-permute-start.63) | collective-permute-done | bytes 262176 | tf_op jit(solution)/shard_map/ppermute | solution.py:42
  283.5 5.5 %collective-permute-done.64 = bf16[1024,128]{1,0:T(8,128)(2,1)S(1)} collective-permute-done((bf16[1024,128]{1,0:T(8,128)(2,1)}, bf16[1024,128]{1,0:T(8,128)(2,1)S(1)}, u32[]{:S(2)}, u32[]{:S(2)}) %collective-permute-start.64) | collective-permute-done | bytes 262176 | tf_op jit(solution)/shard_map/ppermute | solution.py:42
  294.4 6.3 %collective-permute-done.65 = bf16[256,256]{1,0:T(8,128)(2,1)S(1)} collective-permute-done((bf16[256,256]{1,0:T(8,128)(2,1)S(1)}, bf16[256,256]{1,0:T(8,128)(2,1)S(1)}, u32[]{:S(2)}, u32[]{:S(2)}) %collective-permute-start.65) | collective-permute-done | bytes 131104 | tf_op jit(solution)/shard_map/ppermute | solution.py:33
  342.5 3.9 collective-permute-done.77
  347.4 4.6 add_convert_fusion
  376.9 5.5 %attend_back.3 = (bf16[1024,128]{1,0:T(8,128)(2,1)S(1)}, bf16[1024,128]{1,0:T(8,128)(2,1)S(1)}, bf16[1024,128]{1,0:T(8,128)(2,1)S(1)}, bf16[1024,128]{1,0:T(8,128)(2,1)S(1)}, bf16[1024,128]{1,0:T(8,128)(2,1)S(1)}) custom-call(s32[5]{0:T(128)S(1)} %stack.94.scalar_ref, bf16[1024,256]{1,0:T(8,128)(2,1)S(1)} %pad_maximum_fusion.6.own_ref, ...), custom_call_target="tpu_custom_call" | custom-call | flops 2684354560 | bytes 6291456 | tf_op jit(solution)/shard_map/attend_back/pallas_call | solution.py:331
  382.4 7.1 %reduce-scatter.6.cloned.1.call-done = bf16[256,1024]{1,0:T(8,128)(2,1)} async-done(((bf16[1024,1024]{1,0:T(8,128)(2,1)}), bf16[256,1024]{1,0:T(8,128)(2,1)}) %reduce-scatter.6.cloned.1.call-update) | async-done | bytes 524304 | tf_op jit(solution)/shard_map/reduce_scatter | solution.py:563
  403.6 4.4 collective-permute-done.87
  456.6 4.0 collective-permute-done.99
  468.0 10.8 %collective-permute-done.107 = bf16[144,1024]{1,0:T(8,128)(2,1)S(1)} collective-permute-done((bf16[144,1024]{1,0:T(8,128)(2,1)S(1)}, bf16[144,1024]{1,0:T(8,128)(2,1)S(1)}, u32[]{:S(2)}, u32[]{:S(2)}) %collective-permute-start.107) | collective-permute-done | bytes 294944 | tf_op jit(solution)/shard_map/ppermute | solution.py:37
  (658 shorter events, 339.5 us)
Async XLA Ops:
  7.2 80.3 %all-gather.4.cloned.1.call-start = ((), (), s32[]{:S(2)}) async-start(), calls=%async_computation.3 | async-start | bytes 2621440 | tf_op jit(solution)/shard_map/all_gather | solution.py:509
  10.9 20.5 %collective-permute-start.8 = (bf16[256,1024]{1,0:T(8,128)(2,1)}, bf16[256,1024]{1,0:T(8,128)(2,1)S(1)}, u32[]{:S(2)}, u32[]{:S(2)}) collective-permute-start(bf16[256,1024]{1,0:T(8,128)(2,1)} %bitcast.246), channel_id=1, source_target_pairs={{0,64},{64,0},{1,65},{65,1},{2,66},{66,2},{3,67},{67,3},{4,68},{68... | collective-permute-start | bytes 1572872 | tf_op jit(solution)/shard_map/ppermute | solution.py:62
  23.1 15.2 %collective-permute-start.7 = (bf16[144,1024]{1,0:T(8,128)(2,1)S(1)}, bf16[144,1024]{1,0:T(8,128)(2,1)S(1)}, u32[]{:S(2)}, u32[]{:S(2)}) collective-permute-start(bf16[144,1024]{1,0:T(8,128)(2,1)S(1)} %get-tuple-element.59), channel_id=1, source_target_pairs={{0,48},{4,52},{8,56},{12,60},{16,0},{20,4},{24,8},{28,12},{32,16},... | collective-permute-start | bytes 884744 | tf_op jit(solution)/shard_map/ppermute | solution.py:33
  44.3 64.4 %all-gather.6.cloned.1.call-start = ((), (), s32[]{:S(2)}) async-start(), calls=%async_computation.4 | async-start | bytes 1474560 | tf_op jit(solution)/shard_map/all_gather | solution.py:509
  55.6 126.1 %all-gather.8.cloned.1.call-start = ((), (), s32[]{:S(2)}) async-start(), calls=%async_computation.5 | async-start | bytes 2621440 | tf_op jit(solution)/shard_map/all_gather | solution.py:509
  87.5 36.7 %collective-permute-start.28 = (bf16[1024,1024]{1,0:T(8,128)(2,1)}, bf16[1024,1024]{1,0:T(8,128)(2,1)}, u32[]{:S(2)}, u32[]{:S(2)}) collective-permute-start(bf16[1024,1024]{1,0:T(8,128)(2,1)} %all-gather.4.cloned.1.call-done), channel_id=1, source_target_pairs={{0,64},{64,0},{1,65},{65,1},{2,66},{66,2},{3,67},{67,3},{4,68},{68... | collective-permute-start | bytes 6291464 | tf_op jit(solution)/shard_map/ppermute | solution.py:62
  119.8 18.9 %collective-permute-start.32 = (bf16[4,144,1024]{2,1,0:T(8,128)(2,1)}, bf16[4,144,1024]{2,1,0:T(8,128)(2,1)}, u32[]{:S(2)}, u32[]{:S(2)}) collective-permute-start(bf16[4,144,1024]{2,1,0:T(8,128)(2,1)} %pad_maximum_fusion.3), channel_id=1, source_target_pairs={{0,64},{64,0},{1,65},{65,1},{2,66},{66,2},{3,67},{67,3},{4,68},{68... | collective-permute-start | bytes 3538952 | tf_op jit(solution)/shard_map/ppermute | solution.py:62
  132.5 214.9 %reduce-scatter.4.cloned.1.call-start = ((), (), s32[]{:S(2)}) async-start(), calls=%async_computation.6 | async-start | bytes 2621440 | tf_op jit(solution)/shard_map/reduce_scatter | solution.py:563
  152.0 14.1 %collective-permute-start.37 = (bf16[256,256]{1,0:T(8,128)(2,1)S(1)}, bf16[256,256]{1,0:T(8,128)(2,1)S(1)}, u32[]{:S(2)}, u32[]{:S(2)}) collective-permute-start(bf16[256,256]{1,0:T(8,128)(2,1)S(1)} %get-tuple-element.232), channel_id=1, source_target_pairs={{0,32},{4,36},{8,40},{12,44},{16,48},{20,52},{24,56},{28,60},{32,0... | collective-permute-start | bytes 393224 | tf_op jit(solution)/shard_map/ppermute | solution.py:33
  166.8 18.0 %collective-permute-start.41 = (bf16[1024,128]{1,0:T(8,128)(2,1)}, bf16[1024,128]{1,0:T(8,128)(2,1)S(1)}, u32[]{:S(2)}, u32[]{:S(2)}) collective-permute-start(bf16[1024,128]{1,0:T(8,128)(2,1)} %slice.585), channel_id=1, source_target_pairs={{0,3},{4,7},{8,11},{12,15},{16,19},{20,23},{24,27},{28,31},{32,35}... | collective-permute-start | bytes 786440 | tf_op jit(solution)/shard_map/ppermute | solution.py:42
  181.7 29.8 %collective-permute-start.48 = (bf16[1024,1024]{1,0:T(8,128)(2,1)}, bf16[1024,1024]{1,0:T(8,128)(2,1)S(1)}, u32[]{:S(2)}, u32[]{:S(2)}) collective-permute-start(bf16[1024,1024]{1,0:T(8,128)(2,1)} %all-gather.8.cloned.1.call-done), channel_id=1, source_target_pairs={{0,64},{64,0},{1,65},{65,1},{2,66},{66,2},{3,67},{67,3},{4,68},{68... | collective-permute-start | bytes 6291464 | tf_op jit(solution)/shard_map/ppermute | solution.py:62
  261.7 21.8 %collective-permute-start.63 = (bf16[1024,128]{1,0:T(8,128)(2,1)}, bf16[1024,128]{1,0:T(8,128)(2,1)S(1)}, u32[]{:S(2)}, u32[]{:S(2)}) collective-permute-start(bf16[1024,128]{1,0:T(8,128)(2,1)} %get-tuple-element.75), channel_id=1, source_target_pairs={{2,0},{3,1},{6,4},{7,5},{10,8},{11,9},{14,12},{15,13},{18,16},{19,... | collective-permute-start | bytes 786440 | tf_op jit(solution)/shard_map/ppermute | solution.py:42
  263.0 26.0 %collective-permute-start.64 = (bf16[1024,128]{1,0:T(8,128)(2,1)}, bf16[1024,128]{1,0:T(8,128)(2,1)S(1)}, u32[]{:S(2)}, u32[]{:S(2)}) collective-permute-start(bf16[1024,128]{1,0:T(8,128)(2,1)} %get-tuple-element.76), channel_id=1, source_target_pairs={{3,0},{7,4},{11,8},{15,12},{19,16},{23,20},{27,24},{31,28},{35,32}... | collective-permute-start | bytes 786440 | tf_op jit(solution)/shard_map/ppermute | solution.py:42
  266.6 115.8 %reduce-scatter.8.cloned.1.call-start = ((), (), s32[]{:S(2)}) async-start(), calls=%async_computation.8 | async-start | bytes 1310720 | tf_op jit(solution)/shard_map/reduce_scatter | solution.py:563
  308.3 16.2 %collective-permute-start.74 = (bf16[4,128,1024]{2,1,0:T(8,128)(2,1)S(1)}, bf16[4,128,1024]{2,1,0:T(8,128)(2,1)S(1)}, u32[]{:S(2)}, u32[]{:S(2)}) collective-permute-start(bf16[4,128,1024]{2,1,0:T(8,128)(2,1)S(1)} %get-tuple-element.171), channel_id=1, source_target_pairs={{0,64},{64,0},{1,65},{65,1},{2,66},{66,2},{3,67},{67,3},{4,68},{68... | collective-permute-start | bytes 3145736 | tf_op jit(solution)/shard_map/ppermute | solution.py:62
  332.1 15.3 %collective-permute-start.78 = (bf16[1024,1024]{1,0:T(8,128)(2,1)}, bf16[1024,1024]{1,0:T(8,128)(2,1)}, u32[]{:S(2)}, u32[]{:S(2)}) collective-permute-start(bf16[1024,1024]{1,0:T(8,128)(2,1)} %get-tuple-element.167), channel_id=1, source_target_pairs={{0,64},{64,0},{1,65},{65,1},{2,66},{66,2},{3,67},{67,3},{4,68},{68... | collective-permute-start | bytes 6291464 | tf_op jit(solution)/shard_map/ppermute | solution.py:62
  333.7 55.8 %reduce-scatter.6.cloned.1.call-start = ((), (), s32[]{:S(2)}) async-start(), calls=%async_computation.7 | async-start | bytes 2621440 | tf_op jit(solution)/shard_map/reduce_scatter | solution.py:563
  352.0 127.7 %all-reduce.8.cloned.1.call-start = ((), (), s32[]{:S(2)}) async-start(), calls=%async_computation.9 | async-start | bytes 2621440 | tf_op jit(solution)/shard_map/psum | solution.py:614
  371.6 67.3 %collective-permute-start.94 = (bf16[64,1024]{1,0:T(8,128)(2,1)}, bf16[64,1024]{1,0:T(8,128)(2,1)}, u32[]{:S(2)}, u32[]{:S(2)}) collective-permute-start(bf16[64,1024]{1,0:T(8,128)(2,1)} %get-tuple-element.203), channel_id=1, source_target_pairs={{0,12},{4,0},{8,4},{12,8},{16,28},{20,16},{24,20},{28,24},{32,44},... | collective-permute-start | bytes 393224 | tf_op jit(solution)/shard_map/ppermute | solution.py:26
  372.2 66.6 %collective-permute-start.96 = (bf16[64,1024]{1,0:T(8,128)(2,1)}, bf16[64,1024]{1,0:T(8,128)(2,1)}, u32[]{:S(2)}, u32[]{:S(2)}) collective-permute-start(bf16[64,1024]{1,0:T(8,128)(2,1)} %get-tuple-element.204), channel_id=1, source_target_pairs={{0,4},{4,8},{8,12},{12,0},{16,20},{20,24},{24,28},{28,16},{32,36},... | collective-permute-start | bytes 393224 | tf_op jit(solution)/shard_map/ppermute | solution.py:26
  392.2 15.9 %collective-permute-start.87 = (bf16[1024,128]{1,0:T(8,128)(2,1)S(1)}, bf16[1024,128]{1,0:T(8,128)(2,1)S(1)}, u32[]{:S(2)}, u32[]{:S(2)}) collective-permute-start(bf16[1024,128]{1,0:T(8,128)(2,1)S(1)} %get-tuple-element.94), channel_id=1, source_target_pairs={{3,0},{7,4},{11,8},{15,12},{19,16},{23,20},{27,24},{31,28},{35,32}... | collective-permute-start | bytes 786440 | tf_op jit(solution)/shard_map/ppermute | solution.py:42
  463.9 15.0 %collective-permute-start.107 = (bf16[144,1024]{1,0:T(8,128)(2,1)S(1)}, bf16[144,1024]{1,0:T(8,128)(2,1)S(1)}, u32[]{:S(2)}, u32[]{:S(2)}) collective-permute-start(bf16[144,1024]{1,0:T(8,128)(2,1)S(1)} %pad_maximum_fusion.17), channel_id=1, source_target_pairs={{0,1},{1,2},{2,3},{3,0},{4,5},{5,6},{6,7},{7,4},{8,9},{9,10},{10,1... | collective-permute-start | bytes 884744 | tf_op jit(solution)/shard_map/ppermute | solution.py:37
  464.0 14.9 %collective-permute-start.106 = (bf16[144,1024]{1,0:T(8,128)(2,1)S(1)}, bf16[144,1024]{1,0:T(8,128)(2,1)S(1)}, u32[]{:S(2)}, u32[]{:S(2)}) collective-permute-start(bf16[144,1024]{1,0:T(8,128)(2,1)S(1)} %pad_maximum_fusion.17), channel_id=1, source_target_pairs={{0,2},{1,3},{2,0},{3,1},{4,6},{5,7},{6,4},{7,5},{8,10},{9,11},{10,... | collective-permute-start | bytes 884744 | tf_op jit(solution)/shard_map/ppermute | solution.py:37
  465.5 14.0 %collective-permute-start.108 = (bf16[144,1024]{1,0:T(8,128)(2,1)S(1)}, bf16[144,1024]{1,0:T(8,128)(2,1)S(1)}, u32[]{:S(2)}, u32[]{:S(2)}) collective-permute-start(bf16[144,1024]{1,0:T(8,128)(2,1)S(1)} %pad_maximum_fusion.17), channel_id=1, source_target_pairs={{0,3},{1,0},{2,1},{3,2},{4,7},{5,4},{6,5},{7,6},{8,11},{9,8},{10,9... | collective-permute-start | bytes 884744 | tf_op jit(solution)/shard_map/ppermute | solution.py:37
  (209 other events, 1769.6 us)
Sparse Core Ops, SparseCore 0:
  44.4 33.0 all-gather.3
  79.8 28.8 all-gather.5
  132.6 40.7 all-gather.7
  266.7 48.0 reduce-scatter.3
  333.8 21.2 reduce-scatter.7
  357.4 32.1 reduce-scatter.5
  414.4 46.5 all-reduce.7

commit v5 on v4

--- a/solution.py
+++ b/solution.py
@@ -97,6 +97,13 @@
     return center * lax.rsqrt(spread + EPSILON) * gain + bias
 
 
+def column_sum(rows):
+    ones = jnp.ones((8, rows.shape[0]), rows.dtype)
+    return jnp.dot(
+        ones, rows, precision=lax.Precision.HIGHEST, preferred_element_type=FULL
+    )[0:1]
+
+
 def layer_norm_back(grad, values, gain):
     center = values - jnp.mean(values, axis=-1, keepdims=True)
     scale = lax.rsqrt(jnp.mean(center * center, axis=-1, keepdims=True) + EPSILON)
@@ -107,7 +114,7 @@
         - jnp.mean(part, axis=-1, keepdims=True)
         - unit * jnp.mean(part * unit, axis=-1, keepdims=True)
     )
-    return back, jnp.sum(grad * unit, axis=0, keepdims=True), jnp.sum(grad, axis=0, keepdims=True)
+    return back, column_sum(grad * unit), column_sum(grad)
 
 
 def local_dot(left, right):
@@ -140,14 +147,14 @@
     return jnp.where(place >= start_two, start_two, jnp.where(place >= start_one, start_one, 0))
 
 
-def tile_bounds(scalar_ref, pair, rows_all):
+def tile_bounds(scalar_ref, indices, rows_all):
     block, x_here, _, start_one, start_two = [scalar_ref[i] for i in range(5)]
     least, most = [], []
-    for part in range(2):
-        place = block * rows_all + ((x_here + pair * 2 + part) & 3) * TILE
+    for index in indices:
+        place = block * rows_all + ((x_here + index) & 3) * TILE
         least.append(first_of_document(place, start_one, start_two))
         most.append(first_of_document(place + TILE - 1, start_one, start_two))
-    return jnp.minimum(*least), jnp.maximum(*most)
+    return functools.reduce(jnp.minimum, least), functools.reduce(jnp.maximum, most)
 
 
 def tile_limits(scalar_ref, index, rows_all):
@@ -181,8 +188,8 @@
 
         @pl.loop(0, tiles // 2)
         def _(pair, d=d, start=start):
-            least, most = tile_bounds(scalar_ref, pair, rows_all)
             indices = [pair * 2, pair * 2 + 1]
+            least, most = tile_bounds(scalar_ref, indices, rows_all)
 
             def step(masked):
                 key_values = own_ref[:, 0:128] if d == 0 else held[d - 1]
@@ -257,10 +264,10 @@
             start = (block - d) * rows_all
             key_sum[...] = jnp.zeros_like(key_sum)
 
-            @pl.loop(0, tiles // 2)
-            def _(pair):
-                least, most = tile_bounds(scalar_ref, pair, rows_all)
-                indices = [pair * 2, pair * 2 + 1]
+            @pl.loop(0, tiles)
+            def _(index):
+                indices = [index]
+                least, most = tile_bounds(scalar_ref, indices, rows_all)
 
                 def step(masked):
                     key_values = own_ref[:, 0:128] if d == 0 else held[d - 1]
@@ -356,18 +363,14 @@
 X_GROUPS = [[x * SIDE + z for x in range(SIDE)] for z in range(SIDE)]
 
 
-def forward_attention(residual, normed_all, spots, vectors, bias_qkv, w_heads, w_back, early=None):
+def forward_attention(residual, normed_all, spots, vectors, bias_qkv, w_heads, w_back):
     b_out = vectors[2]
     projected = ((nt_dot(normed_all, w_heads) + bias_qkv) * spots["scale"]).astype(LOW)
     width = projected.shape[1] // SIDE
     pieces = [projected[:, d * width : (d + 1) * width] for d in range(SIDE)]
     own = jnp.concatenate([pieces[0]] + [move_x(pieces[d], -d) for d in range(1, SIDE)], axis=0)
-    if early is not None:
-        own, early = tie(own, early)
     others = [move_y_open(own[:, 0:128], d) for d in range(1, SIDE)]
     kept = attend(spots, own, others)
-    if early is not None:
-        kept, early = tie(kept, gather_z(early))
     lanes = lax.broadcasted_iota(jnp.int32, kept.shape, 1)
     mixed = jnp.where(lanes < HEAD_DIM, 0.0, kept).astype(LOW)
     rows = mixed.shape[0] // SIDE
@@ -375,7 +378,7 @@
         [mixed[0:rows]] + [move_x(mixed[d * rows : (d + 1) * rows], d) for d in range(1, SIDE)], axis=1
     )
     hidden = residual + (scatter_z(local_dot(mixed_rows, w_back).astype(LOW)) + b_out)
-    return hidden, (residual, normed_all, own, others, kept, mixed_rows), early
+    return hidden, (residual, normed_all, own, others, kept, mixed_rows)
 
 
 def forward_hidden_units(hidden, vectors, b_up, w_up, w_down):
@@ -391,7 +394,7 @@
     hidden, normed_two_all, up_value, activated = stored
     gain_two = vectors[3]
     grad_down = grad_out.astype(LOW)
-    g_b_down = jnp.sum(grad_down.astype(FULL), axis=0, keepdims=True)
+    g_b_down = column_sum(grad_down)
     _, gelu_pull = jax.vjp(jax.nn.gelu, up_value)
     (grad_up,) = gelu_pull(nt_dot(grad_down_all, w_down))
     grad_up = grad_up.astype(LOW)
@@ -404,31 +407,34 @@
     return grad_hidden, (g_gain_two, g_bias_two, g_b_down), g_b_up, g_w_up, g_w_down
 
 
-def backward_mixed(grad_hidden, stored, w_back, spots):
+def backward_mixed(grad_hidden, stored, w_back, spots, side):
     mixed_rows = stored[5]
     grad_attn = grad_hidden.astype(LOW)
-    g_b_out = jnp.sum(grad_attn.astype(FULL), axis=0, keepdims=True)
-    grad_attn_all = gather_z(grad_attn)
+    g_b_out = column_sum(grad_attn)
+    grad_attn_all, side = tie(gather_z(grad_attn), side)
     grad_mixed = (nt_dot(grad_attn_all, w_back) * spots["upper"]).astype(LOW)
     pieces = [grad_mixed[:, d * 128 : (d + 1) * 128] for d in range(SIDE)]
     grad_own = jnp.concatenate(
         [pieces[0]] + [move_x(pieces[d], -d) for d in range(1, SIDE)], axis=0
     )
     g_w_out = tn_dot(mixed_rows, grad_attn_all).astype(LOW)
-    return grad_own, g_b_out, g_w_out
-
-
-def backward_heads(parts):
+    return grad_own, g_b_out, g_w_out, side
+
+
+def backward_heads(parts, *side):
     dq, dkv0, dkv1, dkv2, dkv3 = parts
     dkv = dkv0.astype(FULL)
     for d, part in enumerate((dkv1, dkv2, dkv3), 1):
         dkv = dkv + move_y_open(part, -d).astype(FULL)
     grad_own = jnp.concatenate([dkv.astype(LOW), dq], axis=1)
+    if side:
+        grad_own, *side = tie(grad_own, *side)
     rows = grad_own.shape[0] // SIDE
-    return jnp.concatenate(
+    grad_qkv = jnp.concatenate(
         [grad_own[0:rows]] + [move_x(grad_own[d * rows : (d + 1) * rows], d) for d in range(1, SIDE)],
         axis=1,
     )
+    return (grad_qkv, *side) if side else grad_qkv
 
 
 def backward_entry(grad_qkv, grad_hidden, stored, vectors, w_heads):
@@ -520,7 +526,7 @@
     half, normed = tie(half_heads(0), normed)
     mine = jnp.stack([half] + [move_x(half, d) for d in range(1, SIDE)])
     half = owner(0, up_own, down_other)
-    normed_all, mine, half = tie(gather_z(normed), mine, half)
+    normed_all, mine, half, grad_last_all = tie(gather_z(normed), mine, half, gather_z(grad_last_all))
     heads_first, bias_heads_first, bias_up_first = join_heads(0, mine, swap(mine))
     units_first = gather_whole(half)
     heads_last = gather_whole(half_heads(1)).reshape(SIDE, -1, model_width)
@@ -537,8 +543,8 @@
         "upper": (jnp.arange(SIDE * 128) % 128 >= HEAD_DIM).astype(FULL),
     }
 
-    hidden, kept_heads_first, grad_last_all = forward_attention(
-        sequence, normed_all, spots, vectors[0], bias_heads_first, *heads_first, grad_last_all
+    hidden, kept_heads_first = forward_attention(
+        sequence, normed_all, spots, vectors[0], bias_heads_first, *heads_first
     )
     units_first = join_units(0, units_first)
     middle, kept_units_first = forward_hidden_units(hidden, vectors[0], bias_up_first, *units_first)
@@ -547,14 +553,18 @@
     heads_last, bias_heads_last, bias_up_last = join_heads(1, mine, theirs)
     middle = middle.astype(LOW).astype(FULL)
     normed_all = gather_z(layer_norm(middle, *vectors[1][0:2]).astype(LOW))
-    hidden, kept_heads_last, _ = forward_attention(
+    hidden, kept_heads_last = forward_attention(
         middle, normed_all, spots, vectors[1], bias_heads_last, *heads_last
     )
     units_last = join_units(1, units_last)
     result, kept_units_last = forward_hidden_units(hidden, vectors[1], bias_up_last, *units_last)
 
+    def choose_grads(layer, first, second):
+        return owner(layer, first, second), owner(layer, second, first)
+
     def swap_grads(layer, first, second):
-        return owner(layer, first, second), swap(owner(layer, second, first))
+        kept, payload = choose_grads(layer, first, second)
+        return kept, swap(payload)
 
     def add_grads(kept, arrived):
         return (kept.astype(FULL) + arrived.astype(FULL)).astype(LOW)
@@ -585,42 +595,44 @@
     grad_hidden, vec_units_last, g_b_up_last, g_up, g_down = backward_hidden_units(
         grad_last, grad_last_all, kept_units_last, vectors[1], *units_last
     )
-    grad_hidden, units_kept, units_arrived = tie(grad_hidden, *swap_grads(1, g_up, g_down))
-    units_sum_last = scatter_whole(add_grads(units_kept, units_arrived))
-    grad_mixed, g_b_out_last, g_out = backward_mixed(grad_hidden, kept_heads_last, heads_last[1], spots)
+    units_sum_last = add_grads(*swap_grads(1, g_up, g_down))
+    grad_mixed, g_b_out_last, g_out, units_sum_last = backward_mixed(
+        grad_hidden, kept_heads_last, heads_last[1], spots, units_sum_last
+    )
+    units_sum_last = scatter_whole(units_sum_last)
     grad_qkv = backward_heads(attend_back(spots, *kept_heads_last[2:5], grad_mixed))
+    grad_qkv, units_sum_last = tie(grad_qkv, units_sum_last)
+    units_sum_last = lax.psum(units_sum_last, "ctx")
     grad_middle, vec_heads_last, g_b_qkv_last, g_heads = backward_entry(
         grad_qkv, grad_hidden, kept_heads_last, vectors[1], heads_last[0]
     )
     heads_kept, heads_arrived = swap_grads(1, *split_heads(g_heads, g_out))
 
     grad_middle = grad_middle.astype(LOW).astype(FULL)
-    grad_down_all, heads_kept, heads_arrived = tie(
-        gather_z(grad_middle.astype(LOW)), heads_kept, heads_arrived
-    )
-    heads_sum_last = scatter_whole(
-        jnp.concatenate(reorder(add_grads(heads_kept, heads_arrived)), axis=0)
-    )
+    heads_sum_last = jnp.concatenate(reorder(add_grads(heads_kept, heads_arrived)), axis=0)
+    grad_down_all, heads_sum_last = tie(gather_z(grad_middle.astype(LOW)), heads_sum_last)
+    heads_sum_last = scatter_whole(heads_sum_last)
     grad_hidden, vec_units_first, g_b_up_first, g_up, g_down = backward_hidden_units(
         grad_middle, grad_down_all, kept_units_first, vectors[0], *units_first
     )
-    grad_hidden, units_kept, units_arrived, units_sum_last = tie(
-        grad_hidden, *swap_grads(0, g_up, g_down), units_sum_last
-    )
-    units_sum_first = scatter_whole(add_grads(units_kept, units_arrived))
-    grad_mixed, g_b_out_first, g_out = backward_mixed(grad_hidden, kept_heads_first, heads_first[1], spots)
-    parts = attend_back(spots, *kept_heads_first[2:5], grad_mixed)
-    parts, units_sum_first, heads_sum_last = tie(parts, units_sum_first, heads_sum_last)
-    units_sum_first, units_sum_last, heads_sum_last = lax.psum(
-        (units_sum_first, units_sum_last, heads_sum_last), "ctx"
-    )
-    grad_qkv = backward_heads(parts)
+    units_sum_first = add_grads(*swap_grads(0, g_up, g_down))
+    grad_mixed, g_b_out_first, g_out, (units_sum_first, units_sum_last) = backward_mixed(
+        grad_hidden, kept_heads_first, heads_first[1], spots, (units_sum_first, units_sum_last)
+    )
+    units_sum_first = scatter_whole(units_sum_first)
+    grad_qkv, units_sum_first, heads_sum_last = backward_heads(
+        attend_back(spots, *kept_heads_first[2:5], grad_mixed), units_sum_first, heads_sum_last
+    )
+    units_sum_first, heads_sum_last = lax.psum((units_sum_first, heads_sum_last), "ctx")
 
     gain_one, bias_one = vectors[0][0:2]
     residual, normed_all = kept_heads_first[0:2]
+    heads_kept, payload = choose_grads(0, *split_heads(tn_dot(grad_qkv, normed_all).astype(LOW), g_out))
+    grad_qkv, payload = tie(grad_qkv, payload)
+    halves = add_grads(heads_kept, swap(payload))
     grad_normed = local_dot(grad_qkv, heads_first[0])
-    g_bias_one = jnp.sum(grad_normed, axis=0, keepdims=True)
-    g_gain_one = jnp.sum(grad_normed * ((normed_all.astype(FULL) - bias_one) / gain_one), axis=0, keepdims=True)
+    g_bias_one = column_sum(grad_normed)
+    g_gain_one = column_sum(grad_normed * ((normed_all.astype(FULL) - bias_one) / gain_one))
     g_b_qkv_first = jnp.sum(grad_qkv.astype(FULL), axis=0)
     sums_first = pack_vectors(
         (g_gain_one, g_bias_one), vec_units_first, g_b_out_first, g_b_up_first, g_b_qkv_first
@@ -629,8 +641,6 @@
     common = jnp.pad(jnp.concatenate([sums_first[:6], sums_last[:6]]), ((0, 4), (0, 0))).astype(LOW)
     chunks = grad_normed.astype(LOW).reshape(SIDE, row_count, model_width)
     chunks = even_pairs([jnp.concatenate([chunks[d], common], axis=0) for d in range(SIDE)], move_z)
-    heads_kept, heads_arrived = swap_grads(0, *split_heads(tn_dot(grad_qkv, normed_all).astype(LOW), g_out))
-    halves = add_grads(heads_kept, heads_arrived)
     sums_first = jnp.concatenate([chunks[row_count : row_count + 6], sums_first[6:]])
     sums_last = jnp.concatenate([chunks[row_count + 6 : row_count + 12], sums_last[6:]])
     sums = owner(0, sums_first, sums_last) + swap(owner(0, sums_last, sums_first))

time: 503 us -> 520 us (1.034)
  matrix products: 35.9 us -> 42.2 us
    ppermute x12, waiting for transfers between devices: 33.4 us -> 45.1 us  [move_y_open(): return lax.ppermute(block, 'ctx', route)]
    broadcast_in_dim x12 -> x0, local copies, waits for them, and re-layouts: 9.27 us -> none  [the longest x3 3.08 us: layer_norm_back(): jnp.sum(grad * unit, axis=0, keepdims=True)]
    dot_general x0 -> x12, matrix products: none -> 7.39 us  [column_sum(): jnp.dot(ones, rows, precision=lax.Precision.HIGHEST, preferred_element_ty...]
    reduce_scatter x3, waiting for transfers between devices: 7.17 us -> 0.06 us  [scatter_whole(): lax.psum_scatter(grads, 'tensor', scatter_dimension=0, tiled=True, axis_i...]
    slice x0 -> x13, local copies, waits for them, and re-layouts: none -> 6.77 us  [the longest x12 6.04 us: column_sum(): jnp.dot(ones, rows, precision=lax.Precision.HIGHEST, preferred_element_ty...]
    unnamed x236 -> x260, local copies, waits for them, and re-layouts: 6.24 us -> 11.4 us
  transfers between devices with their start and end apart: 118 -> 119, of which waited for: 70 -> 76; matrix products, arithmetic and copies ran while one was open for 20% -> 20% of each run, Pallas kernels for 3% -> 4%
where the time goes in v5:
time: 520 us; the launch traced here: 511 us
  waiting for transfers between devices  204 us (39%)
  starting transfers between devices  143 us (28%)
  other arithmetic  54.3 us (10%)
  matrix products  42.2 us (8%)
  local copies, waits for them, and re-layouts  32.5 us (6%)
  Pallas kernels  18.7 us (4%)
  between operations  17.2 us (3%)
    ppermute x48, waiting for transfers between devices, move_z(): return lax.ppermute(block, 'tensor', route)  77.2 us
    ppermute x33, waiting for transfers between devices, move_x(): return lax.ppermute(block, 'tensor', route)  65.5 us
    ppermute x48, starting transfers between devices, move_z(): return lax.ppermute(block, 'tensor', route)  57.6 us
    ppermute x33, starting transfers between devices, move_x(): return lax.ppermute(block, 'tensor', route)  47 us
    ppermute x12, waiting for transfers between devices, move_y_open(): return lax.ppermute(block, 'ctx', route)  45.1 us
    ppermute x12, starting transfers between devices, move_y_open(): return lax.ppermute(block, 'ctx', route)  30.9 us
    dot_general x8, matrix products, local_dot(): return jnp.dot(left, right, preferred_element_type=FULL)  13.2 us
    dot_general x8, matrix products, nt_dot(): lax.dot_general(left, right, (((1,), (1,)), ((), ())), preferred_element_...  12.7 us
  transfers between devices with their start and end apart: 119, of which 76 were waited for; matrix products, arithmetic and copies ran while one was open for 20% of the time, Pallas kernels for 4%

profile of v5, /device:TPU:0, one launch (start us, length us, event | category | flops | bytes accessed | tf_op | source)
XLA Modules:
  0.0 511.5 jit_solution(12853328854625815438)
XLA Ops:
  8.2 4.2 collective-permute-start.11
  37.1 6.7 %collective-permute-done.7 = bf16[144,1024]{1,0:T(8,128)(2,1)S(1)} collective-permute-done((bf16[144,1024]{1,0:T(8,128)(2,1)S(1)}, bf16[144,1024]{1,0:T(8,128)(2,1)S(1)}, u32[]{:S(2)}, u32[]{:S(2)}) %collective-permute-start.7) | collective-permute-done | bytes 294944 | tf_op jit(solution)/shard_map/ppermute | solution.py:33
  57.0 6.9 %collective-permute-done.15 = bf16[256,256]{1,0:T(8,128)(2,1)S(1)} collective-permute-done((bf16[256,256]{1,0:T(8,128)(2,1)S(1)}, bf16[256,256]{1,0:T(8,128)(2,1)S(1)}, u32[]{:S(2)}, u32[]{:S(2)}) %collective-permute-start.15) | collective-permute-done | bytes 131104 | tf_op jit(solution)/shard_map/ppermute | solution.py:33
  66.4 5.2 %collective-permute-start.18 = (bf16[1024,128]{1,0:T(8,128)(2,1)S(1)}, bf16[1024,128]{1,0:T(8,128)(2,1)S(1)}, u32[]{:S(2)}, u32[]{:S(2)}) collective-permute-start(bf16[1024,128]{1,0:T(8,128)(2,1)S(1)} %slice.617), channel_id=1, source_target_pairs={{0,3},{4,7},{8,11},{12,15},{16,19},{20,23},{24,27},{28,31},{32,35}... | collective-permute-start | bytes 786440 | tf_op jit(solution)/shard_map/ppermute | solution.py:42
  86.0 3.9 collective-permute-start.21
  155.7 5.6 %collective-permute-done.38 = bf16[256,256]{1,0:T(8,128)(2,1)S(1)} collective-permute-done((bf16[256,256]{1,0:T(8,128)(2,1)S(1)}, bf16[256,256]{1,0:T(8,128)(2,1)S(1)}, u32[]{:S(2)}, u32[]{:S(2)}) %collective-permute-start.38) | collective-permute-done | bytes 131104 | tf_op jit(solution)/shard_map/ppermute | solution.py:33
  161.4 3.7 collective-permute-done.37
  166.1 9.3 %collective-permute-start.41 = (bf16[1024,128]{1,0:T(8,128)(2,1)S(1)}, bf16[1024,128]{1,0:T(8,128)(2,1)S(1)}, u32[]{:S(2)}, u32[]{:S(2)}) collective-permute-start(bf16[1024,128]{1,0:T(8,128)(2,1)S(1)} %slice.646), channel_id=1, source_target_pairs={{0,3},{4,7},{8,11},{12,15},{16,19},{20,23},{24,27},{28,31},{32,35}... | collective-permute-start | bytes 786440 | tf_op jit(solution)/shard_map/ppermute | solution.py:42
  185.0 3.7 attend.3.kept_ref
  202.2 4.1 collective-permute-done.47
  230.3 3.9 collective-permute-done.54
  259.8 5.9 %attend_back.2 = (bf16[1024,128]{1,0:T(8,128)(2,1)S(1)}, bf16[1024,128]{1,0:T(8,128)(2,1)S(1)}, bf16[1024,128]{1,0:T(8,128)(2,1)S(1)}, bf16[1024,128]{1,0:T(8,128)(2,1)S(1)}, bf16[1024,128]{1,0:T(8,128)(2,1)S(1)}) custom-call(s32[5]{0:T(128)S(1)} %stack.94.scalar_ref, bf16[1024,256]{1,0:T(8,128)(2,1)S(1)} %pad_maximum_fusion.10.own_ref, ...), custom_call_target="tpu_custom_call" | custom-call | flops 2684354560 | bytes 6291456 | tf_op jit(solution)/shard_map/attend_back/pallas_call | solution.py:338
  269.8 10.4 %collective-permute-done.62 = bf16[1024,128]{1,0:T(8,128)(2,1)S(1)} collective-permute-done((bf16[1024,128]{1,0:T(8,128)(2,1)S(1)}, bf16[1024,128]{1,0:T(8,128)(2,1)S(1)}, u32[]{:S(2)}, u32[]{:S(2)}) %collective-permute-start.62) | collective-permute-done | bytes 262176 | tf_op jit(solution)/shard_map/ppermute | solution.py:42
  280.2 10.5 %collective-permute-done.63 = bf16[1024,128]{1,0:T(8,128)(2,1)S(1)} collective-permute-done((bf16[1024,128]{1,0:T(8,128)(2,1)S(1)}, bf16[1024,128]{1,0:T(8,128)(2,1)S(1)}, u32[]{:S(2)}, u32[]{:S(2)}) %collective-permute-start.63) | collective-permute-done | bytes 262176 | tf_op jit(solution)/shard_map/ppermute | solution.py:42
  290.7 4.7 collective-permute-done.64
  334.1 3.9 convert_reduce_fusion.3
  352.3 4.3 collective-permute-done.77
  367.6 3.9 add_convert_fusion
  400.0 5.5 %attend_back.3 = (bf16[1024,128]{1,0:T(8,128)(2,1)S(1)}, bf16[1024,128]{1,0:T(8,128)(2,1)S(1)}, bf16[1024,128]{1,0:T(8,128)(2,1)S(1)}, bf16[1024,128]{1,0:T(8,128)(2,1)S(1)}, bf16[1024,128]{1,0:T(8,128)(2,1)S(1)}) custom-call(s32[5]{0:T(128)S(1)} %stack.94.scalar_ref, bf16[1024,256]{1,0:T(8,128)(2,1)S(1)} %pad_maximum_fusion.7.own_ref, ...), custom_call_target="tpu_custom_call" | custom-call | flops 2684354560 | bytes 6291456 | tf_op jit(solution)/shard_map/attend_back/pallas_call | solution.py:338
  418.0 5.5 %collective-permute-done.87 = bf16[1024,128]{1,0:T(8,128)(2,1)S(1)} collective-permute-done((bf16[1024,128]{1,0:T(8,128)(2,1)S(1)}, bf16[1024,128]{1,0:T(8,128)(2,1)S(1)}, u32[]{:S(2)}, u32[]{:S(2)}) %collective-permute-start.87) | collective-permute-done | bytes 262176 | tf_op jit(solution)/shard_map/ppermute | solution.py:42
  444.4 5.5 %collective-permute-done.91 = bf16[80,1024]{1,0:T(8,128)(2,1)S(1)} collective-permute-done((bf16[80,1024]{1,0:T(8,128)(2,1)S(1)}, bf16[80,1024]{1,0:T(8,128)(2,1)S(1)}, u32[]{:S(2)}, u32[]{:S(2)}) %collective-permute-start.91) | collective-permute-done | bytes 163872 | tf_op jit(solution)/shard_map/ppermute | solution.py:26
  470.0 3.8 collective-permute-done.99
  482.7 4.3 collective-permute-done.107
  487.1 6.4 %collective-permute-done.106 = bf16[144,1024]{1,0:T(8,128)(2,1)S(1)} collective-permute-done((bf16[144,1024]{1,0:T(8,128)(2,1)S(1)}, bf16[144,1024]{1,0:T(8,128)(2,1)S(1)}, u32[]{:S(2)}, u32[]{:S(2)}) %collective-permute-start.106) | collective-permute-done | bytes 294944 | tf_op jit(solution)/shard_map/ppermute | solution.py:37
  (700 shorter events, 362.3 us)
Async XLA Ops:
  7.2 78.7 %all-gather.4.cloned.1.call-start = ((), (), s32[]{:S(2)}) async-start(), calls=%async_computation.3 | async-start | bytes 2621440 | tf_op jit(solution)/shard_map/all_gather | solution.py:515
  8.2 16.7 %collective-permute-start.11 = (bf16[64,1024]{1,0:T(8,128)(2,1)S(1)}, bf16[64,1024]{1,0:T(8,128)(2,1)S(1)}, u32[]{:S(2)}, u32[]{:S(2)}) collective-permute-start(bf16[64,1024]{1,0:T(8,128)(2,1)S(1)} %dynamic-slice_bitcast_fusion.4), channel_id=1, source_target_pairs={{0,12},{4,0},{8,4},{12,8},{16,28},{20,16},{24,20},{28,24},{32,44},... | collective-permute-start | bytes 393224 | tf_op jit(solution)/shard_map/ppermute | solution.py:26
  12.4 15.0 %collective-permute-start.9 = (bf16[64,1024]{1,0:T(8,128)(2,1)S(1)}, bf16[64,1024]{1,0:T(8,128)(2,1)S(1)}, u32[]{:S(2)}, u32[]{:S(2)}) collective-permute-start(bf16[64,1024]{1,0:T(8,128)(2,1)S(1)} %dynamic-slice_bitcast_fusion.4), channel_id=1, source_target_pairs={{0,4},{4,8},{8,12},{12,0},{16,20},{20,24},{24,28},{28,16},{32,36},... | collective-permute-start | bytes 393224 | tf_op jit(solution)/shard_map/ppermute | solution.py:26
  28.3 15.5 %collective-permute-start.7 = (bf16[144,1024]{1,0:T(8,128)(2,1)S(1)}, bf16[144,1024]{1,0:T(8,128)(2,1)S(1)}, u32[]{:S(2)}, u32[]{:S(2)}) collective-permute-start(bf16[144,1024]{1,0:T(8,128)(2,1)S(1)} %get-tuple-element.53), channel_id=1, source_target_pairs={{0,48},{4,52},{8,56},{12,60},{16,0},{20,4},{24,8},{28,12},{32,16},... | collective-permute-start | bytes 884744 | tf_op jit(solution)/shard_map/ppermute | solution.py:33
  47.6 60.1 %all-gather.6.cloned.1.call-start = ((), (), s32[]{:S(2)}) async-start(), calls=%async_computation.4 | async-start | bytes 1474560 | tf_op jit(solution)/shard_map/all_gather | solution.py:515
  48.4 131.1 %all-gather.8.cloned.1.call-start = ((), (), s32[]{:S(2)}) async-start(), calls=%async_computation.5 | async-start | bytes 2621440 | tf_op jit(solution)/shard_map/all_gather | solution.py:515
  85.9 38.7 %collective-permute-start.28 = (bf16[1024,1024]{1,0:T(8,128)(2,1)}, bf16[1024,1024]{1,0:T(8,128)(2,1)}, u32[]{:S(2)}, u32[]{:S(2)}) collective-permute-start(bf16[1024,1024]{1,0:T(8,128)(2,1)} %all-gather.4.cloned.1.call-done), channel_id=1, source_target_pairs={{0,64},{64,0},{1,65},{65,1},{2,66},{66,2},{3,67},{67,3},{4,68},{68... | collective-permute-start | bytes 6291464 | tf_op jit(solution)/shard_map/ppermute | solution.py:62
  119.3 19.9 %collective-permute-start.32 = (bf16[4,144,1024]{2,1,0:T(8,128)(2,1)}, bf16[4,144,1024]{2,1,0:T(8,128)(2,1)S(1)}, u32[]{:S(2)}, u32[]{:S(2)}) collective-permute-start(bf16[4,144,1024]{2,1,0:T(8,128)(2,1)} %pad_maximum_fusion.3), channel_id=1, source_target_pairs={{0,64},{64,0},{1,65},{65,1},{2,66},{66,2},{3,67},{67,3},{4,68},{68... | collective-permute-start | bytes 3538952 | tf_op jit(solution)/shard_map/ppermute | solution.py:62
  132.6 174.0 %reduce-scatter.4.cloned.1.call-start = ((), (), s32[]{:S(2)}) async-start(), calls=%async_computation.6 | async-start | bytes 2621440 | tf_op jit(solution)/shard_map/reduce_scatter | solution.py:573
  166.1 16.0 %collective-permute-start.41 = (bf16[1024,128]{1,0:T(8,128)(2,1)S(1)}, bf16[1024,128]{1,0:T(8,128)(2,1)S(1)}, u32[]{:S(2)}, u32[]{:S(2)}) collective-permute-start(bf16[1024,128]{1,0:T(8,128)(2,1)S(1)} %slice.646), channel_id=1, source_target_pairs={{0,3},{4,7},{8,11},{12,15},{16,19},{20,23},{24,27},{28,31},{32,35}... | collective-permute-start | bytes 786440 | tf_op jit(solution)/shard_map/ppermute | solution.py:42
  179.5 32.3 %collective-permute-start.48 = (bf16[1024,1024]{1,0:T(8,128)(2,1)}, bf16[1024,1024]{1,0:T(8,128)(2,1)S(1)}, u32[]{:S(2)}, u32[]{:S(2)}) collective-permute-start(bf16[1024,1024]{1,0:T(8,128)(2,1)} %all-gather.8.cloned.1.call-done), channel_id=1, source_target_pairs={{0,64},{64,0},{1,65},{65,1},{2,66},{66,2},{3,67},{67,3},{4,68},{68... | collective-permute-start | bytes 6291464 | tf_op jit(solution)/shard_map/ppermute | solution.py:62
  223.1 23.4 %collective-permute-start.58 = (bf16[1024,1024]{1,0:T(8,128)(2,1)S(1)}, bf16[1024,1024]{1,0:T(8,128)(2,1)S(1)}, u32[]{:S(2)}, u32[]{:S(2)}) collective-permute-start(bf16[1024,1024]{1,0:T(8,128)(2,1)S(1)} %get-tuple-element.273), channel_id=1, source_target_pairs={{0,64},{64,0},{1,65},{65,1},{2,66},{66,2},{3,67},{67,3},{4,68},{68... | collective-permute-start | bytes 6291464 | tf_op jit(solution)/shard_map/ppermute | solution.py:62
  249.4 122.1 %all-reduce.9.cloned.1.call-start = ((), (), s32[]{:S(2)}) async-start(), calls=%async_computation.7 | async-start | bytes 1048576 | tf_op jit(solution)/shard_map/psum | solution.py:605
  267.2 23.5 %collective-permute-start.63 = (bf16[1024,128]{1,0:T(8,128)(2,1)S(1)}, bf16[1024,128]{1,0:T(8,128)(2,1)S(1)}, u32[]{:S(2)}, u32[]{:S(2)}) collective-permute-start(bf16[1024,128]{1,0:T(8,128)(2,1)S(1)} %get-tuple-element.66), channel_id=1, source_target_pairs={{2,0},{3,1},{6,4},{7,5},{10,8},{11,9},{14,12},{15,13},{18,16},{19,... | collective-permute-start | bytes 786440 | tf_op jit(solution)/shard_map/ppermute | solution.py:42
  268.5 26.9 %collective-permute-start.64 = (bf16[1024,128]{1,0:T(8,128)(2,1)S(1)}, bf16[1024,128]{1,0:T(8,128)(2,1)S(1)}, u32[]{:S(2)}, u32[]{:S(2)}) collective-permute-start(bf16[1024,128]{1,0:T(8,128)(2,1)S(1)} %get-tuple-element.67), channel_id=1, source_target_pairs={{3,0},{7,4},{11,8},{15,12},{19,16},{23,20},{27,24},{31,28},{35,32}... | collective-permute-start | bytes 786440 | tf_op jit(solution)/shard_map/ppermute | solution.py:42
  313.9 16.3 %collective-permute-start.74 = (bf16[4,128,1024]{2,1,0:T(8,128)(2,1)}, bf16[4,128,1024]{2,1,0:T(8,128)(2,1)}, u32[]{:S(2)}, u32[]{:S(2)}) collective-permute-start(bf16[4,128,1024]{2,1,0:T(8,128)(2,1)} %broadcast_select_fusion.8), channel_id=1, source_target_pairs={{0,64},{64,0},{1,65},{65,1},{2,66},{66,2},{3,67},{67,3},{4,68},{68... | collective-permute-start | bytes 3145736 | tf_op jit(solution)/shard_map/ppermute | solution.py:62
  321.9 101.9 %reduce-scatter.8.cloned.1.call-start = ((), (), s32[]{:S(2)}) async-start(), calls=%async_computation.9 | async-start | bytes 1310720 | tf_op jit(solution)/shard_map/reduce_scatter | solution.py:573
  343.1 24.5 %collective-permute-start.81 = (bf16[1024,1024]{1,0:T(8,128)(2,1)}, bf16[1024,1024]{1,0:T(8,128)(2,1)}, u32[]{:S(2)}, u32[]{:S(2)}) collective-permute-start(bf16[1024,1024]{1,0:T(8,128)(2,1)} %get-tuple-element.275), channel_id=1, source_target_pairs={{0,64},{64,0},{1,65},{65,1},{2,66},{66,2},{3,67},{67,3},{4,68},{68... | collective-permute-start | bytes 6291464 | tf_op jit(solution)/shard_map/ppermute | solution.py:62
  343.1 80.7 %reduce-scatter.6.cloned.1.call-start = ((), (), s32[]{:S(2)}) async-start(), calls=%async_computation.8 | async-start | bytes 2621440 | tf_op jit(solution)/shard_map/reduce_scatter | solution.py:573
  371.5 122.2 %all-reduce.11.cloned.1.call-start = ((), (), s32[]{:S(2)}) async-start(), calls=%async_computation.10 | async-start | bytes 1572864 | tf_op jit(solution)/shard_map/psum | solution.py:626
  376.0 78.3 %collective-permute-start.94 = (bf16[64,1024]{1,0:T(8,128)(2,1)}, bf16[64,1024]{1,0:T(8,128)(2,1)}, u32[]{:S(2)}, u32[]{:S(2)}) collective-permute-start(bf16[64,1024]{1,0:T(8,128)(2,1)} %get-tuple-element.173), channel_id=1, source_target_pairs={{0,12},{4,0},{8,4},{12,8},{16,28},{20,16},{24,20},{28,24},{32,44},... | collective-permute-start | bytes 393224 | tf_op jit(solution)/shard_map/ppermute | solution.py:26
  376.7 77.5 %collective-permute-start.96 = (bf16[64,1024]{1,0:T(8,128)(2,1)}, bf16[64,1024]{1,0:T(8,128)(2,1)}, u32[]{:S(2)}, u32[]{:S(2)}) collective-permute-start(bf16[64,1024]{1,0:T(8,128)(2,1)} %get-tuple-element.174), channel_id=1, source_target_pairs={{0,4},{4,8},{8,12},{12,0},{16,20},{20,24},{24,28},{28,16},{32,36},... | collective-permute-start | bytes 393224 | tf_op jit(solution)/shard_map/ppermute | solution.py:26
  408.2 15.4 %collective-permute-start.87 = (bf16[1024,128]{1,0:T(8,128)(2,1)S(1)}, bf16[1024,128]{1,0:T(8,128)(2,1)S(1)}, u32[]{:S(2)}, u32[]{:S(2)}) collective-permute-start(bf16[1024,128]{1,0:T(8,128)(2,1)S(1)} %get-tuple-element.77), channel_id=1, source_target_pairs={{3,0},{7,4},{11,8},{15,12},{19,16},{23,20},{27,24},{31,28},{35,32}... | collective-permute-start | bytes 786440 | tf_op jit(solution)/shard_map/ppermute | solution.py:42
  477.5 16.0 %collective-permute-start.106 = (bf16[144,1024]{1,0:T(8,128)(2,1)S(1)}, bf16[144,1024]{1,0:T(8,128)(2,1)S(1)}, u32[]{:S(2)}, u32[]{:S(2)}) collective-permute-start(bf16[144,1024]{1,0:T(8,128)(2,1)S(1)} %pad_maximum_fusion.18), channel_id=1, source_target_pairs={{0,2},{1,3},{2,0},{3,1},{4,6},{5,7},{6,4},{7,5},{8,10},{9,11},{10,... | collective-permute-start | bytes 884744 | tf_op jit(solution)/shard_map/ppermute | solution.py:37
  (222 other events, 2023.7 us)
Sparse Core Ops, SparseCore 0:
  47.8 32.4 all-gather.3
  82.5 25.1 all-gather.5
  132.8 40.5 all-gather.7
  249.5 32.0 reduce-scatter.3
  322.0 40.7 all-reduce.8
  365.2 24.0 reduce-scatter.7
  391.7 29.8 reduce-scatter.5
  429.3 43.6 all-reduce.10

commit v6 on v5

--- a/solution.py
+++ b/solution.py
@@ -98,10 +98,7 @@
 
 
 def column_sum(rows):
-    ones = jnp.ones((8, rows.shape[0]), rows.dtype)
-    return jnp.dot(
-        ones, rows, precision=lax.Precision.HIGHEST, preferred_element_type=FULL
-    )[0:1]
+    return jnp.sum(rows.astype(FULL), axis=0)
 
 
 def layer_norm_back(grad, values, gain):
@@ -493,7 +490,12 @@
         axis=0,
     )
     small_other = swap(small)
-    up_own, down_other = w_up[0].T, swap(w_down[0])
+    half_rows = w_down.shape[1] // 2
+    units_own = jnp.concatenate(
+        [w_up[0].T.reshape(2, half_rows, model_width), w_down[0].reshape(2, half_rows, model_width)], axis=1
+    )
+    units_other = swap(lax.dynamic_index_in_dim(units_own, 1 - here, 0, False))
+    units_own = lax.dynamic_index_in_dim(units_own, here, 0, False)
     downward = [(x_here - d) % SIDE for d in range(SIDE)]
 
     def reorder(pieces):
@@ -508,15 +510,22 @@
         back = query_out[:, :128].reshape(SIDE * 128, model_width)
         rows = key_value[:, 128, :512].astype(FULL)
         bias_heads = rows[:, 256:].reshape(1, SIDE * TILE)
-        bias_up = jnp.concatenate(reorder(rows[:, :256])).reshape(1, SIDE * TILE)
+        bias_up = jnp.stack(reorder(rows[:, :256])).reshape(SIDE, 2, half_rows)
+        bias_up = jnp.stack([bias_up[:, 0], bias_up[:, 1]])
+        bias_up = owner(0, bias_up, bias_up[::-1]).reshape(1, SIDE * TILE)
         return (whole.reshape(SIDE * TILE, model_width), back), bias_heads, bias_up
 
     def gather_whole(half):
         return lax.all_gather(half, "tensor", axis=0, tiled=True, axis_index_groups=X_GROUPS)
 
-    def join_units(layer, mine):
-        theirs = swap(mine)
-        return owner(layer, mine, theirs), owner(layer, theirs, mine)
+    def join_units(mine):
+        mine, theirs = [
+            part.reshape(SIDE, 2 * half_rows, model_width) for part in (mine, swap(mine))
+        ]
+        return tuple(
+            jnp.concatenate([mine[:, span], theirs[:, span]]).reshape(-1, model_width)
+            for span in (slice(0, half_rows), slice(half_rows, 2 * half_rows))
+        )
 
     smalls = (owner(0, small, small_other), owner(0, small_other, small))
     vectors = [
@@ -525,12 +534,12 @@
     normed = layer_norm(sequence, *vectors[0][0:2]).astype(LOW)
     half, normed = tie(half_heads(0), normed)
     mine = jnp.stack([half] + [move_x(half, d) for d in range(1, SIDE)])
-    half = owner(0, up_own, down_other)
+    half = owner(0, units_own, units_other)
     normed_all, mine, half, grad_last_all = tie(gather_z(normed), mine, half, gather_z(grad_last_all))
     heads_first, bias_heads_first, bias_up_first = join_heads(0, mine, swap(mine))
     units_first = gather_whole(half)
     heads_last = gather_whole(half_heads(1)).reshape(SIDE, -1, model_width)
-    units_last = gather_whole(owner(1, up_own, down_other))
+    units_last = gather_whole(owner(1, units_own, units_other))
     normed_all, segments = tie(normed_all, segments)
     segment_ids = lax.dynamic_index_in_dim(segments, here, 0, False)
     start_one = jnp.sum((segment_ids < 1).astype(jnp.int32))
@@ -546,7 +555,7 @@
     hidden, kept_heads_first = forward_attention(
         sequence, normed_all, spots, vectors[0], bias_heads_first, *heads_first
     )
-    units_first = join_units(0, units_first)
+    units_first = join_units(units_first)
     middle, kept_units_first = forward_hidden_units(hidden, vectors[0], bias_up_first, *units_first)
     mine = jnp.stack(reorder(heads_last))
     middle, mine, theirs = tie(middle, mine, swap(mine))
@@ -556,7 +565,7 @@
     hidden, kept_heads_last = forward_attention(
         middle, normed_all, spots, vectors[1], bias_heads_last, *heads_last
     )
-    units_last = join_units(1, units_last)
+    units_last = join_units(units_last)
     result, kept_units_last = forward_hidden_units(hidden, vectors[1], bias_up_last, *units_last)
 
     def choose_grads(layer, first, second):
@@ -568,6 +577,14 @@
 
     def add_grads(kept, arrived):
         return (kept.astype(FULL) + arrived.astype(FULL)).astype(LOW)
+
+    def add_units(g_up, g_down):
+        parts = [g.reshape(2, SIDE, half_rows, model_width) for g in (g_up, g_down)]
+        kept, payload = [
+            jnp.concatenate([part[side] for part in parts], axis=1).reshape(-1, model_width)
+            for side in range(2)
+        ]
+        return add_grads(kept, swap(payload))
 
     def scatter_whole(grads):
         return lax.psum_scatter(
@@ -581,12 +598,13 @@
     turn = jnp.stack(downward)[None, :] == jnp.arange(SIDE)[:, None]
 
     def pack_vectors(heads, units, g_b_out, g_b_up, g_b_qkv):
-        by_turn = jnp.sum(
-            jnp.where(turn[:, :, None], g_b_up.reshape(SIDE, 1, TILE), 0.0), axis=0
-        )
+        halves = g_b_up.reshape(2, SIDE, half_rows)
+        halves = owner(0, halves, halves[::-1])
+        by_place = jnp.concatenate([halves[0], halves[1]], axis=1)
+        by_turn = jnp.sum(jnp.where(turn[:, :, None], by_place[:, None], 0.0), axis=0)
         return jnp.concatenate(
             [
-                *heads, g_b_out, *units,
+                jnp.stack([*heads, g_b_out, *units]),
                 jnp.concatenate([by_turn, g_b_qkv.reshape(SIDE, TILE)], axis=1).reshape(2, -1),
             ],
             axis=0,
@@ -595,13 +613,14 @@
     grad_hidden, vec_units_last, g_b_up_last, g_up, g_down = backward_hidden_units(
         grad_last, grad_last_all, kept_units_last, vectors[1], *units_last
     )
-    units_sum_last = add_grads(*swap_grads(1, g_up, g_down))
+    units_sum_last = add_units(g_up, g_down)
     grad_mixed, g_b_out_last, g_out, units_sum_last = backward_mixed(
         grad_hidden, kept_heads_last, heads_last[1], spots, units_sum_last
     )
     units_sum_last = scatter_whole(units_sum_last)
-    grad_qkv = backward_heads(attend_back(spots, *kept_heads_last[2:5], grad_mixed))
-    grad_qkv, units_sum_last = tie(grad_qkv, units_sum_last)
+    grad_qkv, units_sum_last = backward_heads(
+        attend_back(spots, *kept_heads_last[2:5], grad_mixed), units_sum_last
+    )
     units_sum_last = lax.psum(units_sum_last, "ctx")
     grad_middle, vec_heads_last, g_b_qkv_last, g_heads = backward_entry(
         grad_qkv, grad_hidden, kept_heads_last, vectors[1], heads_last[0]
@@ -615,7 +634,7 @@
     grad_hidden, vec_units_first, g_b_up_first, g_up, g_down = backward_hidden_units(
         grad_middle, grad_down_all, kept_units_first, vectors[0], *units_first
     )
-    units_sum_first = add_grads(*swap_grads(0, g_up, g_down))
+    units_sum_first = add_units(g_up, g_down)
     grad_mixed, g_b_out_first, g_out, (units_sum_first, units_sum_last) = backward_mixed(
         grad_hidden, kept_heads_first, heads_first[1], spots, (units_sum_first, units_sum_last)
     )
@@ -627,9 +646,6 @@
 
     gain_one, bias_one = vectors[0][0:2]
     residual, normed_all = kept_heads_first[0:2]
-    heads_kept, payload = choose_grads(0, *split_heads(tn_dot(grad_qkv, normed_all).astype(LOW), g_out))
-    grad_qkv, payload = tie(grad_qkv, payload)
-    halves = add_grads(heads_kept, swap(payload))
     grad_normed = local_dot(grad_qkv, heads_first[0])
     g_bias_one = column_sum(grad_normed)
     g_gain_one = column_sum(grad_normed * ((normed_all.astype(FULL) - bias_one) / gain_one))
@@ -644,11 +660,13 @@
     sums_first = jnp.concatenate([chunks[row_count : row_count + 6], sums_first[6:]])
     sums_last = jnp.concatenate([chunks[row_count + 6 : row_count + 12], sums_last[6:]])
     sums = owner(0, sums_first, sums_last) + swap(owner(0, sums_last, sums_first))
+    halves = add_grads(*swap_grads(0, *split_heads(tn_dot(grad_qkv, normed_all).astype(LOW), g_out)))
     common = sums[:6].astype(LOW)
     split = sums[6:].reshape(SIDE, 1, 512).astype(LOW)
     packs = [
         jnp.concatenate(
             [
+                halves[d],
                 common,
                 jnp.pad(split[d], ((0, 0), (0, model_width - 512))),
                 jnp.zeros((9, model_width), LOW),
@@ -657,11 +675,10 @@
         )
         for d in range(SIDE)
     ]
-    pack = jnp.concatenate([even_pairs(halves, move_x), even_pairs(packs, move_x)], axis=0)
-    pack = even_sum(pack.astype(LOW), move_y)
     pack, units_sum_first, units_sum_last, heads_sum_last = tie(
-        pack, units_sum_first, units_sum_last, heads_sum_last
-    )
+        even_pairs(packs, move_x).astype(LOW), units_sum_first, units_sum_last, heads_sum_last
+    )
+    pack = even_sum(pack, move_y)
     heads_sum_first, pack = pack[:128], pack[128:]
     grad_first = grad_hidden + layer_norm_back(chunks[:row_count], residual, gain_one)[0]
 
@@ -674,6 +691,7 @@
     heads_sum = owner(0, heads_sum_first, heads_sum_last)
     units_theirs = swap(owner(0, units_sum_last, units_sum_first))
     heads_theirs = swap(owner(0, heads_sum_last, heads_sum_first).astype(LOW))
+    low_units, high_units = owner(0, units_sum, units_theirs), owner(0, units_theirs, units_sum)
     g_key_value = heads_sum.astype(FULL)
     g_query_out = heads_theirs.astype(FULL)
     g_w_qkv = jnp.stack([g_query_out[0:64].T, g_key_value[0:64].T, g_key_value[64:128].T], axis=1)
@@ -688,9 +706,9 @@
         pack[2:3],
         pack[3:4],
         pack[4:5],
-        units_sum.astype(FULL).T[None],
+        jnp.concatenate([low_units[:half_rows], high_units[:half_rows]]).astype(FULL).T[None],
         pack[6:7, 0:256],
-        units_theirs.astype(FULL)[None],
+        jnp.concatenate([low_units[half_rows:], high_units[half_rows:]]).astype(FULL)[None],
         pack[5:6],
     )
 

time: 520 us -> 563 us (1.083)
  local copies, waits for them, and re-layouts: 32.5 us -> 79.5 us
  other arithmetic: 54.3 us -> 61.7 us
  matrix products: 42.2 us -> 34.9 us
  starting transfers between devices: 143 us -> 136 us
    all_gather x3, waiting for transfers between devices: 2.14 us -> 29.2 us  [gather_whole(): lax.all_gather(half, 'tensor', axis=0, tiled=True, axis_index_groups=X_GR...]
    reshape x0 -> x8, local copies, waits for them, and re-layouts: none -> 25.9 us  [the longest x4 18 us: join_units(): part.reshape(SIDE, 2 * half_rows, model_width)]
    ppermute x48, waiting for transfers between devices: 77.2 us -> 58.2 us  [move_z(): return lax.ppermute(block, 'tensor', route)]
    convert_element_type x0 -> x2, local copies, waits for them, and re-layouts: none -> 10.7 us  [add_grads(): return (kept.astype(FULL) + arrived.astype(FULL)).astype(LOW)]
    convert_element_type x4 -> x6, other arithmetic: 12.1 us -> 20.5 us  [add_grads(): return (kept.astype(FULL) + arrived.astype(FULL)).astype(LOW)]
    concatenate x6 -> x11, other arithmetic: 0.82 us -> 8.6 us  [the longest x4 4.34 us: join_units(): jnp.concatenate([mine[:, span], theirs[:, span]]).reshape(-1, model_width)]
    dot_general x12 -> x0, matrix products: 7.39 us -> none  [column_sum(): jnp.dot(ones, rows, precision=lax.Precision.HIGHEST, preferred_element_ty...]
    slice x14 -> x11, local copies, waits for them, and re-layouts: 6.64 us -> 14 us  [the longest x2 7.18 us: join_units(): mine[:, span]]
  transfers between devices with their start and end apart: 119 -> 116, of which waited for: 76 -> 64; matrix products, arithmetic and copies ran while one was open for 20% -> 25% of each run, Pallas kernels for 4% -> 3%
where the time goes in v6:
time: 563 us; the launch traced here: 556 us
  waiting for transfers between devices  208 us (37%)
  starting transfers between devices  136 us (24%)
  local copies, waits for them, and re-layouts  79.5 us (14%)
  other arithmetic  61.7 us (11%)
  matrix products  34.9 us (6%)
  Pallas kernels  18.5 us (3%)
  between operations  17.2 us (3%)
    ppermute x48, starting transfers between devices, move_z(): return lax.ppermute(block, 'tensor', route)  63.6 us
    ppermute x30, waiting for transfers between devices, move_x(): return lax.ppermute(block, 'tensor', route)  59.9 us
    ppermute x48, waiting for transfers between devices, move_z(): return lax.ppermute(block, 'tensor', route)  58.2 us
    ppermute x12, waiting for transfers between devices, move_y_open(): return lax.ppermute(block, 'ctx', route)  43.7 us
    ppermute x30, starting transfers between devices, move_x(): return lax.ppermute(block, 'tensor', route)  40.2 us
    all_gather x3, waiting for transfers between devices, gather_whole(): lax.all_gather(half, 'tensor', axis=0, tiled=True, axis_index_groups=X_GR...  29.2 us
    ppermute x12, starting transfers between devices, move_y_open(): return lax.ppermute(block, 'ctx', route)  26.9 us
    convert_element_type x6, other arithmetic, add_grads(): return (kept.astype(FULL) + arrived.astype(FULL)).astype(LOW)  20.5 us
  transfers between devices with their start and end apart: 116, of which 64 were waited for; matrix products, arithmetic and copies ran while one was open for 25% of the time, Pallas kernels for 3%

profile of v6, /device:TPU:0, one launch (start us, length us, event | category | flops | bytes accessed | tf_op | source)
XLA Modules:
  0.0 555.8 jit_solution(12611225719089776846)
XLA Ops:
  44.7 5.7 %collective-permute-done.5 = bf16[144,1024]{1,0:T(8,128)(2,1)S(1)} collective-permute-done((bf16[144,1024]{1,0:T(8,128)(2,1)S(1)}, bf16[144,1024]{1,0:T(8,128)(2,1)S(1)}, u32[]{:S(2)}, u32[]{:S(2)}) %collective-permute-start.5) | collective-permute-done | bytes 294944 | tf_op jit(solution)/shard_map/ppermute | solution.py:33
  61.6 5.7 %collective-permute-done.15 = bf16[256,256]{1,0:T(8,128)(2,1)S(1)} collective-permute-done((bf16[256,256]{1,0:T(8,128)(2,1)S(1)}, bf16[256,256]{1,0:T(8,128)(2,1)S(1)}, u32[]{:S(2)}, u32[]{:S(2)}) %collective-permute-start.15) | collective-permute-done | bytes 131104 | tf_op jit(solution)/shard_map/ppermute | solution.py:33
  71.0 4.7 collective-permute-start.18
  97.9 29.2 %all-gather.4.cloned.1.call-done = bf16[1024,1024]{0,1:T(8,128)(2,1)} async-done(((bf16[256,1024]{0,1:T(8,128)(2,1)}), bf16[1024,1024]{0,1:T(8,128)(2,1)}) %all-gather.4.cloned.1.call-update) | async-done | bytes 2097168 | tf_op jit(solution)/shard_map/all_gather | solution.py:519
  134.9 6.2 %collective-permute-done.24 = bf16[64,1024]{1,0:T(8,128)(2,1)S(1)} collective-permute-done((bf16[64,1024]{1,0:T(8,128)(2,1)S(1)}, bf16[64,1024]{1,0:T(8,128)(2,1)S(1)}, u32[]{:S(2)}, u32[]{:S(2)}) %collective-permute-start.24) | collective-permute-done | bytes 131104 | tf_op jit(solution)/shard_map/ppermute | solution.py:26
  142.6 4.5 reshape.467
  150.7 4.5 reshape.459
  160.1 4.5 reshape.468
  207.9 5.6 %collective-permute-start.41 = (bf16[1024,128]{1,0:T(8,128)(2,1)S(1)}, bf16[1024,128]{1,0:T(8,128)(2,1)S(1)}, u32[]{:S(2)}, u32[]{:S(2)}) collective-permute-start(bf16[1024,128]{1,0:T(8,128)(2,1)S(1)} %slice.712), channel_id=1, source_target_pairs={{0,3},{4,7},{8,11},{12,15},{16,19},{20,23},{24,27},{28,31},{32,35}... | collective-permute-start | bytes 786440 | tf_op jit(solution)/shard_map/ppermute | solution.py:42
  276.7 5.4 collective-permute-done.54
  289.2 5.3 copy.52
  296.5 5.0 add_convert_fusion.1
  311.2 5.5 attend_back.2
  320.7 10.3 %collective-permute-done.62 = bf16[1024,128]{1,0:T(8,128)(2,1)S(1)} collective-permute-done((bf16[1024,128]{1,0:T(8,128)(2,1)S(1)}, bf16[1024,128]{1,0:T(8,128)(2,1)S(1)}, u32[]{:S(2)}, u32[]{:S(2)}) %collective-permute-start.62) | collective-permute-done | bytes 262176 | tf_op jit(solution)/shard_map/ppermute | solution.py:42
  331.0 8.5 %collective-permute-done.63 = bf16[1024,128]{1,0:T(8,128)(2,1)S(1)} collective-permute-done((bf16[1024,128]{1,0:T(8,128)(2,1)S(1)}, bf16[1024,128]{1,0:T(8,128)(2,1)S(1)}, u32[]{:S(2)}, u32[]{:S(2)}) %collective-permute-start.63) | collective-permute-done | bytes 262176 | tf_op jit(solution)/shard_map/ppermute | solution.py:42
  339.4 4.9 collective-permute-done.64
  406.8 5.5 collective-permute-done.77
  418.8 5.3 copy.54
  425.0 5.0 add_convert_fusion
  452.0 5.7 %attend_back.3 = (bf16[1024,128]{1,0:T(8,128)(2,1)S(1)}, bf16[1024,128]{1,0:T(8,128)(2,1)S(1)}, bf16[1024,128]{1,0:T(8,128)(2,1)S(1)}, bf16[1024,128]{1,0:T(8,128)(2,1)S(1)}, bf16[1024,128]{1,0:T(8,128)(2,1)S(1)}) custom-call(s32[5]{0:T(128)S(1)} %stack.162.scalar_ref, bf16[1024,256]{1,0:T(8,128)(2,1)S(1)} %pad_maximum_fusion.19.own_ref, ...), custom_call_target="tpu_custom_call" | custom-call | flops 2684354560 | bytes 6291456 | tf_op jit(solution)/shard_map/attend_back/pallas_call | solution.py:335
  469.8 5.5 collective-permute-done.87
  512.5 7.3 %collective-permute-done.100 = bf16[144,1024]{1,0:T(8,128)(2,1)S(1)} collective-permute-done((bf16[144,1024]{1,0:T(8,128)(2,1)S(1)}, bf16[144,1024]{1,0:T(8,128)(2,1)S(1)}, u32[]{:S(2)}, u32[]{:S(2)}) %collective-permute-start.100) | collective-permute-done | bytes 294944 | tf_op jit(solution)/shard_map/ppermute | solution.py:33
  530.0 5.5 collective-permute-done.105
  535.5 6.7 %collective-permute-done.104 = bf16[144,1024]{1,0:T(8,128)(2,1)S(1)} collective-permute-done((bf16[144,1024]{1,0:T(8,128)(2,1)S(1)}, bf16[144,1024]{1,0:T(8,128)(2,1)S(1)}, u32[]{:S(2)}, u32[]{:S(2)}) %collective-permute-start.104) | collective-permute-done | bytes 294944 | tf_op jit(solution)/shard_map/ppermute | solution.py:37
  (769 shorter events, 376.7 us)
Async XLA Ops:
  7.2 88.4 %all-gather.6.cloned.1.call-start = ((), (), s32[]{:S(2)}) async-start(), calls=%async_computation.4 | async-start | bytes 1474560 | tf_op jit(solution)/shard_map/all_gather | solution.py:519
  12.1 85.8 %all-gather.8.cloned.1.call-start = ((), (), s32[]{:S(2)}) async-start(), calls=%async_computation.5 | async-start | bytes 2621440 | tf_op jit(solution)/shard_map/all_gather | solution.py:519
  16.0 111.1 %all-gather.4.cloned.1.call-start = ((), (), s32[]{:S(2)}) async-start(), calls=%async_computation.3 | async-start | bytes 2621440 | tf_op jit(solution)/shard_map/all_gather | solution.py:519
  30.3 20.1 %collective-permute-start.5 = (bf16[144,1024]{1,0:T(8,128)(2,1)S(1)}, bf16[144,1024]{1,0:T(8,128)(2,1)S(1)}, u32[]{:S(2)}, u32[]{:S(2)}) collective-permute-start(bf16[144,1024]{1,0:T(8,128)(2,1)S(1)} %get-tuple-element.51), channel_id=1, source_target_pairs={{0,16},{4,20},{8,24},{12,28},{16,32},{20,36},{24,40},{28,44},{32,4... | collective-permute-start | bytes 884744 | tf_op jit(solution)/shard_map/ppermute | solution.py:33
  50.8 293.8 %reduce-scatter.4.cloned.1.call-start = ((), (), s32[]{:S(2)}) async-start(), calls=%async_computation.6 | async-start | bytes 2621440 | tf_op jit(solution)/shard_map/reduce_scatter | solution.py:590
  90.9 36.3 %collective-permute-start.21 = (bf16[256,128]{1,0:T(8,128)(2,1)}, bf16[256,128]{1,0:T(8,128)(2,1)S(1)}, u32[]{:S(2)}, u32[]{:S(2)}) collective-permute-start(bf16[256,128]{1,0:T(8,128)(2,1)} %get-tuple-element.264), channel_id=1, source_target_pairs={{0,48},{4,52},{8,56},{12,60},{16,0},{20,4},{24,8},{28,12},{32,16},... | collective-permute-start | bytes 196616 | tf_op jit(solution)/shard_map/ppermute | solution.py:33
  94.8 32.4 %collective-permute-start.20 = (bf16[256,128]{1,0:T(8,128)(2,1)}, bf16[256,128]{1,0:T(8,128)(2,1)S(1)}, u32[]{:S(2)}, u32[]{:S(2)}) collective-permute-start(bf16[256,128]{1,0:T(8,128)(2,1)} %get-tuple-element.265), channel_id=1, source_target_pairs={{0,32},{4,36},{8,40},{12,44},{16,48},{20,52},{24,56},{28,60},{32,0... | collective-permute-start | bytes 196616 | tf_op jit(solution)/shard_map/ppermute | solution.py:33
  94.8 32.5 %collective-permute-start.19 = (bf16[256,128]{1,0:T(8,128)(2,1)S(1)}, bf16[256,128]{1,0:T(8,128)(2,1)S(1)}, u32[]{:S(2)}, u32[]{:S(2)}) collective-permute-start(bf16[256,128]{1,0:T(8,128)(2,1)S(1)} %get-tuple-element.266), channel_id=1, source_target_pairs={{0,16},{4,20},{8,24},{12,28},{16,32},{20,36},{24,40},{28,44},{32,4... | collective-permute-start | bytes 196616 | tf_op jit(solution)/shard_map/ppermute | solution.py:33
  97.9 60.8 %collective-permute-start.48 = (bf16[1024,1024]{0,1:T(8,128)(2,1)}, bf16[1024,1024]{0,1:T(8,128)(2,1)}, u32[]{:S(2)}, u32[]{:S(2)}) collective-permute-start(bf16[1024,1024]{0,1:T(8,128)(2,1)} %all-gather.8.cloned.1.call-done), channel_id=1, source_target_pairs={{0,64},{64,0},{1,65},{65,1},{2,66},{66,2},{3,67},{67,3},{4,68},{68... | collective-permute-start | bytes 6291464 | tf_op jit(solution)/shard_map/ppermute | solution.py:62
  127.1 37.5 %collective-permute-start.28 = (bf16[1024,1024]{0,1:T(8,128)(2,1)}, bf16[1024,1024]{0,1:T(8,128)(2,1)}, u32[]{:S(2)}, u32[]{:S(2)}) collective-permute-start(bf16[1024,1024]{0,1:T(8,128)(2,1)} %all-gather.4.cloned.1.call-done), channel_id=1, source_target_pairs={{0,64},{64,0},{1,65},{65,1},{2,66},{66,2},{3,67},{67,3},{4,68},{68... | collective-permute-start | bytes 6291464 | tf_op jit(solution)/shard_map/ppermute | solution.py:62
  134.9 53.4 %collective-permute-start.32 = (bf16[4,144,1024]{2,1,0:T(8,128)(2,1)S(1)}, bf16[4,144,1024]{2,1,0:T(8,128)(2,1)}, u32[]{:S(2)}, u32[]{:S(2)}) collective-permute-start(bf16[4,144,1024]{2,1,0:T(8,128)(2,1)S(1)} %pad_maximum_fusion.11), channel_id=1, source_target_pairs={{0,64},{64,0},{1,65},{65,1},{2,66},{66,2},{3,67},{67,3},{4,68},{68... | collective-permute-start | bytes 3538952 | tf_op jit(solution)/shard_map/ppermute | solution.py:62
  141.7 30.9 %collective-permute-start.27 = (bf16[64,1024]{1,0:T(8,128)(2,1)S(1)}, bf16[64,1024]{1,0:T(8,128)(2,1)}, u32[]{:S(2)}, u32[]{:S(2)}) collective-permute-start(bf16[64,1024]{1,0:T(8,128)(2,1)S(1)} %add_convert_fusion.8), channel_id=1, source_target_pairs={{0,12},{4,0},{8,4},{12,8},{16,28},{20,16},{24,20},{28,24},{32,44},... | collective-permute-start | bytes 393224 | tf_op jit(solution)/shard_map/ppermute | solution.py:26
  142.2 30.4 %collective-permute-start.26 = (bf16[64,1024]{1,0:T(8,128)(2,1)S(1)}, bf16[64,1024]{1,0:T(8,128)(2,1)}, u32[]{:S(2)}, u32[]{:S(2)}) collective-permute-start(bf16[64,1024]{1,0:T(8,128)(2,1)S(1)} %add_convert_fusion.8), channel_id=1, source_target_pairs={{0,8},{4,12},{8,0},{12,4},{16,24},{20,28},{24,16},{28,20},{32,40},... | collective-permute-start | bytes 393224 | tf_op jit(solution)/shard_map/ppermute | solution.py:26
  268.2 28.3 %collective-permute-start.58 = (bf16[1024,1024]{0,1:T(8,128)(2,1)}, bf16[1024,1024]{0,1:T(8,128)(2,1)}, u32[]{:S(2)}, u32[]{:S(2)}) collective-permute-start(bf16[1024,1024]{0,1:T(8,128)(2,1)} %copy.53), channel_id=1, source_target_pairs={{0,64},{64,0},{1,65},{65,1},{2,66},{66,2},{3,67},{67,3},{4,68},{68... | collective-permute-start | bytes 6291464 | tf_op jit(solution)/shard_map/ppermute | solution.py:62
  301.4 128.6 %all-reduce.9.cloned.1.call-start = ((), (), s32[]{:S(2)}) async-start(), calls=%async_computation.7 | async-start | bytes 1048576 | tf_op jit(solution)/shard_map/psum | solution.py:624
  318.1 21.3 %collective-permute-start.63 = (bf16[1024,128]{1,0:T(8,128)(2,1)S(1)}, bf16[1024,128]{1,0:T(8,128)(2,1)S(1)}, u32[]{:S(2)}, u32[]{:S(2)}) collective-permute-start(bf16[1024,128]{1,0:T(8,128)(2,1)S(1)} %get-tuple-element.64), channel_id=1, source_target_pairs={{2,0},{3,1},{6,4},{7,5},{10,8},{11,9},{14,12},{15,13},{18,16},{19,... | collective-permute-start | bytes 786440 | tf_op jit(solution)/shard_map/ppermute | solution.py:42
  319.4 25.0 %collective-permute-start.64 = (bf16[1024,128]{1,0:T(8,128)(2,1)S(1)}, bf16[1024,128]{1,0:T(8,128)(2,1)S(1)}, u32[]{:S(2)}, u32[]{:S(2)}) collective-permute-start(bf16[1024,128]{1,0:T(8,128)(2,1)S(1)} %get-tuple-element.65), channel_id=1, source_target_pairs={{3,0},{7,4},{11,8},{15,12},{19,16},{23,20},{27,24},{31,28},{35,32}... | collective-permute-start | bytes 786440 | tf_op jit(solution)/shard_map/ppermute | solution.py:42
  372.0 103.5 %reduce-scatter.8.cloned.1.call-start = ((), (), s32[]{:S(2)}) async-start(), calls=%async_computation.9 | async-start | bytes 1310720 | tf_op jit(solution)/shard_map/reduce_scatter | solution.py:590
  398.2 26.8 %collective-permute-start.81 = (bf16[1024,1024]{0,1:T(8,128)(2,1)}, bf16[1024,1024]{0,1:T(8,128)(2,1)}, u32[]{:S(2)}, u32[]{:S(2)}) collective-permute-start(bf16[1024,1024]{0,1:T(8,128)(2,1)} %copy.55), channel_id=1, source_target_pairs={{0,64},{64,0},{1,65},{65,1},{2,66},{66,2},{3,67},{67,3},{4,68},{68... | collective-permute-start | bytes 6291464 | tf_op jit(solution)/shard_map/ppermute | solution.py:62
  398.2 77.3 %reduce-scatter.6.cloned.1.call-start = ((), (), s32[]{:S(2)}) async-start(), calls=%async_computation.8 | async-start | bytes 2621440 | tf_op jit(solution)/shard_map/reduce_scatter | solution.py:590
  430.0 95.5 %all-reduce.11.cloned.1.call-start = ((), (), s32[]{:S(2)}) async-start(), calls=%async_computation.10 | async-start | bytes 1572864 | tf_op jit(solution)/shard_map/psum | solution.py:645
  436.0 73.5 %collective-permute-start.94 = (bf16[64,1024]{1,0:T(8,128)(2,1)}, bf16[64,1024]{1,0:T(8,128)(2,1)}, u32[]{:S(2)}, u32[]{:S(2)}) collective-permute-start(bf16[64,1024]{1,0:T(8,128)(2,1)} %get-tuple-element.203), channel_id=1, source_target_pairs={{0,12},{4,0},{8,4},{12,8},{16,28},{20,16},{24,20},{28,24},{32,44},... | collective-permute-start | bytes 393224 | tf_op jit(solution)/shard_map/ppermute | solution.py:26
  438.7 72.3 %collective-permute-start.96 = (bf16[64,1024]{1,0:T(8,128)(2,1)}, bf16[64,1024]{1,0:T(8,128)(2,1)}, u32[]{:S(2)}, u32[]{:S(2)}) collective-permute-start(bf16[64,1024]{1,0:T(8,128)(2,1)} %get-tuple-element.204), channel_id=1, source_target_pairs={{0,4},{4,8},{8,12},{12,0},{16,20},{20,24},{24,28},{28,16},{32,36},... | collective-permute-start | bytes 393224 | tf_op jit(solution)/shard_map/ppermute | solution.py:26
  512.4 16.6 %collective-permute-start.97 = (f32[64,1024]{1,0:T(8,128)S(1)}, f32[64,1024]{1,0:T(8,128)S(1)}, u32[]{:S(2)}, u32[]{:S(2)}) collective-permute-start(f32[64,1024]{1,0:T(8,128)S(1)} %broadcast_select_fusion.12), channel_id=1, source_target_pairs={{0,64},{64,0},{1,65},{65,1},{2,66},{66,2},{3,67},{67,3},{4,68},{68... | collective-permute-start | bytes 786440 | tf_op jit(solution)/shard_map/ppermute | solution.py:62
  (242 other events, 2105.1 us)
Sparse Core Ops, SparseCore 0:
  12.3 36.9 all-gather.5
  51.5 37.2 all-gather.7
  91.0 36.0 all-gather.3
  301.6 35.3 reduce-scatter.3
  372.1 40.1 all-reduce.8
  414.7 24.0 reduce-scatter.7
  441.2 29.3 reduce-scatter.5
  480.6 43.7 all-reduce.10

commit v7 on v4

--- a/solution.py
+++ b/solution.py
@@ -107,7 +107,7 @@
         - jnp.mean(part, axis=-1, keepdims=True)
         - unit * jnp.mean(part * unit, axis=-1, keepdims=True)
     )
-    return back, jnp.sum(grad * unit, axis=0, keepdims=True), jnp.sum(grad, axis=0, keepdims=True)
+    return back, jnp.sum(grad * unit, axis=0), jnp.sum(grad, axis=0)
 
 
 def local_dot(left, right):
@@ -140,14 +140,14 @@
     return jnp.where(place >= start_two, start_two, jnp.where(place >= start_one, start_one, 0))
 
 
-def tile_bounds(scalar_ref, pair, rows_all):
+def tile_bounds(scalar_ref, indices, rows_all):
     block, x_here, _, start_one, start_two = [scalar_ref[i] for i in range(5)]
     least, most = [], []
-    for part in range(2):
-        place = block * rows_all + ((x_here + pair * 2 + part) & 3) * TILE
+    for index in indices:
+        place = block * rows_all + ((x_here + index) & 3) * TILE
         least.append(first_of_document(place, start_one, start_two))
         most.append(first_of_document(place + TILE - 1, start_one, start_two))
-    return jnp.minimum(*least), jnp.maximum(*most)
+    return functools.reduce(jnp.minimum, least), functools.reduce(jnp.maximum, most)
 
 
 def tile_limits(scalar_ref, index, rows_all):
@@ -181,8 +181,8 @@
 
         @pl.loop(0, tiles // 2)
         def _(pair, d=d, start=start):
-            least, most = tile_bounds(scalar_ref, pair, rows_all)
             indices = [pair * 2, pair * 2 + 1]
+            least, most = tile_bounds(scalar_ref, indices, rows_all)
 
             def step(masked):
                 key_values = own_ref[:, 0:128] if d == 0 else held[d - 1]
@@ -257,10 +257,10 @@
             start = (block - d) * rows_all
             key_sum[...] = jnp.zeros_like(key_sum)
 
-            @pl.loop(0, tiles // 2)
-            def _(pair):
-                least, most = tile_bounds(scalar_ref, pair, rows_all)
-                indices = [pair * 2, pair * 2 + 1]
+            @pl.loop(0, tiles)
+            def _(index):
+                indices = [index]
+                least, most = tile_bounds(scalar_ref, indices, rows_all)
 
                 def step(masked):
                     key_values = own_ref[:, 0:128] if d == 0 else held[d - 1]
@@ -356,18 +356,14 @@
 X_GROUPS = [[x * SIDE + z for x in range(SIDE)] for z in range(SIDE)]
 
 
-def forward_attention(residual, normed_all, spots, vectors, bias_qkv, w_heads, w_back, early=None):
+def forward_attention(residual, normed_all, spots, vectors, bias_qkv, w_heads, w_back):
     b_out = vectors[2]
     projected = ((nt_dot(normed_all, w_heads) + bias_qkv) * spots["scale"]).astype(LOW)
     width = projected.shape[1] // SIDE
     pieces = [projected[:, d * width : (d + 1) * width] for d in range(SIDE)]
     own = jnp.concatenate([pieces[0]] + [move_x(pieces[d], -d) for d in range(1, SIDE)], axis=0)
-    if early is not None:
-        own, early = tie(own, early)
     others = [move_y_open(own[:, 0:128], d) for d in range(1, SIDE)]
     kept = attend(spots, own, others)
-    if early is not None:
-        kept, early = tie(kept, gather_z(early))
     lanes = lax.broadcasted_iota(jnp.int32, kept.shape, 1)
     mixed = jnp.where(lanes < HEAD_DIM, 0.0, kept).astype(LOW)
     rows = mixed.shape[0] // SIDE
@@ -375,7 +371,7 @@
         [mixed[0:rows]] + [move_x(mixed[d * rows : (d + 1) * rows], d) for d in range(1, SIDE)], axis=1
     )
     hidden = residual + (scatter_z(local_dot(mixed_rows, w_back).astype(LOW)) + b_out)
-    return hidden, (residual, normed_all, own, others, kept, mixed_rows), early
+    return hidden, (residual, normed_all, own, others, kept, mixed_rows)
 
 
 def forward_hidden_units(hidden, vectors, b_up, w_up, w_down):
@@ -391,7 +387,7 @@
     hidden, normed_two_all, up_value, activated = stored
     gain_two = vectors[3]
     grad_down = grad_out.astype(LOW)
-    g_b_down = jnp.sum(grad_down.astype(FULL), axis=0, keepdims=True)
+    g_b_down = jnp.sum(grad_down.astype(FULL), axis=0)
     _, gelu_pull = jax.vjp(jax.nn.gelu, up_value)
     (grad_up,) = gelu_pull(nt_dot(grad_down_all, w_down))
     grad_up = grad_up.astype(LOW)
@@ -407,7 +403,7 @@
 def backward_mixed(grad_hidden, stored, w_back, spots):
     mixed_rows = stored[5]
     grad_attn = grad_hidden.astype(LOW)
-    g_b_out = jnp.sum(grad_attn.astype(FULL), axis=0, keepdims=True)
+    g_b_out = jnp.sum(grad_attn.astype(FULL), axis=0)
     grad_attn_all = gather_z(grad_attn)
     grad_mixed = (nt_dot(grad_attn_all, w_back) * spots["upper"]).astype(LOW)
     pieces = [grad_mixed[:, d * 128 : (d + 1) * 128] for d in range(SIDE)]
@@ -520,7 +516,7 @@
     half, normed = tie(half_heads(0), normed)
     mine = jnp.stack([half] + [move_x(half, d) for d in range(1, SIDE)])
     half = owner(0, up_own, down_other)
-    normed_all, mine, half = tie(gather_z(normed), mine, half)
+    normed_all, mine, half, grad_last_all = tie(gather_z(normed), mine, half, gather_z(grad_last_all))
     heads_first, bias_heads_first, bias_up_first = join_heads(0, mine, swap(mine))
     units_first = gather_whole(half)
     heads_last = gather_whole(half_heads(1)).reshape(SIDE, -1, model_width)
@@ -537,8 +533,8 @@
         "upper": (jnp.arange(SIDE * 128) % 128 >= HEAD_DIM).astype(FULL),
     }
 
-    hidden, kept_heads_first, grad_last_all = forward_attention(
-        sequence, normed_all, spots, vectors[0], bias_heads_first, *heads_first, grad_last_all
+    hidden, kept_heads_first = forward_attention(
+        sequence, normed_all, spots, vectors[0], bias_heads_first, *heads_first
     )
     units_first = join_units(0, units_first)
     middle, kept_units_first = forward_hidden_units(hidden, vectors[0], bias_up_first, *units_first)
@@ -547,7 +543,7 @@
     heads_last, bias_heads_last, bias_up_last = join_heads(1, mine, theirs)
     middle = middle.astype(LOW).astype(FULL)
     normed_all = gather_z(layer_norm(middle, *vectors[1][0:2]).astype(LOW))
-    hidden, kept_heads_last, _ = forward_attention(
+    hidden, kept_heads_last = forward_attention(
         middle, normed_all, spots, vectors[1], bias_heads_last, *heads_last
     )
     units_last = join_units(1, units_last)
@@ -576,7 +572,7 @@
         )
         return jnp.concatenate(
             [
-                *heads, g_b_out, *units,
+                jnp.stack([*heads, g_b_out, *units]),
                 jnp.concatenate([by_turn, g_b_qkv.reshape(SIDE, TILE)], axis=1).reshape(2, -1),
             ],
             axis=0,
@@ -619,8 +615,8 @@
     gain_one, bias_one = vectors[0][0:2]
     residual, normed_all = kept_heads_first[0:2]
     grad_normed = local_dot(grad_qkv, heads_first[0])
-    g_bias_one = jnp.sum(grad_normed, axis=0, keepdims=True)
-    g_gain_one = jnp.sum(grad_normed * ((normed_all.astype(FULL) - bias_one) / gain_one), axis=0, keepdims=True)
+    g_bias_one = jnp.sum(grad_normed, axis=0)
+    g_gain_one = jnp.sum(grad_normed * ((normed_all.astype(FULL) - bias_one) / gain_one), axis=0)
     g_b_qkv_first = jnp.sum(grad_qkv.astype(FULL), axis=0)
     sums_first = pack_vectors(
         (g_gain_one, g_bias_one), vec_units_first, g_b_out_first, g_b_up_first, g_b_qkv_first
@@ -639,6 +635,7 @@
     packs = [
         jnp.concatenate(
             [
+                halves[d],
                 common,
                 jnp.pad(split[d], ((0, 0), (0, model_width - 512))),
                 jnp.zeros((9, model_width), LOW),
@@ -647,8 +644,7 @@
         )
         for d in range(SIDE)
     ]
-    pack = jnp.concatenate([even_pairs(halves, move_x), even_pairs(packs, move_x)], axis=0)
-    pack = even_sum(pack.astype(LOW), move_y)
+    pack = even_sum(even_pairs(packs, move_x).astype(LOW), move_y)
     pack, units_sum_first, units_sum_last, heads_sum_last = tie(
         pack, units_sum_first, units_sum_last, heads_sum_last
     )

time: 503 us -> 500 us (level)
  starting transfers between devices: 144 us -> 138 us
    another operation x1 -> x13, local copies, waits for them, and re-layouts: 0.01 us -> 9.34 us  [the longest x12 9.34 us: pack_vectors(): jnp.stack([*heads, g_b_out, *units])]
    broadcast_in_dim x12 -> x0, local copies, waits for them, and re-layouts: 9.27 us -> none  [the longest x3 3.08 us: layer_norm_back(): jnp.sum(grad * unit, axis=0, keepdims=True)]
    ppermute x33 -> x30, starting transfers between devices: 48.9 us -> 40.6 us  [move_x(): return lax.ppermute(block, 'tensor', route)]
    ppermute x33 -> x30, waiting for transfers between devices: 69.6 us -> 75.3 us  [move_x(): return lax.ppermute(block, 'tensor', route)]
  transfers between devices with their start and end apart: 118 -> 115, of which waited for: 70 -> 73; matrix products, arithmetic and copies ran while one was open for 20% -> 21% of each run, Pallas kernels for 3% -> 3%
where the time goes in v7:
time: 500 us; the launch traced here: 491 us
  waiting for transfers between devices  201 us (40%)
  starting transfers between devices  138 us (28%)
  other arithmetic  51.2 us (10%)
  matrix products  35.9 us (7%)
  local copies, waits for them, and re-layouts  28.9 us (6%)
  Pallas kernels  19.6 us (4%)
  between operations  17 us (3%)
    ppermute x30, waiting for transfers between devices, move_x(): return lax.ppermute(block, 'tensor', route)  75.3 us
    ppermute x48, waiting for transfers between devices, move_z(): return lax.ppermute(block, 'tensor', route)  68.6 us
    ppermute x48, starting transfers between devices, move_z(): return lax.ppermute(block, 'tensor', route)  61.2 us
    ppermute x30, starting transfers between devices, move_x(): return lax.ppermute(block, 'tensor', route)  40.6 us
    ppermute x12, waiting for transfers between devices, move_y_open(): return lax.ppermute(block, 'ctx', route)  33.2 us
    ppermute x12, starting transfers between devices, move_y_open(): return lax.ppermute(block, 'ctx', route)  30.1 us
    dot_general x8, matrix products, local_dot(): return jnp.dot(left, right, preferred_element_type=FULL)  14.3 us
    ppermute x3, waiting for transfers between devices, move_y(): lax.ppermute(block, 'ctx', [(y, (y + distance) % SIDE) for y in range(SID...  13.2 us
  transfers between devices with their start and end apart: 115, of which 73 were waited for; matrix products, arithmetic and copies ran while one was open for 21% of the time, Pallas kernels for 3%

profile of v7, /device:TPU:0, one launch (start us, length us, event | category | flops | bytes accessed | tf_op | source)
XLA Modules:
  0.0 491.0 jit_solution(8220435478529168879)
XLA Ops:
  8.8 4.1 collective-permute-start.11
  36.5 7.8 %collective-permute-done.7 = bf16[144,1024]{1,0:T(8,128)(2,1)S(1)} collective-permute-done((bf16[144,1024]{1,0:T(8,128)(2,1)S(1)}, bf16[144,1024]{1,0:T(8,128)(2,1)S(1)}, u32[]{:S(2)}, u32[]{:S(2)}) %collective-permute-start.7) | collective-permute-done | bytes 294944 | tf_op jit(solution)/shard_map/ppermute | solution.py:33
  57.3 6.7 %collective-permute-done.15 = bf16[256,256]{1,0:T(8,128)(2,1)S(1)} collective-permute-done((bf16[256,256]{1,0:T(8,128)(2,1)S(1)}, bf16[256,256]{1,0:T(8,128)(2,1)S(1)}, u32[]{:S(2)}, u32[]{:S(2)}) %collective-permute-start.15) | collective-permute-done | bytes 131104 | tf_op jit(solution)/shard_map/ppermute | solution.py:33
  66.6 5.2 %collective-permute-start.18 = (bf16[1024,128]{1,0:T(8,128)(2,1)S(1)}, bf16[1024,128]{1,0:T(8,128)(2,1)S(1)}, u32[]{:S(2)}, u32[]{:S(2)}) collective-permute-start(bf16[1024,128]{1,0:T(8,128)(2,1)S(1)} %slice.557), channel_id=1, source_target_pairs={{0,3},{4,7},{8,11},{12,15},{16,19},{20,23},{24,27},{28,31},{32,35}... | collective-permute-start | bytes 786440 | tf_op jit(solution)/shard_map/ppermute | solution.py:42
  109.6 3.9 collective-permute-done.23
  153.2 6.7 %collective-permute-done.38 = bf16[256,256]{1,0:T(8,128)(2,1)S(1)} collective-permute-done((bf16[256,256]{1,0:T(8,128)(2,1)S(1)}, bf16[256,256]{1,0:T(8,128)(2,1)S(1)}, u32[]{:S(2)}, u32[]{:S(2)}) %collective-permute-start.38) | collective-permute-done | bytes 131104 | tf_op jit(solution)/shard_map/ppermute | solution.py:33
  165.0 8.8 %collective-permute-start.41 = (bf16[1024,128]{1,0:T(8,128)(2,1)S(1)}, bf16[1024,128]{1,0:T(8,128)(2,1)S(1)}, u32[]{:S(2)}, u32[]{:S(2)}) collective-permute-start(bf16[1024,128]{1,0:T(8,128)(2,1)S(1)} %slice.586), channel_id=1, source_target_pairs={{0,3},{4,7},{8,11},{12,15},{16,19},{20,23},{24,27},{28,31},{32,35}... | collective-permute-start | bytes 786440 | tf_op jit(solution)/shard_map/ppermute | solution.py:42
  198.9 4.1 collective-permute-done.47
  226.8 4.0 collective-permute-done.54
  250.9 6.7 %attend_back.2 = (bf16[1024,128]{1,0:T(8,128)(2,1)S(1)}, bf16[1024,128]{1,0:T(8,128)(2,1)S(1)}, bf16[1024,128]{1,0:T(8,128)(2,1)}, bf16[1024,128]{1,0:T(8,128)(2,1)}, bf16[1024,128]{1,0:T(8,128)(2,1)}) custom-call(s32[5]{0:T(128)S(1)} %stack.142.scalar_ref, bf16[1024,256]{1,0:T(8,128)(2,1)S(1)} %pad_maximum_fusion.14.own_ref, ...), custom_call_target="tpu_custom_call" | custom-call | flops 2684354560 | bytes 6291456 | tf_op jit(solution)/shard_map/attend_back/pallas_call | solution.py:331
  263.8 7.3 %collective-permute-done.62 = bf16[1024,128]{1,0:T(8,128)(2,1)S(1)} collective-permute-done((bf16[1024,128]{1,0:T(8,128)(2,1)}, bf16[1024,128]{1,0:T(8,128)(2,1)S(1)}, u32[]{:S(2)}, u32[]{:S(2)}) %collective-permute-start.62) | collective-permute-done | bytes 262176 | tf_op jit(solution)/shard_map/ppermute | solution.py:42
  271.1 8.8 %collective-permute-done.63 = bf16[1024,128]{1,0:T(8,128)(2,1)S(1)} collective-permute-done((bf16[1024,128]{1,0:T(8,128)(2,1)}, bf16[1024,128]{1,0:T(8,128)(2,1)S(1)}, u32[]{:S(2)}, u32[]{:S(2)}) %collective-permute-start.63) | collective-permute-done | bytes 262176 | tf_op jit(solution)/shard_map/ppermute | solution.py:42
  279.9 5.1 %collective-permute-done.64 = bf16[1024,128]{1,0:T(8,128)(2,1)S(1)} collective-permute-done((bf16[1024,128]{1,0:T(8,128)(2,1)}, bf16[1024,128]{1,0:T(8,128)(2,1)S(1)}, u32[]{:S(2)}, u32[]{:S(2)}) %collective-permute-start.64) | collective-permute-done | bytes 262176 | tf_op jit(solution)/shard_map/ppermute | solution.py:42
  290.9 4.7 collective-permute-done.65
  295.7 5.3 %collective-permute-done.66 = bf16[256,256]{1,0:T(8,128)(2,1)S(1)} collective-permute-done((bf16[256,256]{1,0:T(8,128)(2,1)S(1)}, bf16[256,256]{1,0:T(8,128)(2,1)S(1)}, u32[]{:S(2)}, u32[]{:S(2)}) %collective-permute-start.66) | collective-permute-done | bytes 131104 | tf_op jit(solution)/shard_map/ppermute | solution.py:33
  339.8 4.0 collective-permute-done.77
  344.8 4.5 add_convert_fusion
  373.7 5.7 %attend_back.3 = (bf16[1024,128]{1,0:T(8,128)(2,1)S(1)}, bf16[1024,128]{1,0:T(8,128)(2,1)S(1)}, bf16[1024,128]{1,0:T(8,128)(2,1)S(1)}, bf16[1024,128]{1,0:T(8,128)(2,1)S(1)}, bf16[1024,128]{1,0:T(8,128)(2,1)S(1)}) custom-call(s32[5]{0:T(128)S(1)} %stack.142.scalar_ref, bf16[1024,256]{1,0:T(8,128)(2,1)S(1)} %pad_maximum_fusion.11.own_ref, ...), custom_call_target="tpu_custom_call" | custom-call | flops 2684354560 | bytes 6291456 | tf_op jit(solution)/shard_map/attend_back/pallas_call | solution.py:331
  379.4 5.4 %reduce-scatter.6.cloned.1.call-done = bf16[256,1024]{1,0:T(8,128)(2,1)} async-done(((bf16[1024,1024]{1,0:T(8,128)(2,1)}), bf16[256,1024]{1,0:T(8,128)(2,1)}) %reduce-scatter.6.cloned.1.call-update) | async-done | bytes 524304 | tf_op jit(solution)/shard_map/reduce_scatter | solution.py:559
  398.8 4.4 collective-permute-done.87
  445.3 5.5 %collective-permute-done.100 = bf16[144,1024]{1,0:T(8,128)(2,1)S(1)} collective-permute-done((bf16[144,1024]{1,0:T(8,128)(2,1)S(1)}, bf16[144,1024]{1,0:T(8,128)(2,1)S(1)}, u32[]{:S(2)}, u32[]{:S(2)}) %collective-permute-start.100) | collective-permute-done | bytes 294944 | tf_op jit(solution)/shard_map/ppermute | solution.py:33
  450.8 6.3 %collective-permute-done.101 = bf16[144,1024]{1,0:T(8,128)(2,1)S(1)} collective-permute-done((bf16[144,1024]{1,0:T(8,128)(2,1)S(1)}, bf16[144,1024]{1,0:T(8,128)(2,1)S(1)}, u32[]{:S(2)}, u32[]{:S(2)}) %collective-permute-start.101) | collective-permute-done | bytes 294944 | tf_op jit(solution)/shard_map/ppermute | solution.py:33
  460.8 6.6 %collective-permute-done.105 = bf16[144,1024]{1,0:T(8,128)(2,1)S(1)} collective-permute-done((bf16[144,1024]{1,0:T(8,128)(2,1)S(1)}, bf16[144,1024]{1,0:T(8,128)(2,1)S(1)}, u32[]{:S(2)}, u32[]{:S(2)}) %collective-permute-start.105) | collective-permute-done | bytes 294944 | tf_op jit(solution)/shard_map/ppermute | solution.py:37
  467.3 6.6 %collective-permute-done.104 = bf16[144,1024]{1,0:T(8,128)(2,1)S(1)} collective-permute-done((bf16[144,1024]{1,0:T(8,128)(2,1)S(1)}, bf16[144,1024]{1,0:T(8,128)(2,1)S(1)}, u32[]{:S(2)}, u32[]{:S(2)}) %collective-permute-start.104) | collective-permute-done | bytes 294944 | tf_op jit(solution)/shard_map/ppermute | solution.py:37
  (648 shorter events, 335.8 us)
Async XLA Ops:
  7.2 79.0 %all-gather.4.cloned.1.call-start = ((), (), s32[]{:S(2)}) async-start(), calls=%async_computation.3 | async-start | bytes 2621440 | tf_op jit(solution)/shard_map/all_gather | solution.py:505
  8.8 16.6 %collective-permute-start.11 = (bf16[64,1024]{1,0:T(8,128)(2,1)S(1)}, bf16[64,1024]{1,0:T(8,128)(2,1)S(1)}, u32[]{:S(2)}, u32[]{:S(2)}) collective-permute-start(bf16[64,1024]{1,0:T(8,128)(2,1)S(1)} %get-tuple-element.245), channel_id=1, source_target_pairs={{0,12},{4,0},{8,4},{12,8},{16,28},{20,16},{24,20},{28,24},{32,44},... | collective-permute-start | bytes 393224 | tf_op jit(solution)/shard_map/ppermute | solution.py:26
  13.0 14.8 %collective-permute-start.10 = (bf16[64,1024]{1,0:T(8,128)(2,1)S(1)}, bf16[64,1024]{1,0:T(8,128)(2,1)S(1)}, u32[]{:S(2)}, u32[]{:S(2)}) collective-permute-start(bf16[64,1024]{1,0:T(8,128)(2,1)S(1)} %get-tuple-element.245), channel_id=1, source_target_pairs={{0,8},{4,12},{8,0},{12,4},{16,24},{20,28},{24,16},{28,20},{32,40},... | collective-permute-start | bytes 393224 | tf_op jit(solution)/shard_map/ppermute | solution.py:26
  13.0 15.1 %collective-permute-start.9 = (bf16[64,1024]{1,0:T(8,128)(2,1)S(1)}, bf16[64,1024]{1,0:T(8,128)(2,1)S(1)}, u32[]{:S(2)}, u32[]{:S(2)}) collective-permute-start(bf16[64,1024]{1,0:T(8,128)(2,1)S(1)} %get-tuple-element.245), channel_id=1, source_target_pairs={{0,4},{4,8},{8,12},{12,0},{16,20},{20,24},{24,28},{28,16},{32,36},... | collective-permute-start | bytes 393224 | tf_op jit(solution)/shard_map/ppermute | solution.py:26
  28.9 15.5 %collective-permute-start.7 = (bf16[144,1024]{1,0:T(8,128)(2,1)S(1)}, bf16[144,1024]{1,0:T(8,128)(2,1)S(1)}, u32[]{:S(2)}, u32[]{:S(2)}) collective-permute-start(bf16[144,1024]{1,0:T(8,128)(2,1)S(1)} %get-tuple-element.56), channel_id=1, source_target_pairs={{0,48},{4,52},{8,56},{12,60},{16,0},{20,4},{24,8},{28,12},{32,16},... | collective-permute-start | bytes 884744 | tf_op jit(solution)/shard_map/ppermute | solution.py:33
  48.2 59.8 %all-gather.6.cloned.1.call-start = ((), (), s32[]{:S(2)}) async-start(), calls=%async_computation.4 | async-start | bytes 1474560 | tf_op jit(solution)/shard_map/all_gather | solution.py:505
  49.0 129.0 %all-gather.8.cloned.1.call-start = ((), (), s32[]{:S(2)}) async-start(), calls=%async_computation.5 | async-start | bytes 2621440 | tf_op jit(solution)/shard_map/all_gather | solution.py:505
  86.2 38.6 %collective-permute-start.28 = (bf16[1024,1024]{1,0:T(8,128)(2,1)}, bf16[1024,1024]{1,0:T(8,128)(2,1)}, u32[]{:S(2)}, u32[]{:S(2)}) collective-permute-start(bf16[1024,1024]{1,0:T(8,128)(2,1)} %all-gather.4.cloned.1.call-done), channel_id=1, source_target_pairs={{0,64},{64,0},{1,65},{65,1},{2,66},{66,2},{3,67},{67,3},{4,68},{68... | collective-permute-start | bytes 6291464 | tf_op jit(solution)/shard_map/ppermute | solution.py:62
  119.4 19.1 %collective-permute-start.32 = (bf16[4,144,1024]{2,1,0:T(8,128)(2,1)}, bf16[4,144,1024]{2,1,0:T(8,128)(2,1)}, u32[]{:S(2)}, u32[]{:S(2)}) collective-permute-start(bf16[4,144,1024]{2,1,0:T(8,128)(2,1)} %pad_maximum_fusion.3), channel_id=1, source_target_pairs={{0,64},{64,0},{1,65},{65,1},{2,66},{66,2},{3,67},{67,3},{4,68},{68... | collective-permute-start | bytes 3538952 | tf_op jit(solution)/shard_map/ppermute | solution.py:62
  131.4 213.4 %reduce-scatter.4.cloned.1.call-start = ((), (), s32[]{:S(2)}) async-start(), calls=%async_computation.6 | async-start | bytes 2621440 | tf_op jit(solution)/shard_map/reduce_scatter | solution.py:559
  165.0 15.5 %collective-permute-start.41 = (bf16[1024,128]{1,0:T(8,128)(2,1)S(1)}, bf16[1024,128]{1,0:T(8,128)(2,1)S(1)}, u32[]{:S(2)}, u32[]{:S(2)}) collective-permute-start(bf16[1024,128]{1,0:T(8,128)(2,1)S(1)} %slice.586), channel_id=1, source_target_pairs={{0,3},{4,7},{8,11},{12,15},{16,19},{20,23},{24,27},{28,31},{32,35}... | collective-permute-start | bytes 786440 | tf_op jit(solution)/shard_map/ppermute | solution.py:42
  178.0 30.4 %collective-permute-start.48 = (bf16[1024,1024]{1,0:T(8,128)(2,1)}, bf16[1024,1024]{1,0:T(8,128)(2,1)S(1)}, u32[]{:S(2)}, u32[]{:S(2)}) collective-permute-start(bf16[1024,1024]{1,0:T(8,128)(2,1)} %all-gather.8.cloned.1.call-done), channel_id=1, source_target_pairs={{0,64},{64,0},{1,65},{65,1},{2,66},{66,2},{3,67},{67,3},{4,68},{68... | collective-permute-start | bytes 6291464 | tf_op jit(solution)/shard_map/ppermute | solution.py:62
  258.9 21.0 %collective-permute-start.63 = (bf16[1024,128]{1,0:T(8,128)(2,1)}, bf16[1024,128]{1,0:T(8,128)(2,1)S(1)}, u32[]{:S(2)}, u32[]{:S(2)}) collective-permute-start(bf16[1024,128]{1,0:T(8,128)(2,1)} %get-tuple-element.69), channel_id=1, source_target_pairs={{2,0},{3,1},{6,4},{7,5},{10,8},{11,9},{14,12},{15,13},{18,16},{19,... | collective-permute-start | bytes 786440 | tf_op jit(solution)/shard_map/ppermute | solution.py:42
  260.2 24.8 %collective-permute-start.64 = (bf16[1024,128]{1,0:T(8,128)(2,1)}, bf16[1024,128]{1,0:T(8,128)(2,1)S(1)}, u32[]{:S(2)}, u32[]{:S(2)}) collective-permute-start(bf16[1024,128]{1,0:T(8,128)(2,1)} %get-tuple-element.70), channel_id=1, source_target_pairs={{3,0},{7,4},{11,8},{15,12},{19,16},{23,20},{27,24},{31,28},{35,32}... | collective-permute-start | bytes 786440 | tf_op jit(solution)/shard_map/ppermute | solution.py:42
  263.8 115.6 %reduce-scatter.8.cloned.1.call-start = ((), (), s32[]{:S(2)}) async-start(), calls=%async_computation.8 | async-start | bytes 1310720 | tf_op jit(solution)/shard_map/reduce_scatter | solution.py:559
  305.2 16.5 %collective-permute-start.74 = (bf16[4,128,1024]{2,1,0:T(8,128)(2,1)S(1)}, bf16[4,128,1024]{2,1,0:T(8,128)(2,1)S(1)}, u32[]{:S(2)}, u32[]{:S(2)}) collective-permute-start(bf16[4,128,1024]{2,1,0:T(8,128)(2,1)S(1)} %get-tuple-element.165), channel_id=1, source_target_pairs={{0,64},{64,0},{1,65},{65,1},{2,66},{66,2},{3,67},{67,3},{4,68},{68... | collective-permute-start | bytes 3145736 | tf_op jit(solution)/shard_map/ppermute | solution.py:62
  329.4 15.4 %collective-permute-start.78 = (bf16[1024,1024]{1,0:T(8,128)(2,1)}, bf16[1024,1024]{1,0:T(8,128)(2,1)}, u32[]{:S(2)}, u32[]{:S(2)}) collective-permute-start(bf16[1024,1024]{1,0:T(8,128)(2,1)} %get-tuple-element.161), channel_id=1, source_target_pairs={{0,64},{64,0},{1,65},{65,1},{2,66},{66,2},{3,67},{67,3},{4,68},{68... | collective-permute-start | bytes 6291464 | tf_op jit(solution)/shard_map/ppermute | solution.py:62
  331.0 53.7 %reduce-scatter.6.cloned.1.call-start = ((), (), s32[]{:S(2)}) async-start(), calls=%async_computation.7 | async-start | bytes 2621440 | tf_op jit(solution)/shard_map/reduce_scatter | solution.py:559
  349.4 124.8 %all-reduce.8.cloned.1.call-start = ((), (), s32[]{:S(2)}) async-start(), calls=%async_computation.9 | async-start | bytes 2621440 | tf_op jit(solution)/shard_map/psum | solution.py:610
  367.7 75.7 %collective-permute-start.94 = (bf16[64,1024]{1,0:T(8,128)(2,1)}, bf16[64,1024]{1,0:T(8,128)(2,1)}, u32[]{:S(2)}, u32[]{:S(2)}) collective-permute-start(bf16[64,1024]{1,0:T(8,128)(2,1)} %get-tuple-element.198), channel_id=1, source_target_pairs={{0,12},{4,0},{8,4},{12,8},{16,28},{20,16},{24,20},{28,24},{32,44},... | collective-permute-start | bytes 393224 | tf_op jit(solution)/shard_map/ppermute | solution.py:26
  368.3 75.4 %collective-permute-start.96 = (bf16[64,1024]{1,0:T(8,128)(2,1)}, bf16[64,1024]{1,0:T(8,128)(2,1)}, u32[]{:S(2)}, u32[]{:S(2)}) collective-permute-start(bf16[64,1024]{1,0:T(8,128)(2,1)} %get-tuple-element.199), channel_id=1, source_target_pairs={{0,4},{4,8},{8,12},{12,0},{16,20},{20,24},{24,28},{28,16},{32,36},... | collective-permute-start | bytes 393224 | tf_op jit(solution)/shard_map/ppermute | solution.py:26
  387.3 15.8 %collective-permute-start.87 = (bf16[1024,128]{1,0:T(8,128)(2,1)S(1)}, bf16[1024,128]{1,0:T(8,128)(2,1)S(1)}, u32[]{:S(2)}, u32[]{:S(2)}) collective-permute-start(bf16[1024,128]{1,0:T(8,128)(2,1)S(1)} %get-tuple-element.88), channel_id=1, source_target_pairs={{3,0},{7,4},{11,8},{15,12},{19,16},{23,20},{27,24},{31,28},{35,32}... | collective-permute-start | bytes 786440 | tf_op jit(solution)/shard_map/ppermute | solution.py:42
  440.3 16.8 %collective-permute-start.101 = (bf16[144,1024]{1,0:T(8,128)(2,1)S(1)}, bf16[144,1024]{1,0:T(8,128)(2,1)S(1)}, u32[]{:S(2)}, u32[]{:S(2)}) collective-permute-start(bf16[144,1024]{1,0:T(8,128)(2,1)S(1)} %get-tuple-element.268), channel_id=1, source_target_pairs={{0,48},{4,52},{8,56},{12,60},{16,0},{20,4},{24,8},{28,12},{32,16},... | collective-permute-start | bytes 884744 | tf_op jit(solution)/shard_map/ppermute | solution.py:33
  458.4 15.6 %collective-permute-start.104 = (bf16[144,1024]{1,0:T(8,128)(2,1)S(1)}, bf16[144,1024]{1,0:T(8,128)(2,1)S(1)}, u32[]{:S(2)}, u32[]{:S(2)}) collective-permute-start(bf16[144,1024]{1,0:T(8,128)(2,1)S(1)} %add_convert_fusion.4), channel_id=1, source_target_pairs={{0,1},{1,2},{2,3},{3,0},{4,5},{5,6},{6,7},{7,4},{8,9},{9,10},{10,1... | collective-permute-start | bytes 884744 | tf_op jit(solution)/shard_map/ppermute | solution.py:37
  (205 other events, 1769.8 us)
Sparse Core Ops, SparseCore 0:
  48.3 32.2 all-gather.3
  82.9 25.1 all-gather.5
  131.5 40.9 all-gather.7
  263.9 46.3 reduce-scatter.3
  331.1 19.0 reduce-scatter.7
  352.5 32.2 reduce-scatter.5
  409.6 47.1 all-reduce.7

commit v8 on v7

--- a/solution.py
+++ b/solution.py
@@ -419,7 +419,10 @@
     dkv = dkv0.astype(FULL)
     for d, part in enumerate((dkv1, dkv2, dkv3), 1):
         dkv = dkv + move_y_open(part, -d).astype(FULL)
-    grad_own = jnp.concatenate([dkv.astype(LOW), dq], axis=1)
+    return jnp.concatenate([dkv.astype(LOW), dq], axis=1)
+
+
+def spread_heads(grad_own):
     rows = grad_own.shape[0] // SIDE
     return jnp.concatenate(
         [grad_own[0:rows]] + [move_x(grad_own[d * rows : (d + 1) * rows], d) for d in range(1, SIDE)],
@@ -584,7 +587,7 @@
     grad_hidden, units_kept, units_arrived = tie(grad_hidden, *swap_grads(1, g_up, g_down))
     units_sum_last = scatter_whole(add_grads(units_kept, units_arrived))
     grad_mixed, g_b_out_last, g_out = backward_mixed(grad_hidden, kept_heads_last, heads_last[1], spots)
-    grad_qkv = backward_heads(attend_back(spots, *kept_heads_last[2:5], grad_mixed))
+    grad_qkv = spread_heads(backward_heads(attend_back(spots, *kept_heads_last[2:5], grad_mixed)))
     grad_middle, vec_heads_last, g_b_qkv_last, g_heads = backward_entry(
         grad_qkv, grad_hidden, kept_heads_last, vectors[1], heads_last[0]
     )
@@ -606,11 +609,12 @@
     units_sum_first = scatter_whole(add_grads(units_kept, units_arrived))
     grad_mixed, g_b_out_first, g_out = backward_mixed(grad_hidden, kept_heads_first, heads_first[1], spots)
     parts = attend_back(spots, *kept_heads_first[2:5], grad_mixed)
-    parts, units_sum_first, heads_sum_last = tie(parts, units_sum_first, heads_sum_last)
+    grad_own = backward_heads(parts)
+    grad_own, units_sum_first, heads_sum_last = tie(grad_own, units_sum_first, heads_sum_last)
     units_sum_first, units_sum_last, heads_sum_last = lax.psum(
         (units_sum_first, units_sum_last, heads_sum_last), "ctx"
     )
-    grad_qkv = backward_heads(parts)
+    grad_qkv = spread_heads(grad_own)
 
     gain_one, bias_one = vectors[0][0:2]
     residual, normed_all = kept_heads_first[0:2]

time: 500 us -> 492 us (0.984)
  starting transfers between devices: 138 us -> 131 us
  waiting for transfers between devices: 201 us -> 206 us
    reduce_scatter x3, waiting for transfers between devices: 5.44 us -> 0.06 us  [scatter_whole(): lax.psum_scatter(grads, 'tensor', scatter_dimension=0, tiled=True, axis_i...]
  transfers between devices with their start and end apart: 115 -> 115, of which waited for: 73 -> 74; matrix products, arithmetic and copies ran while one was open for 21% -> 20% of each run, Pallas kernels for 3% -> 3%
where the time goes in v8:
time: 492 us; the launch traced here: 484 us
  waiting for transfers between devices  206 us (42%)
  starting transfers between devices  131 us (27%)
  other arithmetic  48.9 us (10%)
  matrix products  35 us (7%)
  local copies, waits for them, and re-layouts  25.9 us (5%)
  Pallas kernels  19.6 us (4%)
  between operations  17.2 us (3%)
    ppermute x30, waiting for transfers between devices, move_x(): return lax.ppermute(block, 'tensor', route)  78.2 us
    ppermute x48, waiting for transfers between devices, move_z(): return lax.ppermute(block, 'tensor', route)  71.8 us
    ppermute x48, starting transfers between devices, move_z(): return lax.ppermute(block, 'tensor', route)  56.7 us
    ppermute x30, starting transfers between devices, move_x(): return lax.ppermute(block, 'tensor', route)  38.9 us
    ppermute x12, waiting for transfers between devices, move_y_open(): return lax.ppermute(block, 'ctx', route)  37.9 us
    ppermute x12, starting transfers between devices, move_y_open(): return lax.ppermute(block, 'ctx', route)  30.2 us
    dot_general x8, matrix products, local_dot(): return jnp.dot(left, right, preferred_element_type=FULL)  14.3 us
    ppermute x3, waiting for transfers between devices, move_y(): lax.ppermute(block, 'ctx', [(y, (y + distance) % SIDE) for y in range(SID...  13.7 us
  transfers between devices with their start and end apart: 115, of which 74 were waited for; matrix products, arithmetic and copies ran while one was open for 20% of the time, Pallas kernels for 3%

profile of v8, /device:TPU:0, one launch (start us, length us, event | category | flops | bytes accessed | tf_op | source)
XLA Modules:
  0.0 484.0 jit_solution(741695151237863632)
XLA Ops:
  8.8 4.1 collective-permute-start.11
  36.5 7.9 %collective-permute-done.7 = bf16[144,1024]{1,0:T(8,128)(2,1)S(1)} collective-permute-done((bf16[144,1024]{1,0:T(8,128)(2,1)S(1)}, bf16[144,1024]{1,0:T(8,128)(2,1)S(1)}, u32[]{:S(2)}, u32[]{:S(2)}) %collective-permute-start.7) | collective-permute-done | bytes 294944 | tf_op jit(solution)/shard_map/ppermute | solution.py:33
  44.4 3.7 collective-permute-done.5
  57.3 6.8 %collective-permute-done.15 = bf16[256,256]{1,0:T(8,128)(2,1)S(1)} collective-permute-done((bf16[256,256]{1,0:T(8,128)(2,1)S(1)}, bf16[256,256]{1,0:T(8,128)(2,1)S(1)}, u32[]{:S(2)}, u32[]{:S(2)}) %collective-permute-start.15) | collective-permute-done | bytes 131104 | tf_op jit(solution)/shard_map/ppermute | solution.py:33
  66.7 5.2 %collective-permute-start.18 = (bf16[1024,128]{1,0:T(8,128)(2,1)S(1)}, bf16[1024,128]{1,0:T(8,128)(2,1)S(1)}, u32[]{:S(2)}, u32[]{:S(2)}) collective-permute-start(bf16[1024,128]{1,0:T(8,128)(2,1)S(1)} %slice.557), channel_id=1, source_target_pairs={{0,3},{4,7},{8,11},{12,15},{16,19},{20,23},{24,27},{28,31},{32,35}... | collective-permute-start | bytes 786440 | tf_op jit(solution)/shard_map/ppermute | solution.py:42
  86.4 3.9 collective-permute-start.21
  109.6 3.9 collective-permute-done.23
  153.2 6.6 %collective-permute-done.38 = bf16[256,256]{1,0:T(8,128)(2,1)S(1)} collective-permute-done((bf16[256,256]{1,0:T(8,128)(2,1)S(1)}, bf16[256,256]{1,0:T(8,128)(2,1)S(1)}, u32[]{:S(2)}, u32[]{:S(2)}) %collective-permute-start.38) | collective-permute-done | bytes 131104 | tf_op jit(solution)/shard_map/ppermute | solution.py:33
  165.0 8.9 %collective-permute-start.41 = (bf16[1024,128]{1,0:T(8,128)(2,1)S(1)}, bf16[1024,128]{1,0:T(8,128)(2,1)S(1)}, u32[]{:S(2)}, u32[]{:S(2)}) collective-permute-start(bf16[1024,128]{1,0:T(8,128)(2,1)S(1)} %slice.586), channel_id=1, source_target_pairs={{0,3},{4,7},{8,11},{12,15},{16,19},{20,23},{24,27},{28,31},{32,35}... | collective-permute-start | bytes 786440 | tf_op jit(solution)/shard_map/ppermute | solution.py:42
  199.0 4.1 collective-permute-done.47
  226.9 4.0 collective-permute-done.54
  251.0 6.7 %attend_back.2 = (bf16[1024,128]{1,0:T(8,128)(2,1)S(1)}, bf16[1024,128]{1,0:T(8,128)(2,1)S(1)}, bf16[1024,128]{1,0:T(8,128)(2,1)}, bf16[1024,128]{1,0:T(8,128)(2,1)}, bf16[1024,128]{1,0:T(8,128)(2,1)}) custom-call(s32[5]{0:T(128)S(1)} %stack.142.scalar_ref, bf16[1024,256]{1,0:T(8,128)(2,1)S(1)} %pad_maximum_fusion.14.own_ref, ...), custom_call_target="tpu_custom_call" | custom-call | flops 2684354560 | bytes 6291456 | tf_op jit(solution)/shard_map/attend_back/pallas_call | solution.py:331
  264.0 7.3 %collective-permute-done.62 = bf16[1024,128]{1,0:T(8,128)(2,1)S(1)} collective-permute-done((bf16[1024,128]{1,0:T(8,128)(2,1)}, bf16[1024,128]{1,0:T(8,128)(2,1)S(1)}, u32[]{:S(2)}, u32[]{:S(2)}) %collective-permute-start.62) | collective-permute-done | bytes 262176 | tf_op jit(solution)/shard_map/ppermute | solution.py:42
  271.2 8.7 %collective-permute-done.63 = bf16[1024,128]{1,0:T(8,128)(2,1)S(1)} collective-permute-done((bf16[1024,128]{1,0:T(8,128)(2,1)}, bf16[1024,128]{1,0:T(8,128)(2,1)S(1)}, u32[]{:S(2)}, u32[]{:S(2)}) %collective-permute-start.63) | collective-permute-done | bytes 262176 | tf_op jit(solution)/shard_map/ppermute | solution.py:42
  279.9 5.2 %collective-permute-done.64 = bf16[1024,128]{1,0:T(8,128)(2,1)S(1)} collective-permute-done((bf16[1024,128]{1,0:T(8,128)(2,1)}, bf16[1024,128]{1,0:T(8,128)(2,1)S(1)}, u32[]{:S(2)}, u32[]{:S(2)}) %collective-permute-start.64) | collective-permute-done | bytes 262176 | tf_op jit(solution)/shard_map/ppermute | solution.py:42
  291.0 4.6 collective-permute-done.65
  296.1 5.1 %collective-permute-done.66 = bf16[256,256]{1,0:T(8,128)(2,1)S(1)} collective-permute-done((bf16[256,256]{1,0:T(8,128)(2,1)S(1)}, bf16[256,256]{1,0:T(8,128)(2,1)S(1)}, u32[]{:S(2)}, u32[]{:S(2)}) %collective-permute-start.66) | collective-permute-done | bytes 131104 | tf_op jit(solution)/shard_map/ppermute | solution.py:33
  339.3 3.9 collective-permute-done.77
  344.1 4.6 add_convert_fusion
  373.3 5.7 %attend_back.3 = (bf16[1024,128]{1,0:T(8,128)(2,1)S(1)}, bf16[1024,128]{1,0:T(8,128)(2,1)S(1)}, bf16[1024,128]{1,0:T(8,128)(2,1)S(1)}, bf16[1024,128]{1,0:T(8,128)(2,1)S(1)}, bf16[1024,128]{1,0:T(8,128)(2,1)S(1)}) custom-call(s32[5]{0:T(128)S(1)} %stack.142.scalar_ref, bf16[1024,256]{1,0:T(8,128)(2,1)S(1)} %pad_maximum_fusion.11.own_ref, ...), custom_call_target="tpu_custom_call" | custom-call | flops 2684354560 | bytes 6291456 | tf_op jit(solution)/shard_map/attend_back/pallas_call | solution.py:331
  391.0 5.5 %collective-permute-done.87 = bf16[1024,128]{1,0:T(8,128)(2,1)S(1)} collective-permute-done((bf16[1024,128]{1,0:T(8,128)(2,1)S(1)}, bf16[1024,128]{1,0:T(8,128)(2,1)S(1)}, u32[]{:S(2)}, u32[]{:S(2)}) %collective-permute-start.87) | collective-permute-done | bytes 262176 | tf_op jit(solution)/shard_map/ppermute | solution.py:42
  437.5 7.1 %collective-permute-done.100 = bf16[144,1024]{1,0:T(8,128)(2,1)S(1)} collective-permute-done((bf16[144,1024]{1,0:T(8,128)(2,1)S(1)}, bf16[144,1024]{1,0:T(8,128)(2,1)S(1)}, u32[]{:S(2)}, u32[]{:S(2)}) %collective-permute-start.100) | collective-permute-done | bytes 294944 | tf_op jit(solution)/shard_map/ppermute | solution.py:33
  453.3 7.0 %collective-permute-done.105 = bf16[144,1024]{1,0:T(8,128)(2,1)S(1)} collective-permute-done((bf16[144,1024]{1,0:T(8,128)(2,1)S(1)}, bf16[144,1024]{1,0:T(8,128)(2,1)S(1)}, u32[]{:S(2)}, u32[]{:S(2)}) %collective-permute-start.105) | collective-permute-done | bytes 294944 | tf_op jit(solution)/shard_map/ppermute | solution.py:37
  460.3 6.7 %collective-permute-done.104 = bf16[144,1024]{1,0:T(8,128)(2,1)S(1)} collective-permute-done((bf16[144,1024]{1,0:T(8,128)(2,1)S(1)}, bf16[144,1024]{1,0:T(8,128)(2,1)S(1)}, u32[]{:S(2)}, u32[]{:S(2)}) %collective-permute-start.104) | collective-permute-done | bytes 294944 | tf_op jit(solution)/shard_map/ppermute | solution.py:37
  (667 shorter events, 329.7 us)
Async XLA Ops:
  7.2 79.0 %all-gather.4.cloned.1.call-start = ((), (), s32[]{:S(2)}) async-start(), calls=%async_computation.3 | async-start | bytes 2621440 | tf_op jit(solution)/shard_map/all_gather | solution.py:508
  8.8 16.6 %collective-permute-start.11 = (bf16[64,1024]{1,0:T(8,128)(2,1)S(1)}, bf16[64,1024]{1,0:T(8,128)(2,1)S(1)}, u32[]{:S(2)}, u32[]{:S(2)}) collective-permute-start(bf16[64,1024]{1,0:T(8,128)(2,1)S(1)} %get-tuple-element.237), channel_id=1, source_target_pairs={{0,12},{4,0},{8,4},{12,8},{16,28},{20,16},{24,20},{28,24},{32,44},... | collective-permute-start | bytes 393224 | tf_op jit(solution)/shard_map/ppermute | solution.py:26
  12.9 15.1 %collective-permute-start.9 = (bf16[64,1024]{1,0:T(8,128)(2,1)S(1)}, bf16[64,1024]{1,0:T(8,128)(2,1)S(1)}, u32[]{:S(2)}, u32[]{:S(2)}) collective-permute-start(bf16[64,1024]{1,0:T(8,128)(2,1)S(1)} %get-tuple-element.237), channel_id=1, source_target_pairs={{0,4},{4,8},{8,12},{12,0},{16,20},{20,24},{24,28},{28,16},{32,36},... | collective-permute-start | bytes 393224 | tf_op jit(solution)/shard_map/ppermute | solution.py:26
  28.9 15.5 %collective-permute-start.7 = (bf16[144,1024]{1,0:T(8,128)(2,1)S(1)}, bf16[144,1024]{1,0:T(8,128)(2,1)S(1)}, u32[]{:S(2)}, u32[]{:S(2)}) collective-permute-start(bf16[144,1024]{1,0:T(8,128)(2,1)S(1)} %get-tuple-element.52), channel_id=1, source_target_pairs={{0,48},{4,52},{8,56},{12,60},{16,0},{20,4},{24,8},{28,12},{32,16},... | collective-permute-start | bytes 884744 | tf_op jit(solution)/shard_map/ppermute | solution.py:33
  48.2 59.9 %all-gather.6.cloned.1.call-start = ((), (), s32[]{:S(2)}) async-start(), calls=%async_computation.4 | async-start | bytes 1474560 | tf_op jit(solution)/shard_map/all_gather | solution.py:508
  49.0 129.1 %all-gather.8.cloned.1.call-start = ((), (), s32[]{:S(2)}) async-start(), calls=%async_computation.5 | async-start | bytes 2621440 | tf_op jit(solution)/shard_map/all_gather | solution.py:508
  86.2 38.5 %collective-permute-start.28 = (bf16[1024,1024]{1,0:T(8,128)(2,1)}, bf16[1024,1024]{1,0:T(8,128)(2,1)}, u32[]{:S(2)}, u32[]{:S(2)}) collective-permute-start(bf16[1024,1024]{1,0:T(8,128)(2,1)} %all-gather.4.cloned.1.call-done), channel_id=1, source_target_pairs={{0,64},{64,0},{1,65},{65,1},{2,66},{66,2},{3,67},{67,3},{4,68},{68... | collective-permute-start | bytes 6291464 | tf_op jit(solution)/shard_map/ppermute | solution.py:62
  119.4 19.1 %collective-permute-start.32 = (bf16[4,144,1024]{2,1,0:T(8,128)(2,1)}, bf16[4,144,1024]{2,1,0:T(8,128)(2,1)}, u32[]{:S(2)}, u32[]{:S(2)}) collective-permute-start(bf16[4,144,1024]{2,1,0:T(8,128)(2,1)} %pad_maximum_fusion.3), channel_id=1, source_target_pairs={{0,64},{64,0},{1,65},{65,1},{2,66},{66,2},{3,67},{67,3},{4,68},{68... | collective-permute-start | bytes 3538952 | tf_op jit(solution)/shard_map/ppermute | solution.py:62
  131.4 212.8 %reduce-scatter.4.cloned.1.call-start = ((), (), s32[]{:S(2)}) async-start(), calls=%async_computation.6 | async-start | bytes 2621440 | tf_op jit(solution)/shard_map/reduce_scatter | solution.py:562
  165.0 15.6 %collective-permute-start.41 = (bf16[1024,128]{1,0:T(8,128)(2,1)S(1)}, bf16[1024,128]{1,0:T(8,128)(2,1)S(1)}, u32[]{:S(2)}, u32[]{:S(2)}) collective-permute-start(bf16[1024,128]{1,0:T(8,128)(2,1)S(1)} %slice.586), channel_id=1, source_target_pairs={{0,3},{4,7},{8,11},{12,15},{16,19},{20,23},{24,27},{28,31},{32,35}... | collective-permute-start | bytes 786440 | tf_op jit(solution)/shard_map/ppermute | solution.py:42
  178.1 30.5 %collective-permute-start.48 = (bf16[1024,1024]{1,0:T(8,128)(2,1)}, bf16[1024,1024]{1,0:T(8,128)(2,1)S(1)}, u32[]{:S(2)}, u32[]{:S(2)}) collective-permute-start(bf16[1024,1024]{1,0:T(8,128)(2,1)} %all-gather.8.cloned.1.call-done), channel_id=1, source_target_pairs={{0,64},{64,0},{1,65},{65,1},{2,66},{66,2},{3,67},{67,3},{4,68},{68... | collective-permute-start | bytes 6291464 | tf_op jit(solution)/shard_map/ppermute | solution.py:62
  259.0 20.9 %collective-permute-start.63 = (bf16[1024,128]{1,0:T(8,128)(2,1)}, bf16[1024,128]{1,0:T(8,128)(2,1)S(1)}, u32[]{:S(2)}, u32[]{:S(2)}) collective-permute-start(bf16[1024,128]{1,0:T(8,128)(2,1)} %get-tuple-element.65), channel_id=1, source_target_pairs={{2,0},{3,1},{6,4},{7,5},{10,8},{11,9},{14,12},{15,13},{18,16},{19,... | collective-permute-start | bytes 786440 | tf_op jit(solution)/shard_map/ppermute | solution.py:42
  260.3 24.8 %collective-permute-start.64 = (bf16[1024,128]{1,0:T(8,128)(2,1)}, bf16[1024,128]{1,0:T(8,128)(2,1)S(1)}, u32[]{:S(2)}, u32[]{:S(2)}) collective-permute-start(bf16[1024,128]{1,0:T(8,128)(2,1)} %get-tuple-element.66), channel_id=1, source_target_pairs={{3,0},{7,4},{11,8},{15,12},{19,16},{23,20},{27,24},{31,28},{35,32}... | collective-permute-start | bytes 786440 | tf_op jit(solution)/shard_map/ppermute | solution.py:42
  263.9 132.8 %reduce-scatter.8.cloned.1.call-start = ((), (), s32[]{:S(2)}) async-start(), calls=%async_computation.8 | async-start | bytes 1310720 | tf_op jit(solution)/shard_map/reduce_scatter | solution.py:562
  305.7 16.1 %collective-permute-start.74 = (bf16[4,128,1024]{2,1,0:T(8,128)(2,1)S(1)}, bf16[4,128,1024]{2,1,0:T(8,128)(2,1)S(1)}, u32[]{:S(2)}, u32[]{:S(2)}) collective-permute-start(bf16[4,128,1024]{2,1,0:T(8,128)(2,1)S(1)} %get-tuple-element.157), channel_id=1, source_target_pairs={{0,64},{64,0},{1,65},{65,1},{2,66},{66,2},{3,67},{67,3},{4,68},{68... | collective-permute-start | bytes 3145736 | tf_op jit(solution)/shard_map/ppermute | solution.py:62
  328.8 15.3 %collective-permute-start.78 = (bf16[1024,1024]{1,0:T(8,128)(2,1)}, bf16[1024,1024]{1,0:T(8,128)(2,1)}, u32[]{:S(2)}, u32[]{:S(2)}) collective-permute-start(bf16[1024,1024]{1,0:T(8,128)(2,1)} %get-tuple-element.153), channel_id=1, source_target_pairs={{0,64},{64,0},{1,65},{65,1},{2,66},{66,2},{3,67},{67,3},{4,68},{68... | collective-permute-start | bytes 6291464 | tf_op jit(solution)/shard_map/ppermute | solution.py:62
  330.5 66.3 %reduce-scatter.6.cloned.1.call-start = ((), (), s32[]{:S(2)}) async-start(), calls=%async_computation.7 | async-start | bytes 2621440 | tf_op jit(solution)/shard_map/reduce_scatter | solution.py:562
  348.8 118.4 %all-reduce.8.cloned.1.call-start = ((), (), s32[]{:S(2)}) async-start(), calls=%async_computation.9 | async-start | bytes 2621440 | tf_op jit(solution)/shard_map/psum | solution.py:614
  367.6 67.4 %collective-permute-start.94 = (bf16[64,1024]{1,0:T(8,128)(2,1)}, bf16[64,1024]{1,0:T(8,128)(2,1)}, u32[]{:S(2)}, u32[]{:S(2)}) collective-permute-start(bf16[64,1024]{1,0:T(8,128)(2,1)} %get-tuple-element.190), channel_id=1, source_target_pairs={{0,12},{4,0},{8,4},{12,8},{16,28},{20,16},{24,20},{28,24},{32,44},... | collective-permute-start | bytes 393224 | tf_op jit(solution)/shard_map/ppermute | solution.py:26
  368.2 67.8 %collective-permute-start.96 = (bf16[64,1024]{1,0:T(8,128)(2,1)}, bf16[64,1024]{1,0:T(8,128)(2,1)}, u32[]{:S(2)}, u32[]{:S(2)}) collective-permute-start(bf16[64,1024]{1,0:T(8,128)(2,1)} %get-tuple-element.191), channel_id=1, source_target_pairs={{0,4},{4,8},{8,12},{12,0},{16,20},{20,24},{24,28},{28,16},{32,36},... | collective-permute-start | bytes 393224 | tf_op jit(solution)/shard_map/ppermute | solution.py:26
  381.6 14.9 %collective-permute-start.87 = (bf16[1024,128]{1,0:T(8,128)(2,1)S(1)}, bf16[1024,128]{1,0:T(8,128)(2,1)S(1)}, u32[]{:S(2)}, u32[]{:S(2)}) collective-permute-start(bf16[1024,128]{1,0:T(8,128)(2,1)S(1)} %get-tuple-element.75), channel_id=1, source_target_pairs={{3,0},{7,4},{11,8},{15,12},{19,16},{23,20},{27,24},{31,28},{35,32}... | collective-permute-start | bytes 786440 | tf_op jit(solution)/shard_map/ppermute | solution.py:42
  435.0 15.1 %collective-permute-start.102 = (bf16[144,1024]{1,0:T(8,128)(2,1)S(1)}, bf16[144,1024]{1,0:T(8,128)(2,1)S(1)}, u32[]{:S(2)}, u32[]{:S(2)}) collective-permute-start(bf16[144,1024]{1,0:T(8,128)(2,1)S(1)} %get-tuple-element.261), channel_id=1, source_target_pairs={{0,16},{4,20},{8,24},{12,28},{16,32},{20,36},{24,40},{28,44},{32,4... | collective-permute-start | bytes 884744 | tf_op jit(solution)/shard_map/ppermute | solution.py:33
  437.4 15.0 %collective-permute-start.97 = (f32[64,1024]{1,0:T(8,128)S(1)}, f32[64,1024]{1,0:T(8,128)S(1)}, u32[]{:S(2)}, u32[]{:S(2)}) collective-permute-start(f32[64,1024]{1,0:T(8,128)S(1)} %broadcast_select_fusion.28), channel_id=1, source_target_pairs={{0,64},{64,0},{1,65},{65,1},{2,66},{66,2},{3,67},{67,3},{4,68},{68... | collective-permute-start | bytes 786440 | tf_op jit(solution)/shard_map/ppermute | solution.py:62
  450.4 16.5 %collective-permute-start.104 = (bf16[144,1024]{1,0:T(8,128)(2,1)S(1)}, bf16[144,1024]{1,0:T(8,128)(2,1)S(1)}, u32[]{:S(2)}, u32[]{:S(2)}) collective-permute-start(bf16[144,1024]{1,0:T(8,128)(2,1)S(1)} %add_convert_fusion.4), channel_id=1, source_target_pairs={{0,1},{1,2},{2,3},{3,0},{4,5},{5,6},{6,7},{7,4},{8,9},{9,10},{10,1... | collective-permute-start | bytes 884744 | tf_op jit(solution)/shard_map/ppermute | solution.py:37
  (214 other events, 1861.7 us)
Sparse Core Ops, SparseCore 0:
  48.4 32.2 all-gather.3
  82.9 25.2 all-gather.5
  131.5 40.9 all-gather.7
  264.0 45.7 reduce-scatter.3
  330.5 19.7 reduce-scatter.7
  352.6 32.1 reduce-scatter.5
  402.2 44.4 all-reduce.7
